TPU v7x, 32 devices: a whole 2x2x4 slice. The times are simulated.
32 devices in a mesh: seq: 8 (over z, x), tp: 4 (over y, core).
Axes of the slice: x: 2, y: 2, z: 4, core: 2. Of those that a mesh axis runs over, the one named last changes fastest.
Arguments:
- tokens: bfloat16 [6144, 1024], P('seq'), may hold values from -6 to 6
- grad_out: bfloat16 [6144, 1024], P('seq'), may hold values from -6 to 6
- noise_level: int32 [16], replicated, may hold values from 0 to 999
- context_mask: int32 [16], replicated, may hold values 0 or 1
- frame_clip: int32 [16], replicated, may hold values from 0 to 2, as said below
- level_table: bfloat16 [1000, 1024], replicated, may hold values from -6 to 6
- master: float32 [4, 4718592], P('tp', 'seq')
- moment_one: float32 [4, 4718592], P('tp', 'seq')
- moment_two: float32 [4, 4718592], P('tp', 'seq'), as said below
- average: float32 [4, 4718592], P('tp', 'seq')
Outputs:
- result: bfloat16 [6144, 1024], P('seq')
- input_grad: float32 [6144, 1024], P('seq')
- new_master: float32 [4, 4718592], P('tp', 'seq')
- new_one: float32 [4, 4718592], P('tp', 'seq')
- new_two: float32 [4, 4718592], P('tp', 'seq')
- new_average: float32 [4, 4718592], P('tp', 'seq')
Inputs may be any that keep to these rules, and one draw needn't show every extreme that they name: `frame_clip`: clip 0 has exactly one frame among the 2 frames of each token group; every other clip has 4 to 7 frames. `moment_two`: positive.
All inputs are finite; a program needn't handle non-finite values.
Results may differ from a plain program's by a relative error of at most 0.02.
The roundings to bfloat16 on the way count: a program that leaves them out, or rounds other values in their place, can miss the bound.
Values may be sent and summed in bfloat16 or wider, within the bound.
A program may use at most 256 MiB of HBM per device.

v0:
```python
import functools

import jax
import jax.numpy as jnp
from jax import lax
from jax.sharding import PartitionSpec as P

D = 1024
HEADS = 16
HEAD = 64
FF = 4096
TOK_FRAME = 384
STEP = 7


NORM_EPSILON = 1e-06
RATE_FACTOR = 2.5
BETA_FIRST = 0.5
BETA_SECOND = 0.5
ADAM_EPSILON = 1e-08
WEIGHT_DECAY = 0.01
AVERAGE_RATE = 0.9
MASKED_SCORE = -1e30
HIGHEST = lax.Precision.HIGHEST


def normalize(rows):
    centred = rows - jnp.mean(rows, axis=1, keepdims=True)
    inverse = lax.rsqrt(jnp.mean(centred * centred, axis=1, keepdims=True) + NORM_EPSILON)
    return (centred * inverse, inverse)


def norm_back(grads, normed, inverse):
    return inverse * (
        grads
        - jnp.mean(grads, axis=1, keepdims=True)
        - normed * jnp.mean(grads * normed, axis=1, keepdims=True)
    )


def by_frame(rows, frame_count):
    return rows.reshape(frame_count, -1, rows.shape[1])


def frame_scale(rows, factor, frame_count):
    return (by_frame(rows, frame_count) * factor[:, None, :]).reshape(rows.shape)


def frame_affine(rows, factor, offset_rows, frame_count):
    return (
        by_frame(rows, frame_count) * (1.0 + factor)[:, None, :] + offset_rows[:, None, :]
    ).reshape(rows.shape)


def frame_total(rows, frame_count):
    return jnp.sum(by_frame(rows, frame_count), axis=1)


def inner(left, right):
    return lax.dot_general(
        left, right, (((0,), (0,)), ((), ())), preferred_element_type=jnp.float32
    )


def outer_back(left, right):
    return lax.dot_general(
        left, right, (((1,), (1,)), ((), ())), preferred_element_type=jnp.float32
    )


def split_heads(rows):
    return rows.reshape(rows.shape[0], -1, HEAD)


def visibility(query_offset, query_count, key_offset, key_count, frame_clip):
    query_frames = (query_offset + jnp.arange(query_count, dtype=jnp.int32)) // TOK_FRAME
    key_frames = (key_offset + jnp.arange(key_count, dtype=jnp.int32)) // TOK_FRAME
    query_clips = jnp.repeat(
        lax.dynamic_slice_in_dim(frame_clip, query_offset // TOK_FRAME, query_count // TOK_FRAME),
        TOK_FRAME,
    )
    key_clips = jnp.repeat(
        lax.dynamic_slice_in_dim(frame_clip, key_offset // TOK_FRAME, key_count // TOK_FRAME),
        TOK_FRAME,
    )
    return (query_clips[:, None] == key_clips[None, :]) & (
        key_frames[None, :] <= query_frames[:, None]
    )


def raw_scores(query_heads, key_heads):
    return jnp.einsum(
        "qhe,khe->hqk", query_heads, key_heads, preferred_element_type=jnp.float32
    ) * HEAD ** (-0.5)


def fold_blocks(update, running, arrays, offset, block_rows):
    block_count = arrays[0].shape[0] // block_rows
    stacked = tuple(
        (array.reshape((block_count, block_rows) + array.shape[1:]) for array in arrays)
    )

    def fold_advance(carried, element):
        position, pieces = element
        return (update(carried, pieces, offset + position * block_rows), None)

    final, unused = lax.scan(
        fold_advance, running, (jnp.arange(block_count, dtype=jnp.int32), stacked)
    )
    return final


def map_blocks(produce, arrays, block_rows):
    block_count = arrays[0].shape[0] // block_rows
    stacked = tuple(
        (array.reshape((block_count, block_rows) + array.shape[1:]) for array in arrays)
    )

    def map_advance(carried, element):
        position, pieces = element
        return (carried, produce(pieces, position * block_rows))

    unused, outputs = lax.scan(
        map_advance, jnp.zeros((), jnp.int32), (jnp.arange(block_count, dtype=jnp.int32), stacked)
    )
    return outputs.reshape((block_count * block_rows,) + outputs.shape[2:])


def attention_fold(query_heads, query_offset, frame_clip):

    def update(running, pieces, offset):
        row_max, row_total, weighted = running
        key_heads = split_heads(pieces[0])
        value_heads = split_heads(pieces[1]).astype(jnp.float32)
        visible = visibility(
            query_offset, query_heads.shape[0], offset, key_heads.shape[0], frame_clip
        )[None]
        scores = jnp.where(visible, raw_scores(query_heads, key_heads), MASKED_SCORE)
        new_max = jnp.maximum(row_max, jnp.max(scores, axis=2))
        weights = jnp.where(visible, jnp.exp(scores - new_max[:, :, None]), 0.0)
        factor = jnp.exp(row_max - new_max)
        row_total = row_total * factor + jnp.sum(weights, axis=2)
        weighted = weighted * factor[:, :, None] + jnp.einsum(
            "hqk,khe->hqe", weights, value_heads, precision=HIGHEST
        )
        return (new_max, row_total, weighted)

    def folder(running, pieces, offset):
        return fold_blocks(update, running, pieces, offset, query_heads.shape[0])

    return folder


def query_grad_fold(query_heads, grad_heads, log_total, row_delta, query_offset, frame_clip):

    def update(running, pieces, offset):
        key_heads = split_heads(pieces[0])
        value_heads = split_heads(pieces[1])
        visible = visibility(
            query_offset, query_heads.shape[0], offset, key_heads.shape[0], frame_clip
        )[None]
        weights = jnp.where(
            visible, jnp.exp(raw_scores(query_heads, key_heads) - log_total[:, :, None]), 0.0
        )
        grad_weights = jnp.einsum(
            "qhe,khe->hqk", grad_heads, value_heads, preferred_element_type=jnp.float32
        )
        grad_scores = (weights * (grad_weights - row_delta[:, :, None])).astype(jnp.bfloat16)
        return running + jnp.einsum(
            "hqk,khe->hqe", grad_scores, key_heads, preferred_element_type=jnp.float32
        ) * HEAD ** (-0.5)

    def folder(running, pieces, offset):
        return fold_blocks(update, running, pieces, offset, query_heads.shape[0])

    return folder


def key_terms(
    query_heads,
    grad_heads,
    log_total,
    row_delta,
    query_offset,
    key_heads,
    value_heads,
    key_offset,
    frame_clip,
):
    visible = visibility(
        query_offset, query_heads.shape[0], key_offset, key_heads.shape[0], frame_clip
    )[None]
    weights = jnp.where(
        visible, jnp.exp(raw_scores(query_heads, key_heads) - log_total[:, :, None]), 0.0
    )
    grad_weights = jnp.einsum(
        "qhe,khe->hqk", grad_heads, value_heads, preferred_element_type=jnp.float32
    )
    grad_scores = (weights * (grad_weights - row_delta[:, :, None])).astype(jnp.bfloat16)
    key_grad = jnp.einsum(
        "hqk,qhe->khe", grad_scores, query_heads, preferred_element_type=jnp.float32
    ) * HEAD ** (-0.5)
    value_grad = jnp.einsum(
        "hqk,qhe->khe", weights, grad_heads.astype(jnp.float32), precision=HIGHEST
    )
    key_count = key_heads.shape[0]
    return jnp.concatenate(
        [key_grad.reshape(key_count, -1), value_grad.reshape(key_count, -1)], axis=1
    )


def local(
    tokens,
    grad_out,
    noise_level,
    context_mask,
    frame_clip,
    level_table,
    master,
    moment_one,
    moment_two,
    average,
):
    tp_count = lax.axis_size("tp")
    local_rows = tokens.shape[0]
    frame_count = local_rows // TOK_FRAME
    group = lax.axis_index("seq")
    row_offset = group * local_rows
    frame_offset = group * frame_count
    head_cols = HEADS * HEAD // tp_count
    hidden_cols = FF // tp_count
    mod_cols = 6 * D // tp_count
    gathered = lax.all_gather(master.astype(jnp.bfloat16), "seq", axis=1, tiled=True)[0]
    edge_one = 3 * D * head_cols
    edge_two = edge_one + head_cols * D
    edge_three = edge_two + D * hidden_cols
    edge_four = edge_three + hidden_cols * D
    w_qkv = gathered[:edge_one].reshape(D, 3 * head_cols)
    w_out = gathered[edge_one:edge_two].reshape(head_cols, D)
    w_up = gathered[edge_two:edge_three].reshape(D, hidden_cols)
    w_down = gathered[edge_three:edge_four].reshape(hidden_cols, D)
    w_mod = gathered[edge_four:].reshape(D, mod_cols)
    levels = lax.dynamic_slice_in_dim(noise_level, frame_offset, frame_count)
    context = lax.dynamic_slice_in_dim(context_mask, frame_offset, frame_count)
    effective = levels * (1 - context)
    one_hot = (
        effective[:, None] == jnp.arange(level_table.shape[0], dtype=jnp.int32)[None, :]
    ).astype(jnp.bfloat16)
    condition = jax.nn.silu(
        jnp.dot(one_hot, level_table, preferred_element_type=jnp.float32)
    ).astype(jnp.bfloat16)
    modulation = lax.all_gather(
        jnp.dot(condition, w_mod, preferred_element_type=jnp.float32), "tp", axis=1, tiled=True
    )
    shift_one, scale_one, gate_one, shift_two, scale_two, gate_two = [
        modulation[:, column_part * D : (column_part + 1) * D] for column_part in range(6)
    ]
    inputs = tokens.astype(jnp.float32)
    normed_one, inverse_one = normalize(inputs)
    first_in = frame_affine(normed_one, scale_one, shift_one, frame_count).astype(jnp.bfloat16)
    projected = jnp.dot(first_in, w_qkv, preferred_element_type=jnp.float32).astype(jnp.bfloat16)
    query_rows = projected[:, :head_cols]
    key_rows = projected[:, head_cols : 2 * head_cols]
    value_rows = projected[:, 2 * head_cols :]
    query_heads = split_heads(query_rows)
    head_count = query_heads.shape[1]
    start_state = (
        jnp.full((head_count, local_rows), MASKED_SCORE, jnp.float32),
        jnp.zeros((head_count, local_rows), jnp.float32),
        jnp.zeros((head_count, local_rows, HEAD), jnp.float32),
    )
    row_max, row_total, weighted = attention_fold(query_heads, row_offset, frame_clip)(
        start_state,
        (
            lax.all_gather(key_rows, "seq", axis=0, tiled=True),
            lax.all_gather(value_rows, "seq", axis=0, tiled=True),
        ),
        jnp.int32(0),
    )
    log_total = row_max + jnp.log(row_total)
    attended_full = weighted / row_total[:, :, None]
    attended = (
        jnp.transpose(attended_full, (1, 0, 2)).reshape(local_rows, head_cols).astype(jnp.bfloat16)
    )
    attn_part = jnp.dot(attended, w_out, preferred_element_type=jnp.float32)
    attn = lax.psum(attn_part, "tp")
    middle = inputs + frame_scale(attn, gate_one, frame_count)
    normed_two, inverse_two = normalize(middle)
    second_in = frame_affine(normed_two, scale_two, shift_two, frame_count).astype(jnp.bfloat16)
    up_rows = jnp.dot(second_in, w_up, preferred_element_type=jnp.float32)
    activated, gelu_back = jax.vjp(functools.partial(jax.nn.gelu, approximate=True), up_rows)
    hidden = activated.astype(jnp.bfloat16)
    mlp_part = jnp.dot(hidden, w_down, preferred_element_type=jnp.float32)
    mlp = lax.psum(mlp_part, "tp")
    result = middle + frame_scale(mlp, gate_two, frame_count)
    upstream = grad_out.astype(jnp.float32)
    gate_two_grad = frame_total(mlp_part * upstream, frame_count)
    mlp_grad = frame_scale(upstream, gate_two, frame_count).astype(jnp.bfloat16)
    down_grad = inner(hidden, mlp_grad)
    up_grad = gelu_back(outer_back(mlp_grad, w_down))[0].astype(jnp.bfloat16)
    up_weight_grad = inner(second_in, up_grad)
    second_grad = outer_back(up_grad, w_up)
    scale_two_grad = frame_total(second_grad * normed_two, frame_count)
    shift_two_grad = frame_total(second_grad, frame_count)
    middle_part = norm_back(
        frame_scale(second_grad, 1.0 + scale_two, frame_count), normed_two, inverse_two
    )
    middle_grad = upstream + lax.psum(middle_part, "tp")
    gate_one_grad = frame_total(attn_part * middle_grad, frame_count)
    attn_grad = frame_scale(middle_grad, gate_one, frame_count).astype(jnp.bfloat16)
    out_weight_grad = inner(attended, attn_grad)
    attended_grad = outer_back(attn_grad, w_out).astype(jnp.bfloat16)
    grad_heads = split_heads(attended_grad)
    row_delta = jnp.sum(
        jnp.transpose(grad_heads.astype(jnp.float32), (1, 0, 2)) * attended_full, axis=2
    )
    query_zero = jnp.zeros((head_count, local_rows, HEAD), jnp.float32)
    query_folder = query_grad_fold(
        query_heads, grad_heads, log_total, row_delta, row_offset, frame_clip
    )
    all_keys, all_values = (
        lax.all_gather(key_rows, "seq", axis=0, tiled=True),
        lax.all_gather(value_rows, "seq", axis=0, tiled=True),
    )
    query_grad = query_folder(query_zero, (all_keys, all_values), 0)

    def produce(pieces, block_offset):
        return key_terms(
            query_heads,
            grad_heads,
            log_total,
            row_delta,
            row_offset,
            split_heads(pieces[0]),
            split_heads(pieces[1]),
            block_offset,
            frame_clip,
        )

    key_value_grad = lax.psum_scatter(
        map_blocks(produce, (all_keys, all_values), local_rows),
        "seq",
        scatter_dimension=0,
        tiled=True,
    )
    query_grad_rows = jnp.transpose(query_grad, (1, 0, 2)).reshape(local_rows, head_cols)
    qkv_grad = jnp.concatenate([query_grad_rows, key_value_grad], axis=1).astype(jnp.bfloat16)
    qkv_weight_grad = inner(first_in, qkv_grad)
    first_grad = outer_back(qkv_grad, w_qkv)
    scale_one_grad = frame_total(first_grad * normed_one, frame_count)
    shift_one_grad = frame_total(first_grad, frame_count)
    input_part = norm_back(
        frame_scale(first_grad, 1.0 + scale_one, frame_count), normed_one, inverse_one
    )
    input_grad = middle_grad + lax.psum(input_part, "tp")
    mod_terms = jnp.concatenate(
        [
            shift_one_grad,
            scale_one_grad,
            gate_one_grad,
            shift_two_grad,
            scale_two_grad,
            gate_two_grad,
        ],
        axis=1,
    )
    mod_grad = lax.psum_scatter(mod_terms, "tp", scatter_dimension=1, tiled=True).astype(
        jnp.bfloat16
    )
    mod_weight_grad = inner(condition, mod_grad)
    flat_grads = jnp.concatenate(
        [
            qkv_weight_grad.reshape(-1),
            out_weight_grad.reshape(-1),
            up_weight_grad.reshape(-1),
            down_grad.reshape(-1),
            mod_weight_grad.reshape(-1),
        ]
    )
    grad_shard = lax.psum_scatter(flat_grads[None, :], "seq", scatter_dimension=1, tiled=True)
    learn_rate = RATE_FACTOR * D ** (-0.5)
    new_one = BETA_FIRST * moment_one + (1.0 - BETA_FIRST) * grad_shard
    new_two = BETA_SECOND * moment_two + (1.0 - BETA_SECOND) * grad_shard * grad_shard
    first_hat = new_one / (1.0 - BETA_FIRST**STEP)
    second_hat = new_two / (1.0 - BETA_SECOND**STEP)
    new_master = master - learn_rate * (
        first_hat / (jnp.sqrt(second_hat) + ADAM_EPSILON) + WEIGHT_DECAY * master
    )
    new_average = AVERAGE_RATE * average + (1.0 - AVERAGE_RATE) * new_master
    return (result.astype(jnp.bfloat16), input_grad, new_master, new_one, new_two, new_average)


def solution(mesh):
    in_specs = (
        P("seq", None),
        P("seq", None),
        P(),
        P(),
        P(),
        P(),
        P("tp", "seq"),
        P("tp", "seq"),
        P("tp", "seq"),
        P("tp", "seq"),
    )
    out_specs = (
        P("seq", None),
        P("seq", None),
        P("tp", "seq"),
        P("tp", "seq"),
        P("tp", "seq"),
        P("tp", "seq"),
    )
    return jax.shard_map(local, mesh=mesh, in_specs=in_specs, out_specs=out_specs, check_vma=False)
```

profile of v0, /device:TPU:0, one launch (start us, length us, event | category | flops | bytes accessed | tf_op | source)
XLA Modules:
  0.0 2141.1 jit_solution(6460019184999021969)
XLA Ops:
  17.0 361.0 %all-gather.4.cloned.1.call-done = bf16[1,4718592]{1,0:T(2,128)(2,1)} async-done(((bf16[1,589824]{1,0:T(2,128)(2,1)}), bf16[1,4718592]{1,0:T(2,128)(2,1)}) %all-gather.4.cloned.1.call-update) | async-done | bytes 9437200 | tf_op jit(solution)/shard_map/all_gather | solution.py:233
  377.9 27.3 %slice_reduce_fusion.3 = bf16[786432]{0:T(1024)(128)(2,1)S(1)} fusion(bf16[1,4718592]{1,0:T(2,128)(2,1)} %all-gather.4.cloned.1.call-done), kind=kLoop, calls=%fused_computation.130 | loop fusion | bytes 3145728 | tf_op jit(solution)/shard_map/slice | solution.py:238
  407.5 55.2 %slice_reduce_fusion = bf16[1572864]{0:T(1024)(128)(2,1)} fusion(bf16[1,4718592]{1,0:T(2,128)(2,1)} %all-gather.4.cloned.1.call-done), kind=kLoop, calls=%fused_computation.86 | loop fusion | bytes 6291456 | tf_op jit(solution)/shard_map/slice | solution.py:242
  482.2 9.8 slice_reduce_fusion.4
  493.1 48.8 %all-gather.8.cloned.1.call-done = bf16[6144,256]{0,1:T(8,128)(2,1)} async-done(((bf16[768,256]{0,1:T(8,128)(2,1)}), bf16[6144,256]{0,1:T(8,128)(2,1)}) %all-gather.8.cloned.1.call-update) | async-done | bytes 3145744 | tf_op jit(solution)/shard_map/all_gather | solution.py:276
  545.7 58.0 %all-gather.6.cloned.1.call-done = bf16[6144,256]{0,1:T(8,128)(2,1)} async-done(((bf16[768,256]{0,1:T(8,128)(2,1)}), bf16[6144,256]{0,1:T(8,128)(2,1)}) %all-gather.6.cloned.1.call-update) | async-done | bytes 3145744 | tf_op jit(solution)/shard_map/all_gather | solution.py:275
  607.5 107.0 %while.46 = (s32[]{:T(128)}, f32[4,768]{1,0:T(4,128)S(1)}, f32[4,768]{1,0:T(4,128)S(1)}, f32[4,768,64]{1,2,0:T(8,128)S(1)}, s32[2]{0:T(128)S(1)}, /*index=5*/s32...) while((s32[]{:T(128)}, f32[4,768]{1,0:T(4,128)S(1)}, ...), condition=%wide.region_5.6_spmd.clone, body=%wide.region_2.5_spmd.clone.sunk | while | flops 2144629248 | bytes 35230056 | solution.py:107
  717.9 47.6 %slice_reduce_fusion.2 = (bf16[1048576]{0:T(1024)(128)(2,1)}, bf16[1048576]{0:T(1024)(128)(2,1)}) fusion(bf16[1,4718592]{1,0:T(2,128)(2,1)} %all-gather.4.cloned.1.call-done), kind=kLoop, calls=%fused_computation.103 | loop fusion | bytes 8388608 | tf_op jit(solution)/shard_map/slice | solution.py:240
  801.9 68.6 %all-reduce.9.cloned.1.call-done = f32[768,1024]{1,0:T(8,128)} async-done(((f32[768,1024]{1,0:T(8,128)}), f32[768,1024]{1,0:T(8,128)}) %all-reduce.9.cloned.1.call-update) | async-done | bytes 3145744 | tf_op jit(solution)/shard_map/psum | solution.py:308
  875.0 251.9 %while.45 = (s32[]{:T(128)}, f32[8,768,512]{2,1,0:T(8,128)}, s32[2]{0:T(128)S(1)}, s32[8]{0:T(128)S(1)}, s32[16]{0:T(128)S(1)}, /*index=5*/s32[]{:T(128)}, bf16[...) while((s32[]{:T(128)}, f32[8,768,512]{2,1,0:T(8,128)}, ...), condition=%wide.region_17.18_spmd, body=%wide.region_16.17_spmd.sunk | while | flops 2741515776 | bytes 49815996 | solution.py:123
  891.8 10.5 fusion.181
  923.2 10.5 fusion.181
  954.6 10.5 fusion.181
  986.0 10.5 fusion.181
  1017.4 10.5 fusion.181
  1048.8 10.5 fusion.181
  1080.3 10.5 fusion.181
  1111.7 10.5 fusion.181
  1151.0 136.8 %while.47 = (s32[]{:T(128)}, f32[4,768,64]{1,2,0:T(8,128)}, s32[2]{0:T(128)S(1)}, s32[8]{0:T(128)S(1)}, s32[16]{0:T(128)S(1)}, /*index=5*/s32[]{:T(128)}, bf16[8...) while((s32[]{:T(128)}, f32[4,768,64]{1,2,0:T(8,128)}, ...), condition=%wide.region_15.16_spmd.clone, body=%wide.region_14.15_spmd.clone.sunk | while | flops 922498560 | bytes 26800524 | solution.py:107
  1159.5 8.6 fusion.197
  1176.3 8.9 fusion.197
  1193.5 8.7 fusion.197
  1210.4 8.7 fusion.197
  1227.4 8.8 fusion.197
  1244.5 8.6 fusion.197
  1278.1 9.7 fusion.197
  1289.2 45.9 %reduce-scatter.6.cloned.1.call-done = f32[768,512]{1,0:T(8,128)} async-done(((f32[6144,512]{1,0:T(8,128)}), f32[768,512]{1,0:T(8,128)}) %reduce-scatter.6.cloned.1.call-update) | async-done | bytes 1572880 | tf_op jit(solution)/shard_map/reduce_scatter | solution.py:340
  1367.1 108.5 %all-reduce.13.cloned.1.call-done = (f32[768,1024]{1,0:T(8,128)}, f32[768,1024]{1,0:T(8,128)}) async-done(((f32[768,1024]{1,0:T(8,128)}, f32[768,1024]{1,0:T(8,128)}), (f32[768,1024]{1,0:T(8,128)}, f32[768,1024]{1,0:T(8,128)})) %all-reduce.13.cloned.1.call-update) | async-done | bytes 6291472 | tf_op jit(solution)/shard_map/psum | solution.py:294
  1475.6 10.5 fusion.79
  1497.0 33.8 %reduce-scatter.8.cloned.1.call-done = f32[1536,2]{1,0:T(8,128)} async-done(((f32[6144,2]{1,0:T(8,128)}), f32[1536,2]{1,0:T(8,128)}) %reduce-scatter.8.cloned.1.call-update) | async-done | bytes 12304
  1554.3 560.8 %all-reduce.11.cloned.1.call-done = f32[1,4718592]{1,0:T(1,128)} async-done(((f32[1,4718592]{1,0:T(1,128)}), f32[1,4718592]{1,0:T(1,128)}) %all-reduce.11.cloned.1.call-update) | async-done | bytes 18874384
  2115.1 19.1 multiply_add_fusion.1
  (567 shorter events, 506.4 us)
Async XLA Ops:
  7.2 9.3 copy-start
  7.2 5.5 copy-start.41
  7.2 5.5 copy-start.42
  7.2 370.7 %all-gather.4.cloned.1.call-start = ((), (), s32[]{:S(2)}) async-start(), calls=%async_computation.2 | async-start | bytes 21233664 | tf_op jit(solution)/shard_map/all_gather | solution.py:233
  12.6 529.3 %all-gather.8.cloned.1.call-start = ((), (), s32[]{:S(2)}) async-start(), calls=%async_computation.4 | async-start | bytes 3538944 | tf_op jit(solution)/shard_map/all_gather | solution.py:276
  14.5 463.0 %copy-start.33 = (f32[768]{0:T(1024)}, f32[768]{0:T(1024)S(1)}, u32[]{:S(2)}) copy-start(f32[768]{0:T(1024)S(1)} %broadcast_multiply_fusion.5) | copy-start | bytes 9220
  16.5 461.0 %copy-start.37 = (f32[768]{0:T(1024)}, f32[768]{0:T(1024)S(1)}, u32[]{:S(2)}) copy-start(f32[768]{0:T(1024)S(1)} %add_rsqrt_fusion.1) | copy-start | bytes 9220
  17.0 452.7 %copy-start.39 = (bf16[2,1024]{1,0:T(2,128)(2,1)}, bf16[2,1024]{1,0:T(2,128)(2,1)S(1)}, u32[]{:S(2)}) copy-start(bf16[2,1024]{1,0:T(2,128)(2,1)S(1)} %fusion.89) | copy-start | bytes 12292
  469.7 7.9 copy-start.3
  469.7 9.1 copy-start.12
  477.5 296.5 %copy-start.35 = (f32[2,1024]{1,0:T(2,128)}, f32[2,1024]{1,0:T(2,128)S(1)}, u32[]{:S(2)}) copy-start(f32[2,1024]{1,0:T(2,128)S(1)} %get-tuple-element.960) | copy-start | bytes 24580
  481.3 122.4 %all-gather.6.cloned.1.call-start = ((), (), s32[]{:S(2)}) async-start(), calls=%async_computation.3 | async-start | bytes 3538944 | tf_op jit(solution)/shard_map/all_gather | solution.py:275
  482.0 302.9 %all-reduce.7.cloned.1.call-start = ((), (), s32[]{:S(2)}) async-start(), calls=%async_computation.5 | async-start | bytes 6291456 | tf_op jit(solution)/shard_map/psum | solution.py:286
  717.9 152.6 %all-reduce.9.cloned.1.call-start = ((), (), s32[]{:S(2)}) async-start(), calls=%async_computation.6 | async-start | bytes 6291456 | tf_op jit(solution)/shard_map/psum | solution.py:308
  776.1 8.9 copy-start.4
  787.4 10.8 copy-start.2
  801.8 68.7 %copy-start.9 = (bf16[768,1024]{1,0:T(8,128)(2,1)S(1)}, bf16[768,1024]{1,0:T(8,128)(2,1)}, u32[]{:S(2)}) copy-start(bf16[768,1024]{1,0:T(8,128)(2,1)} %param.17) | copy-start | bytes 4718596
  801.8 533.3 %reduce-scatter.6.cloned.1.call-start = ((), (), s32[]{:S(2)}) async-start(), calls=%async_computation.7 | async-start | bytes 14155776 | tf_op jit(solution)/shard_map/reduce_scatter | solution.py:340
  883.7 8.1 copy-start.27
  915.1 8.1 copy-start.27
  946.5 8.1 copy-start.27
  977.9 8.1 copy-start.27
  1009.3 8.1 copy-start.27
  1040.7 8.1 copy-start.27
  1072.2 8.1 copy-start.27
  1103.6 8.1 copy-start.27
  1127.6 348.0 %all-reduce.13.cloned.1.call-start = ((), (), s32[]{:S(2)}) async-start(), calls=%async_computation.10 | async-start | bytes 12582912 | tf_op jit(solution)/shard_map/psum | solution.py:294
  1356.6 174.2 %reduce-scatter.8.cloned.1.call-start = ((), (), s32[]{:S(2)}) async-start(), calls=%async_computation.8 | async-start | bytes 3932160
  1362.8 112.8 %copy-start.10 = (bf16[768,1024]{1,0:T(8,128)(2,1)S(1)}, bf16[768,1024]{1,0:T(8,128)(2,1)}, u32[]{:S(2)}) copy-start(bf16[768,1024]{1,0:T(8,128)(2,1)} %param.17) | copy-start | bytes 4718596
  1492.6 622.5 %all-reduce.11.cloned.1.call-start = ((), (), s32[]{:S(2)}) async-start(), calls=%async_computation.9 | async-start | bytes 37748736
  1492.6 39.6 %copy-start.40 = (bf16[2,1024]{1,0:T(2,128)(2,1)S(1)}, bf16[2,1024]{1,0:T(2,128)(2,1)}, u32[]{:S(2)}) copy-start(bf16[2,1024]{1,0:T(2,128)(2,1)} %copy-done.39) | copy-start | bytes 12292
  2115.1 19.1 copy-start.1
  (52 other events, 159.5 us)
Sparse Core Ops, SparseCore 0:
  12.8 365.1 all-gather.3
  481.4 60.4 all-gather.7
  544.7 58.9 all-gather.5
  718.0 66.9 all-reduce.6
  801.9 68.5 all-reduce.8
  1127.7 207.3 reduce-scatter.5
  1356.7 118.8 all-reduce.12
  1492.7 38.1 reduce-scatter.7
  1547.8 567.2 all-reduce.10
where the time goes:
time: 2150 us; the launch traced here: 2140 us
  waiting for transfers between devices  1290 us (60%)
  matrix products  401 us (19%)
  local copies, waits for them, and re-layouts  301 us (14%)
  other arithmetic  107 us (5%)
    unnamed x11, waiting for transfers between devices  595 us
    all_gather x1, waiting for transfers between devices, local(): lax.all_gather(master.astype(jnp.bfloat16), 'seq', axis=1, tiled=True)[0]  361 us
    psum x1, waiting for transfers between devices, local(): mlp = lax.psum(mlp_part, 'tp')  109 us
    dot_general x24, matrix products, raw_scores(): jnp.einsum('qhe,khe->hqk', query_heads, key_heads, preferred_element_type...  94.1 us
    dot_general x8, matrix products, key_terms(): jnp.einsum('hqk,qhe->khe', weights, grad_heads.astype(jnp.float32), preci...  83.8 us
    dot_general x8, matrix products, update(): jnp.einsum('hqk,khe->hqe', grad_scores, key_heads, preferred_element_type...  70.7 us
    psum x1, waiting for transfers between devices, local(): middle_grad = upstream + lax.psum(middle_part, 'tp')  68.6 us
    dot_general x8, matrix products, key_terms(): jnp.einsum('hqk,qhe->khe', grad_scores, query_heads, preferred_element_ty...  64.7 us
  transfers between devices with their start and end apart: 9, of which 9 were waited for; matrix products, arithmetic and copies ran while one was open for 12% of the time, Pallas kernels for 0%

commit v1 on v0

v1 whole, which is shorter than its diff:
```python
import functools

import jax
import jax.numpy as jnp
from jax import lax
from jax.experimental import pallas as pl
from jax.experimental.pallas import tpu as pltpu
from jax.sharding import PartitionSpec as P

D = 1024
HEADS = 16
HEAD = 64
FF = 4096
TOK_FRAME = 384
STEP = 7
TP = 4
ZN = 4
HD = HEADS * HEAD // TP
QKV = 3 * HD
FT = FF // TP
MT = 6 * D // TP
F_DEV = 2
BROWS = HD + 2 * FT
LANES = 128
MCOLS = MT // LANES

NORM_EPSILON = 1e-06
RATE_FACTOR = 2.5
BETA_FIRST = 0.5
BETA_SECOND = 0.5
ADAM_EPSILON = 1e-08
WEIGHT_DECAY = 0.01
AVERAGE_RATE = 0.9
MESH = pl.DeviceIdType.MESH
VM = pl.BlockSpec(memory_space=pltpu.VMEM)
SM = pl.BlockSpec(memory_space=pltpu.SMEM)
DMA = pltpu.SemaphoreType.DMA
F32 = jnp.float32
BF16 = jnp.bfloat16
VMEM_LIMIT = 56 * 2**20


def mm(left, right):
    return jnp.dot(left, right, preferred_element_type=F32)


def mm_tn(left, right):
    return lax.dot_general(left, right, (((0,), (0,)), ((), ())), preferred_element_type=F32)


def mm_nt(left, right):
    return lax.dot_general(left, right, (((1,), (1,)), ((), ())), preferred_element_type=F32)


class Plan:
    def __init__(self, seq_count):
        self.n = seq_count
        self.r = seq_count // ZN
        self.shard = (D * QKV + BROWS * D + D * MT) // seq_count
        self.unit = self.shard // 3
        self.uq = self.unit // QKV
        self.ub = self.unit // D
        self.um = self.unit // MT
        self.nq = D // self.uq
        self.nb = self.nq + BROWS // self.ub
        self.nm = D // self.um
        self.first_mod = self.nb // 3
        self.flat_rows = self.unit // LANES
        self.frames = seq_count * F_DEV


def place(plan):
    s = lax.axis_index("seq")
    t = lax.axis_index("tp")
    return s, t, lax.div(s, plan.r), lax.rem(s, plan.r)


def remote(src, dst, send_sem, recv_sem, s, t):
    return pltpu.make_async_remote_copy(
        src_ref=src,
        dst_ref=dst,
        send_sem=send_sem,
        recv_sem=recv_sem,
        device_id=(s, t),
        device_id_type=MESH,
    )


def greet(peers):
    barrier = pltpu.get_barrier_semaphore()
    for s, t in peers:
        pl.semaphore_signal(barrier, inc=1, device_id=(s, t), device_id_type=MESH)
    pl.semaphore_wait(barrier, len(peers))


def by_kind(plan, k, act):
    @pl.when(k < plan.nq)
    def _():
        act("q")

    @pl.when((k >= plan.nq) & (k < plan.nb))
    def _():
        act("b")


def call(kernel, outs, scratch, ins, cid=None, cost=None, name=None):
    params = dict(vmem_limit_bytes=VMEM_LIMIT)
    if cid is not None:
        params.update(collective_id=cid, has_side_effects=True)
    return pl.pallas_call(
        kernel,
        out_shape=outs,
        in_specs=ins,
        out_specs=jax.tree.map(lambda _: VM, outs),
        scratch_shapes=scratch,
        compiler_params=pltpu.CompilerParams(**params),
        name=name,
    )


def gather_kernel(
    plan, master, cond, wq, wb, mod, tile, macc, mpart, mrecv,
    send_sem, recv_sem, msend, mrecv_sem, tsend, trecv,
):
    s, t, z, r = place(plan)
    n, rn = plan.n, plan.r
    greet(
        [(lax.rem(s + d, n), t) for d in range(1, n)]
        + [(s, lax.rem(t + d, TP)) for d in range(1, TP)]
    )

    def unit(k, kind):
        if kind == "q":
            return wq.at[pl.ds(pl.multiple_of(k * plan.uq, plan.uq), plan.uq)]
        return wb.at[pl.ds(pl.multiple_of((k - plan.nq) * plan.ub, plan.ub), plan.ub)]

    def move(k, lu, kind, sem, owner_r, to_s):
        ref = unit(k, kind)
        return remote(ref, ref, send_sem.at[lu, sem], recv_sem.at[lu, owner_r], to_s, t)

    def spread(k, lu, up, down, act):
        def for_kind(kind):
            if up is not None:
                @pl.when(up)
                def _():
                    act(move(k, lu, kind, 0, r, s + rn))
            if down is not None:
                @pl.when(down)
                def _():
                    act(move(k, lu, kind, 1, r, s - rn))
            for d in range(1, rn):
                act(move(k, lu, kind, 1 + d, r, z * rn + lax.rem(r + d, rn)))

        by_kind(plan, k, for_kind)

    start = lambda copy: copy.start()
    finish = lambda copy: copy.wait_send()

    for i in range(3):
        k = 3 * s + i
        base = i * plan.flat_rows

        def fill(kind):
            if kind == "q":
                rows, ref, at, cols = plan.uq, wq, k * plan.uq, QKV // LANES
            else:
                rows, ref, at, cols = plan.ub, wb, (k - plan.nq) * plan.ub, D // LANES
            at = pl.multiple_of(at, rows)
            for j in range(cols):
                ref[pl.ds(at, rows), j * LANES : (j + 1) * LANES] = master[
                    pl.ds(base + j, rows, stride=cols), :
                ].astype(BF16)

        by_kind(plan, k, fill)
        spread(k, 3 * z + i, z < ZN - 1, z > 0, start)

    macc[...] = jnp.zeros_like(macc)
    for i in range(3):
        k = 3 * s + i
        base = i * plan.flat_rows

        @pl.when(k >= plan.nb)
        def _():
            for j in range(MCOLS):
                tile[:, j * LANES : (j + 1) * LANES] = master[
                    pl.ds(base + j, plan.um, stride=MCOLS), :
                ].astype(BF16)
            macc[...] += mm(cond[k - plan.nb], tile[...])

    fm = plan.first_mod

    @pl.when(s >= fm)
    def _():
        for f in range(plan.frames):
            for j in range(MCOLS):
                mpart[f // F_DEV, pl.ds((f % F_DEV) * MCOLS + j, 1), :] = macc[
                    pl.ds(f, 1), j * LANES : (j + 1) * LANES
                ]
        mrecv[s - fm] = mpart[s]
        for d in range(1, n):
            to = lax.rem(s + d, n)
            remote(mpart.at[to], mrecv.at[s - fm], msend.at[d - 1], mrecv_sem.at[s - fm], to, t).start()

    for src in range(fm, n):
        @pl.when(s != src)
        def _():
            remote(
                mpart.at[0], mrecv.at[src - fm], msend.at[0], mrecv_sem.at[src - fm], s, t
            ).wait_recv()

    total = mrecv[0]
    for src in range(1, n - fm):
        total = total + mrecv[src]
    mod[t] = total
    for d in range(1, TP):
        remote(mod.at[t], mod.at[t], tsend.at[d - 1], trecv.at[t], s, lax.rem(t + d, TP)).start()

    for d in range(1, ZN):
        for i in range(3):
            for side in (0, 1):
                zs = z - d if side == 0 else z + d
                k = 3 * (zs * rn + r) + i
                lu = 3 * zs + i

                @pl.when((zs >= 0) & (zs < ZN))
                def _():
                    by_kind(plan, k, lambda kind: move(k, lu, kind, 0, r, s).wait_recv())
                    if side == 0:
                        spread(k, lu, z < ZN - 1, None, start)
                    else:
                        spread(k, lu, None, z > 0, start)

    for d in range(1, rn):
        other = lax.rem(r + d, rn)
        for zs in range(ZN):
            for i in range(3):
                k = 3 * (zs * rn + other) + i
                by_kind(plan, k, lambda kind: move(k, 3 * zs + i, kind, 0, other, s).wait_recv())

    for d in range(1, TP):
        other = lax.rem(t + d, TP)
        remote(mod.at[t], mod.at[other], tsend.at[0], trecv.at[other], s, t).wait_recv()
        remote(mod.at[t], mod.at[t], tsend.at[d - 1], trecv.at[t], s, other).wait_send()

    @pl.when(s >= fm)
    def _():
        for d in range(1, n):
            to = lax.rem(s + d, n)
            remote(mpart.at[to], mrecv.at[s - fm], msend.at[d - 1], mrecv_sem.at[s - fm], to, t).wait_send()

    for i in range(3):
        spread(3 * s + i, 3 * z + i, z < ZN - 1, z > 0, finish)
    for d in range(1, ZN):
        for i in range(3):
            for side in (0, 1):
                zs = z - d if side == 0 else z + d
                k = 3 * (zs * rn + r) + i
                lu = 3 * zs + i

                @pl.when((zs >= 0) & (zs < ZN))
                def _():
                    if side == 0:
                        spread(k, lu, z < ZN - 1, None, finish)
                    else:
                        spread(k, lu, None, z > 0, finish)


def gather_weights(plan, master, cond_units, cid):
    n = plan.n
    mrows = F_DEV * MCOLS
    return call(
        functools.partial(gather_kernel, plan),
        (
            jax.ShapeDtypeStruct((D, QKV), BF16),
            jax.ShapeDtypeStruct((BROWS, D), BF16),
            jax.ShapeDtypeStruct((TP, mrows, LANES), F32),
        ),
        [
            pltpu.VMEM((plan.um, MT), BF16),
            pltpu.VMEM((plan.frames, MT), F32),
            pltpu.VMEM((n, mrows, LANES), F32),
            pltpu.VMEM((n - plan.first_mod, mrows, LANES), F32),
            DMA((3 * ZN, plan.r + 1)),
            DMA((3 * ZN, plan.r)),
            DMA((n - 1,)),
            DMA((n - plan.first_mod,)),
            DMA((TP - 1,)),
            DMA((TP,)),
        ],
        [VM, VM],
        cid,
        name="gather_weights",
    )(master, cond_units)


def qkv_kernel(plan, q, kv, q_out, kv_out, qs, ks, rs, qr, kr, rr):
    s, t, z, r = place(plan)
    rn = plan.r
    greet(
        [(lax.rem(z + d, ZN) * rn + r, t) for d in range(1, ZN)]
        + [(z * rn + lax.rem(r + d, rn), t) for d in range(1, rn)]
    )

    def kv_copy(d):
        h = lax.rem(z + d, ZN)
        return remote(kv.at[h], kv_out.at[s], ks.at[d - 1], kr.at[z], h * rn + r, t)

    def q_copy(d):
        h = lax.rem(z + d, ZN)
        return remote(q.at[h], q_out.at[z], qs.at[d - 1], qr.at[z], h * rn + r, t)

    def side_copy(zs, e):
        at = zs * rn + r
        src = kv_out.at[at]
        return remote(src, src, rs.at[zs, e - 1], rr.at[at], z * rn + lax.rem(r + e, rn), t)

    for d in range(1, ZN):
        kv_copy(d).start()
    for d in range(1, ZN):
        q_copy(d).start()
    kv_out[s] = kv[z]
    q_out[z] = q[z]
    for e in range(1, rn):
        side_copy(z, e).start()
    for d in range(1, ZN):
        zs = lax.rem(z + d, ZN)
        remote(kv.at[0], kv_out.at[zs * rn + r], ks.at[0], kr.at[zs], s, t).wait_recv()
        for e in range(1, rn):
            side_copy(zs, e).start()
    for d in range(1, ZN):
        zs = lax.rem(z + d, ZN)
        remote(q.at[0], q_out.at[zs], qs.at[0], qr.at[zs], s, t).wait_recv()
    for e in range(1, rn):
        for zs in range(ZN):
            at = zs * rn + lax.rem(r + e, rn)
            remote(kv_out.at[at], kv_out.at[at], rs.at[0, 0], rr.at[at], s, t).wait_recv()
    for d in range(1, ZN):
        kv_copy(d).wait_send()
        q_copy(d).wait_send()
    for zs in range(ZN):
        for e in range(1, rn):
            side_copy(zs, e).wait_send()


def exchange_qkv(plan, q, kv, cid):
    rn = plan.r
    return call(
        functools.partial(qkv_kernel, plan),
        (
            jax.ShapeDtypeStruct((ZN, TOK_FRAME, LANES), BF16),
            jax.ShapeDtypeStruct((plan.n, F_DEV * TOK_FRAME, LANES), BF16),
        ),
        [DMA((ZN - 1,)), DMA((ZN - 1,)), DMA((ZN, rn - 1)), DMA((ZN,)), DMA((ZN,)), DMA((plan.n,))],
        [VM, VM],
        cid,
        name="exchange_qkv",
    )(q, kv)


def heads_kernel(plan, x, out, send_sem, recv_sem):
    s, t, z, r = place(plan)
    rn = plan.r
    greet([(lax.rem(z + d, ZN) * rn + r, t) for d in range(1, ZN)])

    def copy(d):
        to = lax.rem(z + d, ZN)
        return remote(x.at[to], out.at[z], send_sem.at[d - 1], recv_sem.at[z], to * rn + r, t)

    for d in range(1, ZN):
        copy(d).start()
    out[z] = x[z]
    for d in range(1, ZN):
        zs = lax.rem(z + d, ZN)
        remote(x.at[0], out.at[zs], send_sem.at[0], recv_sem.at[zs], s, t).wait_recv()
    for d in range(1, ZN):
        copy(d).wait_send()


def exchange_heads(plan, x, cid, name):
    return call(
        functools.partial(heads_kernel, plan),
        jax.ShapeDtypeStruct(x.shape, x.dtype),
        [DMA((ZN - 1,)), DMA((ZN,))],
        [VM],
        cid,
        name=name,
    )(x)


def dkv_kernel(plan, dq, dkv, q_out, kv_out, stage, side, qs, ks, rs, qr, kr, rr):
    s, t, z, r = place(plan)
    rn = plan.r
    greet(
        [(lax.rem(z + d, ZN) * rn + r, t) for d in range(1, ZN)]
        + [(z * rn + lax.rem(r + d, rn), t) for d in range(1, rn)]
    )

    def side_copy(d, e):
        zs = lax.rem(z + d, ZN)
        other = lax.rem(r + e, rn)
        return remote(
            dkv.at[zs * rn + other], side.at[e - 1, d], rs.at[d, e - 1], rr.at[d, e - 1],
            z * rn + other, t,
        )

    def q_copy(d):
        to = lax.rem(z + d, ZN)
        return remote(dq.at[to], q_out.at[z], qs.at[d - 1], qr.at[z], to * rn + r, t)

    def kv_copy(d):
        to = lax.rem(z + d, ZN)
        return remote(stage.at[d], kv_out.at[z], ks.at[d - 1], kr.at[z], to * rn + r, t)

    order = list(range(1, ZN)) + [0]
    for d in order:
        for e in range(1, rn):
            side_copy(d, e).start()
    for d in range(1, ZN):
        q_copy(d).start()
    q_out[z] = dq[z]
    for d in order:
        zs = lax.rem(z + d, ZN)
        total = dkv[zs * rn + r].astype(F32)
        for e in range(1, rn):
            side_copy(d, e).wait_recv()
            total = total + side[e - 1, d].astype(F32)
        if d == 0:
            kv_out[z] = total.astype(BF16)
        else:
            stage[d] = total.astype(BF16)
            kv_copy(d).start()
    for d in range(1, ZN):
        zs = lax.rem(z + d, ZN)
        remote(dq.at[0], q_out.at[zs], qs.at[0], qr.at[zs], s, t).wait_recv()
        remote(stage.at[d], kv_out.at[zs], ks.at[0], kr.at[zs], s, t).wait_recv()
    for d in range(1, ZN):
        q_copy(d).wait_send()
        kv_copy(d).wait_send()
    for d in order:
        for e in range(1, rn):
            side_copy(d, e).wait_send()


def exchange_dkv(plan, dq, dkv, cid):
    rn = plan.r
    rows = F_DEV * TOK_FRAME
    return call(
        functools.partial(dkv_kernel, plan),
        (
            jax.ShapeDtypeStruct((ZN, TOK_FRAME, LANES), BF16),
            jax.ShapeDtypeStruct((ZN, rows, LANES), BF16),
        ),
        [
            pltpu.VMEM((ZN, rows, LANES), BF16),
            pltpu.VMEM((rn - 1, ZN, rows, LANES), BF16),
            DMA((ZN - 1,)), DMA((ZN - 1,)), DMA((ZN, rn - 1)),
            DMA((ZN,)), DMA((ZN,)), DMA((ZN, rn - 1)),
        ],
        [VM, VM],
        cid,
        name="exchange_dkv",
    )(dq, dkv)


def padded(rows, low):
    zero = jnp.zeros_like(rows)
    return jnp.concatenate([rows, zero] if low else [zero, rows], axis=1)


def attend_kernel(plan, meta, q, kv, o, ot, lse, m_ref, l_ref, acc):
    r = meta[plan.frames]
    scale = HEAD ** (-0.5)

    def group(zq, carry):
        parts = []
        for f in range(F_DEV):
            frame = (zq * plan.r + r) * F_DEV + f
            clip = meta[frame]
            pack = q[zq]
            qz = padded(pack[:, f * HEAD : (f + 1) * HEAD], True) * jnp.asarray(scale, BF16)
            m_ref[...] = jnp.full_like(m_ref, -1e30)
            l_ref[...] = jnp.zeros_like(l_ref)
            acc[...] = jnp.zeros_like(acc)

            def block(j, inner):
                @pl.when(meta[j] == clip)
                def _():
                    rows = pl.multiple_of(lax.rem(j, F_DEV) * TOK_FRAME, TOK_FRAME)
                    keys = kv[lax.div(j, F_DEV), pl.ds(rows, TOK_FRAME), :]
                    st = mm_nt(keys, qz)
                    m_old = m_ref[...]
                    m_new = jnp.maximum(m_old, jnp.max(st, axis=0, keepdims=True))
                    p = jnp.exp(st - m_new)
                    alpha = jnp.exp(m_old - m_new)
                    m_ref[...] = m_new
                    l_ref[...] = l_ref[...] * alpha + jnp.sum(p, axis=0, keepdims=True)
                    acc[...] = acc[...] * alpha + mm_tn(keys, p.astype(BF16))

                return inner

            lax.fori_loop(0, frame + 1, block, 0)
            total = l_ref[...]
            out = acc[HEAD:, :] / total
            ot[zq * F_DEV + f] = out
            lse[zq * F_DEV + f] = m_ref[...] + jnp.log(total)
            parts.append(out.T)
        o[zq] = jnp.concatenate(parts, axis=1).astype(BF16)
        return carry

    lax.fori_loop(0, ZN, group, 0)


def attend(plan, meta, q, kv):
    frames = ZN * F_DEV
    return call(
        functools.partial(attend_kernel, plan),
        (
            jax.ShapeDtypeStruct((ZN, TOK_FRAME, LANES), BF16),
            jax.ShapeDtypeStruct((frames, HEAD, TOK_FRAME), F32),
            jax.ShapeDtypeStruct((frames, 1, TOK_FRAME), F32),
        ),
        [
            pltpu.VMEM((1, TOK_FRAME), F32),
            pltpu.VMEM((1, TOK_FRAME), F32),
            pltpu.VMEM((LANES, TOK_FRAME), F32),
        ],
        [SM, VM, VM],
        name="attend",
    )(meta, q, kv)


def attend_back_kernel(plan, meta, q, kv, do, ot, lse, dq, dkv, dkv_acc, dq_acc):
    r = meta[plan.frames]
    scale = HEAD ** (-0.5)
    dkv_acc[...] = jnp.zeros_like(dkv_acc)

    def group(zq, carry):
        parts = []
        for f in range(F_DEV):
            frame = (zq * plan.r + r) * F_DEV + f
            clip = meta[frame]
            columns = slice(f * HEAD, (f + 1) * HEAD)
            qz = padded(q[zq][:, columns], True) * jnp.asarray(scale, BF16)
            grads = do[zq][:, columns]
            doz = padded(grads, False)
            delta = jnp.sum(grads.astype(F32).T * ot[zq * F_DEV + f], axis=0, keepdims=True)
            logs = lse[zq * F_DEV + f]
            dq_acc[...] = jnp.zeros_like(dq_acc)

            def block(j, inner):
                @pl.when(meta[j] == clip)
                def _():
                    g = lax.div(j, F_DEV)
                    rows = pl.multiple_of(lax.rem(j, F_DEV) * TOK_FRAME, TOK_FRAME)
                    keys = kv[g, pl.ds(rows, TOK_FRAME), :]
                    pt = jnp.exp(mm_nt(keys, qz) - logs)
                    dst = (pt * (mm_nt(keys, doz) - delta)).astype(BF16)
                    dkv_acc[g, pl.ds(rows, TOK_FRAME), :] += mm(dst, qz) + mm(pt.astype(BF16), doz)
                    dq_acc[...] += mm_tn(keys, dst)

                return inner

            lax.fori_loop(0, frame + 1, block, 0)
            parts.append((dq_acc[:HEAD, :] * scale).T)
        dq[zq] = jnp.concatenate(parts, axis=1).astype(BF16)
        return carry

    lax.fori_loop(0, ZN, group, 0)
    dkv[...] = dkv_acc[...].astype(BF16)


def attend_back(plan, meta, q, kv, do, ot, lse):
    return call(
        functools.partial(attend_back_kernel, plan),
        (
            jax.ShapeDtypeStruct((ZN, TOK_FRAME, LANES), BF16),
            jax.ShapeDtypeStruct((plan.n, F_DEV * TOK_FRAME, LANES), BF16),
        ),
        [
            pltpu.VMEM((plan.n, F_DEV * TOK_FRAME, LANES), F32),
            pltpu.VMEM((LANES, TOK_FRAME), F32),
        ],
        [SM, VM, VM, VM, VM, VM],
        name="attend_back",
    )(meta, q, kv, do, ot, lse)


def total_kernel(chunks, part, out, sbuf, cbuf, ybuf, yrecv, ss, cs, ys, yr, osem, orsem):
    s = lax.axis_index("seq")
    t = lax.axis_index("tp")
    core = lax.rem(t, 2)
    sibling = t + 1 - 2 * core
    across = lax.rem(t + 2, TP)
    greet([(s, sibling), (s, across)])
    half = TOK_FRAME
    rows = half // chunks
    mine = core * half
    theirs = half - mine

    def c_copy(ch):
        return remote(sbuf.at[ch], cbuf.at[ch], ss.at[ch], cs.at[ch], s, sibling)

    def y_copy(ch):
        return remote(ybuf.at[ch], yrecv.at[ch], ys.at[ch], yr.at[ch], s, across)

    def o_copy(ch, base):
        ref = out.at[pl.ds(pl.multiple_of(base + ch * rows, rows), rows)]
        return remote(ref, ref, osem.at[ch], orsem.at[ch], s, sibling)

    for ch in range(chunks):
        sbuf[ch] = part[pl.ds(pl.multiple_of(theirs + ch * rows, rows), rows), :].astype(BF16)
        c_copy(ch).start()
    for ch in range(chunks):
        c_copy(ch).wait_recv()
        ybuf[ch] = (
            part[pl.ds(pl.multiple_of(mine + ch * rows, rows), rows), :] + cbuf[ch].astype(F32)
        ).astype(BF16)
        y_copy(ch).start()
    for ch in range(chunks):
        y_copy(ch).wait_recv()
        out[pl.ds(pl.multiple_of(mine + ch * rows, rows), rows), :] = ybuf[ch].astype(F32) + yrecv[
            ch
        ].astype(F32)
        o_copy(ch, mine).start()
    for ch in range(chunks):
        o_copy(ch, theirs).wait_recv()
    for ch in range(chunks):
        c_copy(ch).wait_send()
        y_copy(ch).wait_send()
        o_copy(ch, mine).wait_send()


def total_tp(part, cid, name):
    chunks = 4
    rows = TOK_FRAME // chunks
    buf = pltpu.VMEM((chunks, rows, D), BF16)
    return call(
        functools.partial(total_kernel, chunks),
        jax.ShapeDtypeStruct(part.shape, F32),
        [buf] * 4 + [DMA((chunks,))] * 6,
        [VM],
        cid,
        name=name,
    )(part)


def scatter_kernel(plan, gq, gb, oq, ob, rq, rb, cq, cb, rs, rr, cs, cr):
    s, t, z, r = place(plan)
    rn = plan.r
    greet(
        [(z * rn + lax.rem(r + d, rn), t) for d in range(1, rn)]
        + [(lax.rem(z + d, ZN) * rn + r, t) for d in (1, ZN - 1)]
    )

    def own(k, kind):
        if kind == "q":
            return gq.at[pl.ds(pl.multiple_of(k * plan.uq, plan.uq), plan.uq)]
        return gb.at[pl.ds(pl.multiple_of((k - plan.nq) * plan.ub, plan.ub), plan.ub)]

    a = 2 - lax.div(z, 2)
    b = 2 * lax.div(ZN - 1 - z, ZN - 1)

    def owner(j):
        return lax.rem(a * j + b, 3)

    def side_copy(zo, i, d, kind):
        other = lax.rem(r + d, rn)
        k = 3 * (zo * rn + other) + i
        lu = 3 * zo + i
        buf = rq if kind == "q" else rb
        return k, remote(
            own(k, kind), buf.at[d - 1, lu], rs.at[lu, d - 1], rr.at[lu, d - 1], z * rn + other, t
        )

    def chain_copy(lu, kind, side, to):
        src = (rq if kind == "q" else rb).at[0, lu]
        dst = (cq if kind == "q" else cb).at[side, lu]
        return remote(src, dst, cs.at[lu], cr.at[lu, side], to, t)

    for j in range(3):
        for i in range(3):
            for d in range(1, rn):
                k = 3 * (owner(j) * rn + lax.rem(r + d, rn)) + i
                by_kind(plan, k, lambda kind: side_copy(owner(j), i, d, kind)[1].start())

    for j in range(3):
        zo = owner(j)
        for i in range(3):
            k = 3 * (zo * rn + r) + i
            lu = 3 * zo + i

            def step(kind):
                side = rq if kind == "q" else rb
                chain = cq if kind == "q" else cb
                out = oq if kind == "q" else ob
                for d in range(1, rn):
                    remote(
                        own(k, kind), side.at[d - 1, lu], rs.at[lu, d - 1], rr.at[lu, d - 1], s, t
                    ).wait_recv()
                total = own(k, kind)[...].astype(F32)
                for d in range(1, rn):
                    total = total + side[d - 1, lu].astype(F32)
                out[i] = total

                @pl.when((zo <= z) & (z < ZN - 1))
                def _():
                    chain_copy(lu, kind, 0, s).wait_recv()
                    out[i] += chain[0, lu].astype(F32)

                @pl.when((zo >= z) & (z > 0))
                def _():
                    chain_copy(lu, kind, 1, s).wait_recv()
                    out[i] += chain[1, lu].astype(F32)

                @pl.when(zo != z)
                def _():
                    side[0, lu] = out[i].astype(BF16)

                @pl.when(zo < z)
                def _():
                    chain_copy(lu, kind, 0, s - rn).start()

                @pl.when(zo > z)
                def _():
                    chain_copy(lu, kind, 1, s + rn).start()

            by_kind(plan, k, step)

    for j in range(3):
        zo = owner(j)
        for i in range(3):
            for d in range(1, rn):
                k = 3 * (zo * rn + lax.rem(r + d, rn)) + i
                by_kind(plan, k, lambda kind: side_copy(zo, i, d, kind)[1].wait_send())
            k = 3 * (zo * rn + r) + i

            def close(kind):
                @pl.when(zo != z)
                def _():
                    chain_copy(3 * zo + i, kind, 0, s).wait_send()

            by_kind(plan, k, close)


def scatter_grads(plan, gq, gb, cid):
    rn = plan.r
    return call(
        functools.partial(scatter_kernel, plan),
        (
            jax.ShapeDtypeStruct((3, plan.uq, QKV), F32),
            jax.ShapeDtypeStruct((3, plan.ub, D), F32),
        ),
        [
            pltpu.VMEM((rn - 1, 9, plan.uq, QKV), BF16),
            pltpu.VMEM((rn - 1, 9, plan.ub, D), BF16),
            pltpu.VMEM((2, 9, plan.uq, QKV), BF16),
            pltpu.VMEM((2, 9, plan.ub, D), BF16),
            DMA((9, rn - 1)), DMA((9, rn - 1)), DMA((9,)), DMA((9, 2)),
        ],
        [VM, VM],
        cid,
        name="scatter_grads",
    )(gq, gb)


def adam_kernel(plan, meta, oq, ob, cond, dmod, master, one, two, average, n_master, n_one, n_two, n_average):
    s = meta[0]
    rate = RATE_FACTOR * D ** (-0.5)
    scale_one = 1.0 / (1.0 - BETA_FIRST**STEP)
    scale_two = 1.0 / (1.0 - BETA_SECOND**STEP)

    def update(rows, grad):
        first = BETA_FIRST * one[rows, :] + (1.0 - BETA_FIRST) * grad
        second = BETA_SECOND * two[rows, :] + (1.0 - BETA_SECOND) * grad * grad
        weight = master[rows, :]
        weight = weight - rate * (
            (first * scale_one) / (jnp.sqrt(second * scale_two) + ADAM_EPSILON)
            + WEIGHT_DECAY * weight
        )
        n_one[rows, :] = first
        n_two[rows, :] = second
        n_master[rows, :] = weight
        n_average[rows, :] = AVERAGE_RATE * average[rows, :] + (1.0 - AVERAGE_RATE) * weight

    for i in range(3):
        k = 3 * s + i
        base = i * plan.flat_rows

        def from_matrix(kind):
            src = oq if kind == "q" else ob
            rows = plan.uq if kind == "q" else plan.ub
            cols = (QKV if kind == "q" else D) // LANES
            for j in range(cols):
                update(
                    pl.ds(base + j, rows, stride=cols), src[i, :, j * LANES : (j + 1) * LANES]
                )

        by_kind(plan, k, from_matrix)

        @pl.when(k >= plan.nb)
        def _():
            at = cond[k - plan.nb]
            for j in range(MCOLS):
                update(
                    pl.ds(base + j, plan.um, stride=MCOLS),
                    mm(at, dmod[:, j * LANES : (j + 1) * LANES]),
                )


def adam(plan, meta, oq, ob, cond_rows, dmod, master, one, two, average):
    shape = jax.ShapeDtypeStruct(master.shape, F32)
    return call(
        functools.partial(adam_kernel, plan),
        (shape,) * 4,
        [],
        [SM] + [VM] * 8,
        name="adam",
    )(meta, oq, ob, cond_rows, dmod, master, one, two, average)


def normalize(rows):
    centred = rows - jnp.mean(rows, axis=1, keepdims=True)
    inverse = lax.rsqrt(jnp.mean(centred * centred, axis=1, keepdims=True) + NORM_EPSILON)
    return (centred * inverse, inverse)


def norm_back(grads, normed, inverse):
    return inverse * (
        grads
        - jnp.mean(grads, axis=1, keepdims=True)
        - normed * jnp.mean(grads * normed, axis=1, keepdims=True)
    )


def by_frame(rows):
    return rows.reshape(F_DEV, TOK_FRAME, rows.shape[1])


def frame_scale(rows, factor):
    return (by_frame(rows) * factor[:, None, :]).reshape(rows.shape)


def frame_affine(rows, factor, offset_rows):
    return (by_frame(rows) * (1.0 + factor)[:, None, :] + offset_rows[:, None, :]).reshape(
        rows.shape
    )


def frame_total(rows):
    return jnp.sum(by_frame(rows), axis=1)


def pack_heads(rows):
    return rows.reshape(F_DEV, TOK_FRAME, ZN, HEAD).transpose(2, 1, 0, 3).reshape(
        ZN, TOK_FRAME, F_DEV * HEAD
    )


def unpack_heads(packs):
    return packs.reshape(ZN, TOK_FRAME, F_DEV, HEAD).transpose(2, 1, 0, 3).reshape(
        F_DEV * TOK_FRAME, ZN * HEAD
    )


def local(
    tokens,
    grad_out,
    noise_level,
    context_mask,
    frame_clip,
    level_table,
    master,
    moment_one,
    moment_two,
    average,
):
    plan = Plan(lax.axis_size("seq"))
    s = lax.axis_index("seq")
    t = lax.axis_index("tp")
    rows = F_DEV * TOK_FRAME
    flat = lambda x: x.reshape(-1, LANES)

    effective = noise_level * (1 - context_mask)
    one_hot = (
        effective[:, None] == jnp.arange(level_table.shape[0], dtype=jnp.int32)[None, :]
    ).astype(BF16)
    condition = jax.nn.silu(mm(one_hot, level_table)).astype(BF16)
    cond_units = condition.reshape(plan.frames, plan.nm, plan.um).transpose(1, 0, 2)

    wq, wb, mod_blocks = gather_weights(plan, flat(master), cond_units, 0)
    w_out, w_up, w_down = wb[:HD], wb[HD : HD + FT], wb[HD + FT :]
    modulation = (
        mod_blocks.reshape(TP, F_DEV, MT).transpose(1, 0, 2).reshape(F_DEV, TP * MT)
    )
    shift_one, scale_one, gate_one, shift_two, scale_two, gate_two = [
        modulation[:, part * D : (part + 1) * D] for part in range(6)
    ]

    inputs = tokens.astype(F32)
    normed_one, inverse_one = normalize(inputs)
    first_in = frame_affine(normed_one, scale_one, shift_one).astype(BF16)
    projected = mm(first_in, wq).astype(BF16)
    kv = jnp.stack(
        [
            jnp.concatenate(
                [
                    projected[:, HD + h * HEAD : HD + (h + 1) * HEAD],
                    projected[:, 2 * HD + h * HEAD : 2 * HD + (h + 1) * HEAD],
                ],
                axis=1,
            )
            for h in range(ZN)
        ]
    )
    q_mine, kv_all = exchange_qkv(plan, pack_heads(projected[:, :HD]), kv, 1)
    meta = jnp.concatenate([frame_clip, lax.rem(s, plan.r)[None]]).astype(jnp.int32)
    o_mine, o_rows, lse = attend(plan, meta, q_mine, kv_all)
    attended = unpack_heads(exchange_heads(plan, o_mine, 2, "exchange_o"))
    attn = total_tp(mm(attended, w_out), 3, "total_attn")

    middle = inputs + frame_scale(attn, gate_one)
    normed_two, inverse_two = normalize(middle)
    second_in = frame_affine(normed_two, scale_two, shift_two).astype(BF16)
    up_rows = mm(second_in, w_up)
    activated, gelu_back = jax.vjp(functools.partial(jax.nn.gelu, approximate=True), up_rows)
    hidden = activated.astype(BF16)
    mlp = total_tp(mm(hidden, w_down), 4, "total_mlp")
    result = (middle + frame_scale(mlp, gate_two)).astype(BF16)
    upstream = grad_out.astype(F32)
    gate_two_grad = frame_total(mlp * upstream)
    mlp_grad = frame_scale(upstream, gate_two).astype(BF16)
    down_grad = mm_tn(hidden, mlp_grad)
    up_grad = gelu_back(mm_nt(mlp_grad, w_down))[0].astype(BF16)
    up_weight_grad = mm_tn(second_in, up_grad)
    second_grad = total_tp(mm_nt(up_grad, w_up), 5, "total_second")
    scale_two_grad = frame_total(second_grad * normed_two)
    shift_two_grad = frame_total(second_grad)
    middle_grad = upstream + norm_back(
        frame_scale(second_grad, 1.0 + scale_two), normed_two, inverse_two
    )
    gate_one_grad = frame_total(attn * middle_grad)
    attn_grad = frame_scale(middle_grad, gate_one).astype(BF16)
    out_weight_grad = mm_tn(attended, attn_grad)
    attended_grad = mm_nt(attn_grad, w_out).astype(BF16)
    do_mine = exchange_heads(plan, pack_heads(attended_grad), 6, "exchange_do")
    dq_mine, dkv_all = attend_back(plan, meta, q_mine, kv_all, do_mine, o_rows, lse)
    dq_heads, dkv_heads = exchange_dkv(plan, dq_mine, dkv_all, 7)
    qkv_grad = jnp.concatenate(
        [unpack_heads(dq_heads)]
        + [dkv_heads[h][:, :HEAD] for h in range(ZN)]
        + [dkv_heads[h][:, HEAD:] for h in range(ZN)],
        axis=1,
    )
    qkv_weight_grad = mm_tn(first_in, qkv_grad)
    first_grad = total_tp(mm_nt(qkv_grad, wq), 8, "total_first")
    scale_one_grad = frame_total(first_grad * normed_one)
    shift_one_grad = frame_total(first_grad)
    input_grad = middle_grad + norm_back(
        frame_scale(first_grad, 1.0 + scale_one), normed_one, inverse_one
    )
    mod_terms = jnp.concatenate(
        [
            shift_one_grad,
            scale_one_grad,
            gate_one_grad,
            shift_two_grad,
            scale_two_grad,
            gate_two_grad,
        ],
        axis=1,
    )
    mod_grad = lax.all_gather(
        lax.dynamic_slice_in_dim(mod_terms, t * MT, MT, axis=1), "seq", axis=0, tiled=True
    ).astype(BF16)
    grads_b = jnp.concatenate([out_weight_grad, up_weight_grad, down_grad], axis=0).astype(BF16)
    own_q, own_b = scatter_grads(plan, qkv_weight_grad.astype(BF16), grads_b, 9)
    updated = adam(
        plan,
        s[None].astype(jnp.int32),
        own_q,
        own_b,
        cond_units.transpose(0, 2, 1),
        mod_grad,
        flat(master),
        flat(moment_one),
        flat(moment_two),
        flat(average),
    )
    new_master, new_one, new_two, new_average = [x.reshape(master.shape) for x in updated]
    return (result, input_grad, new_master, new_one, new_two, new_average)


def solution(mesh):
    token_spec = P("seq", None)
    weight_spec = P("tp", "seq")
    in_specs = (token_spec, token_spec, P(), P(), P(), P()) + (weight_spec,) * 4
    out_specs = (token_spec, token_spec) + (weight_spec,) * 4
    return jax.shard_map(local, mesh=mesh, in_specs=in_specs, out_specs=out_specs, check_vma=False)
```

time: 2150 us -> 591 us (0.27)
  waiting for transfers between devices: 1290 us -> 0 us
  Pallas kernels: 0 us -> 440 us
  matrix products: 401 us -> 36.4 us
  local copies, waits for them, and re-layouts: 301 us -> 17.5 us
  other arithmetic: 107 us -> 54.4 us
  blocking collectives: 5.23 us -> 34.5 us
    unnamed x11 -> x0, waiting for transfers between devices: 595 us -> none
    all_gather x3 -> x0, waiting for transfers between devices: 468 us -> none  [the longest x1 361 us: local(): lax.all_gather(master.astype(jnp.bfloat16), 'seq', axis=1, tiled=True)[0]]
    pallas_call x0 -> x13, Pallas kernels: none -> 440 us  [the longest x4 104 us: total_tp(): call(functools.partial(total_kernel, chunks), jax.ShapeDtypeStruct(part.s...]
    dot_general x71 -> x13, matrix products: 401 us -> 36.4 us  [the longest x4 14.7 us: mm_nt(): lax.dot_general(left, right, (((1,), (1,)), ((), ())), preferred_element_...]
    psum x3 -> x0, waiting for transfers between devices: 183 us -> none  [the longest x1 109 us: local(): mlp = lax.psum(mlp_part, 'tp')]
    slice x5 -> x15, local copies, waits for them, and re-layouts: 141 us -> 2.06 us  [the longest x8 0.99 us: local(): dkv_heads[h][:, HEAD:]]
    reduce_scatter x1 -> x0, waiting for transfers between devices: 45.9 us -> none  [local(): lax.psum_scatter(map_blocks(produce, (all_keys, all_values), local_rows),...]
    dynamic_slice x73 -> x0, local copies, waits for them, and re-layouts: 45 us -> none  [the longest x48 43.1 us: fold_blocks(): lax.scan(fold_advance, running, (jnp.arange(block_count, dtype=jnp.int32)...]
  transfers between devices with their start and end apart: 9 -> 0, of which waited for: 9 -> 0; matrix products, arithmetic and copies ran while one was open for 12% -> 0% of each run, Pallas kernels for 0% -> 0%
where the time goes in v1:
time: 591 us; the launch traced here: 584 us
  Pallas kernels  440 us (74%)
  other arithmetic  54.4 us (9%)
  matrix products  36.4 us (6%)
  blocking collectives  34.5 us (6%)
  local copies, waits for them, and re-layouts  17.5 us (3%)
    pallas_call x4, Pallas kernels, total_tp(): call(functools.partial(total_kernel, chunks), jax.ShapeDtypeStruct(part.s...  104 us
    pallas_call x1, Pallas kernels, scatter_grads(): call(functools.partial(scatter_kernel, plan), (jax.ShapeDtypeStruct((3, p...  88.3 us
    pallas_call x1, Pallas kernels, gather_weights(): call(functools.partial(gather_kernel, plan), (jax.ShapeDtypeStruct((D, QK...  87.1 us
    pallas_call x1, Pallas kernels, exchange_qkv(): call(functools.partial(qkv_kernel, plan), (jax.ShapeDtypeStruct((ZN, TOK_...  40.3 us
    pallas_call x2, Pallas kernels, exchange_heads(): call(functools.partial(heads_kernel, plan), jax.ShapeDtypeStruct(x.shape,...  35.1 us
    all_gather x1, blocking collectives, local(): lax.all_gather(lax.dynamic_slice_in_dim(mod_terms, t * MT, MT, axis=1), '...  34.5 us
    pallas_call x1, Pallas kernels, exchange_dkv(): call(functools.partial(dkv_kernel, plan), (jax.ShapeDtypeStruct((ZN, TOK_...  34.2 us
    pallas_call x1, Pallas kernels, attend_back(): call(functools.partial(attend_back_kernel, plan), (jax.ShapeDtypeStruct((...  19.5 us

profile of v1, /device:TPU:0, one launch (start us, length us, event | category | flops | bytes accessed | tf_op | source)
XLA Modules:
  0.0 584.3 jit_solution(15137563917575380773)
XLA Ops:
  7.9 87.1 %gather_weights.1 = (bf16[1024,768]{1,0:T(8,128)(2,1)}, bf16[2304,1024]{1,0:T(8,128)(2,1)}, f32[4,24,128]{2,1,0:T(8,128)}) custom-call(f32[4608,128]{1,0:T(8,128)} %bitcast.137, bf16[8,16,128]{2,1,0:T(8,128)(2,1)} %copy.43.cond), custom_call_target="tpu_custom_call" | custom-call | tf_op jit(solution)/shard_map/gather_weights/pallas_call | solution.py:271
  96.4 4.8 fusion.18
  105.8 40.3 %exchange_qkv.1 = (bf16[4,384,128]{2,1,0:T(8,128)(2,1)}, bf16[8,768,128]{2,1,0:T(8,128)(2,1)}) custom-call(bf16[4,384,128]{2,1,0:T(8,128)(2,1)} %copy.47.q, bf16[4,768,128]{2,1,0:T(8,128)(2,1)} %pad_maximum_fusion.1.kv), custom_call_target="tpu_custom_call" | custom-call | tf_op jit(solution)/shard_map/exchange_qkv/pallas_call | solution.py:347
  146.1 19.1 %attend.1 = (bf16[4,384,128]{2,1,0:T(8,128)(2,1)}, f32[8,64,384]{2,1,0:T(8,128)}, f32[8,1,384]{2,1,0:T(1,128)}) custom-call(s32[17]{0:T(128)} %pad_add_fusion.meta, bf16[4,384,128]{2,1,0:T(8,128)(2,1)} %get-tuple-element.26.q, bf16[8,768,128]{2,1,0:T(8,128)(2,1)} %get-tuple-element.27.kv), custom_call_target="tpu_custom_call" | custom-call | tf_op jit(solution)/shard_map/attend/pallas_call | solution.py:515
  165.2 22.2 %exchange_o.1 = bf16[4,384,128]{2,1,0:T(8,128)(2,1)} custom-call(bf16[4,384,128]{2,1,0:T(8,128)(2,1)} %get-tuple-element.28.x), custom_call_target="tpu_custom_call" | custom-call | tf_op jit(solution)/shard_map/exchange_o/pallas_call | solution.py:380
  189.1 3.3 fusion.39.part
  192.4 25.5 %total_attn.1 = f32[768,1024]{1,0:T(8,128)} custom-call(f32[768,1024]{1,0:T(8,128)} %fusion.39.part), custom_call_target="tpu_custom_call" | custom-call | tf_op jit(solution)/shard_map/total_attn/pallas_call | solution.py:637
  224.2 4.7 fusion.16
  228.9 3.4 convolution_convert_fusion
  232.3 3.7 fusion.30.part
  236.0 26.6 %total_mlp.1 = f32[768,1024]{1,0:T(8,128)} custom-call(f32[768,1024]{1,0:T(8,128)} %fusion.30.part), custom_call_target="tpu_custom_call" | custom-call | tf_op jit(solution)/shard_map/total_mlp/pallas_call | solution.py:637
  262.6 3.2 convolution_convert_fusion.1
  265.8 5.1 fusion.34.part
  270.9 26.5 %total_second.1 = f32[768,1024]{1,0:T(8,128)} custom-call(f32[768,1024]{1,0:T(8,128)} %fusion.34.part), custom_call_target="tpu_custom_call" | custom-call | tf_op jit(solution)/shard_map/total_second/pallas_call | solution.py:637
  297.4 2.7 reduce_sum.137
  300.1 2.9 fusion.26
  303.9 7.7 %convert_multiply_fusion = (f32[768,1024]{1,0:T(8,128)}, bf16[768,1024]{1,0:T(8,128)(2,1)}, f32[768,1024]{1,0:T(8,128)}, f32[768,1024]{1,0:T(8,128)}, f32[768,1024]{1,0:T(8,128)}) fusion(f32[768,1024]{1,0:T(8,128)} %total_mlp.1, bf16[768,1024]{1,0:T(8,128)(2,1)} %param.11, f32[768,1024]{1,0:T(8,128)S(1)} %get-tuple-element.49, f32[2,1024]{1,0:T(2,128)S(1)} %copy-done.23, ...), kind=kLoop, calls=%fused_computation.8 | loop fusion | flops 11796480 | bytes 28340224 | tf_op jit(solution)/shard_map/mul | solution.py:930
  311.5 2.7 reduce_sum.139
  314.2 2.8 reduce_sum.138
  317.0 2.6 reduce_sum.136
  322.5 2.7 pad_maximum_fusion.gb
  326.5 12.8 %exchange_do.1.do = bf16[4,384,128]{2,1,0:T(8,128)(2,1)} custom-call(bf16[4,384,128]{2,1,0:T(8,128)(2,1)} %copy.52.x), custom_call_target="tpu_custom_call" | custom-call | tf_op jit(solution)/shard_map/exchange_do/pallas_call | solution.py:380
  339.3 19.5 %attend_back.1 = (bf16[4,384,128]{2,1,0:T(8,128)(2,1)}, bf16[8,768,128]{2,1,0:T(8,128)(2,1)}) custom-call(s32[17]{0:T(128)} %pad_add_fusion.meta, bf16[4,384,128]{2,1,0:T(8,128)(2,1)} %get-tuple-element.26.q, bf16[8,768,128]{2,1,0:T(8,128)(2,1)} %get-tuple-element.27.kv, bf16[4,384,128]{2,1,0:T(8,128)(2,1)} %exchange_do.1.do, ...), custom_call_target="tpu_custom_call" | custom-call | tf_op jit(solution)/shard_map/attend_back/pallas_call | solution.py:573
  358.9 34.2 %exchange_dkv.1 = (bf16[4,384,128]{2,1,0:T(8,128)(2,1)}, bf16[4,768,128]{2,1,0:T(8,128)(2,1)}) custom-call(bf16[4,384,128]{2,1,0:T(8,128)(2,1)} %get-tuple-element.32.dq, bf16[8,768,128]{2,1,0:T(8,128)(2,1)} %get-tuple-element.33.dkv), custom_call_target="tpu_custom_call" | custom-call | tf_op jit(solution)/shard_map/exchange_dkv/pallas_call | solution.py:447
  402.4 3.9 convolution_convert_fusion.2.gq
  406.3 88.3 %scatter_grads.1 = (f32[3,256,768]{2,1,0:T(8,128)}, f32[3,192,1024]{2,1,0:T(8,128)}) custom-call(bf16[1024,768]{1,0:T(8,128)(2,1)} %convolution_convert_fusion.2.gq, bf16[2304,1024]{1,0:T(8,128)(2,1)} %pad_maximum_fusion.gb), custom_call_target="tpu_custom_call" | custom-call | tf_op jit(solution)/shard_map/scatter_grads/pallas_call | solution.py:747
  494.6 3.1 fusion.51.part
  497.7 25.7 %total_first.1 = f32[768,1024]{1,0:T(8,128)} custom-call(f32[768,1024]{1,0:T(8,128)} %fusion.51.part), custom_call_target="tpu_custom_call" | custom-call | tf_op jit(solution)/shard_map/total_first/pallas_call | solution.py:637
  525.8 3.1 fusion.25
  528.9 5.7 fusion.2
  536.9 34.5 %all-gather = bf16[8,2,1536]{2,1,0:T(2,128)(2,1)S(1)} all-gather(bf16[1,2,1536]{2,1,0:T(2,128)(2,1)S(1)} %dynamic-slice_bitcast_fusion), channel_id=1, replica_groups=mesh['seq'=8,'tp'=4] {'seq'}, dimensions={0}, use_global_device_ids=true | all-gather | bytes 55296 | tf_op jit(solution)/shard_map/all_gather | solution.py:972
  572.0 12.1 %adam.1 = (f32[4608,128]{1,0:T(8,128)}, f32[4608,128]{1,0:T(8,128)}, f32[4608,128]{1,0:T(8,128)}, f32[4608,128]{1,0:T(8,128)}) custom-call(s32[1]{0:T(128)} %bitcast.29.meta, f32[3,256,768]{2,1,0:T(8,128)} %get-tuple-element.36.oq, f32[3,192,1024]{2,1,0:T(8,128)} %get-tuple-element.37.ob, bf16[8,128,16]{2,1,0:T(8,128)(2,1)} %bitcast.142, ...), custom_call_target="tpu_custom_call" | custom-call | tf_op jit(solution)/shard_map/adam/pallas_call | solution.py:812
  (155 shorter events, 40.3 us)
Async XLA Ops:
  0.6 5.8 %copy-start = (bf16[1000,1024]{1,0:T(8,128)(2,1)S(1)}, bf16[1000,1024]{1,0:T(8,128)(2,1)}, u32[]{:S(2)}) copy-start(bf16[1000,1024]{1,0:T(8,128)(2,1)} %param.15) | copy-start | bytes 6144004
  4.5 91.9 %copy-start.18 = (f32[768]{0:T(1024)}, f32[768]{0:T(1024)S(1)}, u32[]{:S(2)}) copy-start(f32[768]{0:T(1024)S(1)} %broadcast_multiply_fusion.5) | copy-start | bytes 9220
  6.5 94.7 %copy-start.26 = (f32[768]{0:T(1024)}, f32[768]{0:T(1024)S(1)}, u32[]{:S(2)}) copy-start(f32[768]{0:T(1024)S(1)} %add_rsqrt_fusion.1) | copy-start | bytes 9220
  7.1 94.1 %copy-start.8 = (bf16[16,1024]{0,1:T(8,128)(2,1)}, bf16[16,1024]{0,1:T(8,128)(2,1)S(1)}, u32[]{:S(2)}) copy-start(bf16[16,1024]{0,1:T(8,128)(2,1)S(1)} %copy.42) | copy-start | bytes 98308
  96.4 4.8 copy-start.22
  96.4 4.8 copy-start.33
  192.4 25.5 %copy-start.2 = (bf16[768,1024]{1,0:T(8,128)(2,1)S(1)}, bf16[768,1024]{1,0:T(8,128)(2,1)}, u32[]{:S(2)}) copy-start(bf16[768,1024]{1,0:T(8,128)(2,1)} %param.10) | copy-start | bytes 4718596
  192.4 25.5 %copy-start.20 = (f32[2,1024]{1,0:T(2,128)S(1)}, f32[2,1024]{1,0:T(2,128)}, u32[]{:S(2)}) copy-start(f32[2,1024]{1,0:T(2,128)} %get-tuple-element.81) | copy-start | bytes 24580
  217.9 4.4 slice-start
  221.1 3.0 copy-start.24
  236.0 26.6 %copy-start.35 = (bf16[768,1024]{1,0:T(8,128)(2,1)S(1)}, bf16[768,1024]{1,0:T(8,128)(2,1)}, u32[]{:S(2)}) copy-start(bf16[768,1024]{1,0:T(8,128)(2,1)} %fusion.16) | copy-start | bytes 4718596
  300.0 3.0 copy-start.4
  300.1 3.8 copy-start.6
  300.1 3.8 copy-start.17
  300.1 3.8 copy-start.23
  300.1 3.8 copy-start.25
  314.2 5.5 copy-start.7
  314.2 5.5 copy-start.21
  320.1 2.4 copy-start.9
  320.1 2.4 copy-start.10
  393.0 2.5 copy-start.14
  395.8 6.6 %copy-start.12 = (bf16[768,1024]{1,0:T(8,128)(2,1)S(1)}, bf16[768,1024]{1,0:T(8,128)(2,1)}, u32[]{:S(2)}) copy-start(bf16[768,1024]{1,0:T(8,128)(2,1)} %copy-done.11) | copy-start | bytes 4718596
  406.3 88.3 %copy-start.15 = (bf16[768,768]{0,1:T(8,128)(2,1)S(1)}, bf16[768,768]{0,1:T(8,128)(2,1)}, u32[]{:S(2)}) copy-start(bf16[768,768]{0,1:T(8,128)(2,1)} %constant_dynamic-update-slice_fusion) | copy-start | bytes 3538948
  406.3 88.3 %copy-start.34 = (bf16[1024,768]{1,0:T(8,128)(2,1)S(1)}, bf16[1024,768]{1,0:T(8,128)(2,1)}, u32[]{:S(2)}) copy-start(bf16[1024,768]{1,0:T(8,128)(2,1)} %get-tuple-element.25) | copy-start | bytes 4718596
  523.4 2.4 copy-start.3
  523.4 2.3 copy-start.19
  523.5 2.3 copy-start.27
  525.8 3.1 copy-start.5
  534.6 2.1 copy-start.29
  534.6 2.2 copy-start.31
  534.6 2.2 copy-start.30
  572.0 12.1 %copy-start.1 = (bf16[1000,1024]{1,0:T(8,128)(2,1)S(1)}, bf16[1000,1024]{1,0:T(8,128)(2,1)}, u32[]{:S(2)}) copy-start(bf16[1000,1024]{1,0:T(8,128)(2,1)} %param.15) | copy-start | bytes 6144004
  (6 other events, 9.7 us)

commit v2 on v1

--- a/solution.py
+++ b/solution.py
@@ -23,6 +23,9 @@
 BROWS = HD + 2 * FT
 LANES = 128
 MCOLS = MT // LANES
+PACK = TOK_FRAME // 2
+TILE = 256
+TILES = D // TILE
 
 NORM_EPSILON = 1e-06
 RATE_FACTOR = 2.5
@@ -31,6 +34,8 @@
 ADAM_EPSILON = 1e-08
 WEIGHT_DECAY = 0.01
 AVERAGE_RATE = 0.9
+GELU_A = 0.7978845608028654
+GELU_B = 0.044715
 MESH = pl.DeviceIdType.MESH
 VM = pl.BlockSpec(memory_space=pltpu.VMEM)
 SM = pl.BlockSpec(memory_space=pltpu.SMEM)
@@ -50,6 +55,20 @@
 
 def mm_nt(left, right):
     return lax.dot_general(left, right, (((1,), (1,)), ((), ())), preferred_element_type=F32)
+
+
+def normalize(rows):
+    centred = rows - jnp.mean(rows, axis=1, keepdims=True)
+    inverse = lax.rsqrt(jnp.mean(centred * centred, axis=1, keepdims=True) + NORM_EPSILON)
+    return (centred * inverse, inverse)
+
+
+def norm_back(grads, normed, inverse):
+    return inverse * (
+        grads
+        - jnp.mean(grads, axis=1, keepdims=True)
+        - normed * jnp.mean(grads * normed, axis=1, keepdims=True)
+    )
 
 
 class Plan:
@@ -119,8 +138,8 @@
 
 
 def gather_kernel(
-    plan, master, cond, wq, wb, mod, tile, macc, mpart, mrecv,
-    send_sem, recv_sem, msend, mrecv_sem, tsend, trecv,
+    plan, master, cond, wq, wb, mod, wo, tile, macc, mpart, mrecv,
+    send_sem, recv_sem, msend, mrecv_sem, tsend, trecv, osend, orecv,
 ):
     s, t, z, r = place(plan)
     n, rn = plan.n, plan.r
@@ -237,8 +256,13 @@
                 k = 3 * (zs * rn + other) + i
                 by_kind(plan, k, lambda kind: move(k, 3 * zs + i, kind, 0, other, s).wait_recv())
 
+    wo[t] = wb[:HD]
+    for d in range(1, TP):
+        remote(wo.at[t], wo.at[t], osend.at[d - 1], orecv.at[t], s, lax.rem(t + d, TP)).start()
     for d in range(1, TP):
         other = lax.rem(t + d, TP)
+        remote(wo.at[t], wo.at[other], osend.at[0], orecv.at[other], s, t).wait_recv()
+        remote(wo.at[t], wo.at[t], osend.at[d - 1], orecv.at[t], s, other).wait_send()
         remote(mod.at[t], mod.at[other], tsend.at[0], trecv.at[other], s, t).wait_recv()
         remote(mod.at[t], mod.at[t], tsend.at[d - 1], trecv.at[t], s, other).wait_send()
 
@@ -274,6 +298,7 @@
             jax.ShapeDtypeStruct((D, QKV), BF16),
             jax.ShapeDtypeStruct((BROWS, D), BF16),
             jax.ShapeDtypeStruct((TP, mrows, LANES), F32),
+            jax.ShapeDtypeStruct((TP, HD, D), BF16),
         ),
         [
             pltpu.VMEM((plan.um, MT), BF16),
@@ -284,6 +309,8 @@
             DMA((3 * ZN, plan.r)),
             DMA((n - 1,)),
             DMA((n - plan.first_mod,)),
+            DMA((TP - 1,)),
+            DMA((TP,)),
             DMA((TP - 1,)),
             DMA((TP,)),
         ],
@@ -355,36 +382,6 @@
         cid,
         name="exchange_qkv",
     )(q, kv)
-
-
-def heads_kernel(plan, x, out, send_sem, recv_sem):
-    s, t, z, r = place(plan)
-    rn = plan.r
-    greet([(lax.rem(z + d, ZN) * rn + r, t) for d in range(1, ZN)])
-
-    def copy(d):
-        to = lax.rem(z + d, ZN)
-        return remote(x.at[to], out.at[z], send_sem.at[d - 1], recv_sem.at[z], to * rn + r, t)
-
-    for d in range(1, ZN):
-        copy(d).start()
-    out[z] = x[z]
-    for d in range(1, ZN):
-        zs = lax.rem(z + d, ZN)
-        remote(x.at[0], out.at[zs], send_sem.at[0], recv_sem.at[zs], s, t).wait_recv()
-    for d in range(1, ZN):
-        copy(d).wait_send()
-
-
-def exchange_heads(plan, x, cid, name):
-    return call(
-        functools.partial(heads_kernel, plan),
-        jax.ShapeDtypeStruct(x.shape, x.dtype),
-        [DMA((ZN - 1,)), DMA((ZN,))],
-        [VM],
-        cid,
-        name=name,
-    )(x)
 
 
 def dkv_kernel(plan, dq, dkv, q_out, kv_out, stage, side, qs, ks, rs, qr, kr, rr):
@@ -472,7 +469,6 @@
     scale = HEAD ** (-0.5)
 
     def group(zq, carry):
-        parts = []
         for f in range(F_DEV):
             frame = (zq * plan.r + r) * F_DEV + f
             clip = meta[frame]
@@ -503,8 +499,8 @@
             out = acc[HEAD:, :] / total
             ot[zq * F_DEV + f] = out
             lse[zq * F_DEV + f] = m_ref[...] + jnp.log(total)
-            parts.append(out.T)
-        o[zq] = jnp.concatenate(parts, axis=1).astype(BF16)
+            rows = out.T
+            o[zq, f] = jnp.concatenate([rows[:PACK], rows[PACK:]], axis=1).astype(BF16)
         return carry
 
     lax.fori_loop(0, ZN, group, 0)
@@ -515,7 +511,7 @@
     return call(
         functools.partial(attend_kernel, plan),
         (
-            jax.ShapeDtypeStruct((ZN, TOK_FRAME, LANES), BF16),
+            jax.ShapeDtypeStruct((ZN, F_DEV, PACK, LANES), BF16),
             jax.ShapeDtypeStruct((frames, HEAD, TOK_FRAME), F32),
             jax.ShapeDtypeStruct((frames, 1, TOK_FRAME), F32),
         ),
@@ -541,7 +537,7 @@
             clip = meta[frame]
             columns = slice(f * HEAD, (f + 1) * HEAD)
             qz = padded(q[zq][:, columns], True) * jnp.asarray(scale, BF16)
-            grads = do[zq][:, columns]
+            grads = jnp.concatenate([do[zq, f][:, :HEAD], do[zq, f][:, HEAD:]], axis=0)
             doz = padded(grads, False)
             delta = jnp.sum(grads.astype(F32).T * ot[zq * F_DEV + f], axis=0, keepdims=True)
             logs = lse[zq * F_DEV + f]
@@ -644,6 +640,299 @@
     )(part)
 
 
+def loop(count, step, body):
+    def turn(i, carry):
+        body(pl.multiple_of(i * step, step))
+        return carry
+
+    lax.fori_loop(0, count // step, turn, 0)
+
+
+def add_to(ref, row, values):
+    ref[pl.ds(row, 1), :] += jnp.sum(values, axis=0, keepdims=True)
+
+
+def middle_kernel(
+    plan, o_mine, wo, wb, tokens, grad_out, mod,
+    result, gb, do_out, dmid, dmod,
+    oall, attended, attn, mid, norm, inv, sin, hidden, dmlp, dhid, dup,
+    own, csend, crecv, ysend, yrecv, dattn, dsend, dwo, wsend, wrecv,
+    o_s, o_r, f_s, f_r, n_s, n_r, c_s, c_r, y_s, y_r, d_s, d_r, w_s, w_r, e_s, e_r,
+):
+    s, t, z, r = place(plan)
+    rn = plan.r
+    y = lax.div(t, 2)
+    c = lax.rem(t, 2)
+    sib = 2 * y + 1 - c
+    across = lax.rem(t + 2, TP)
+    mine = pl.multiple_of(c * TOK_FRAME, TOK_FRAME)
+    theirs = pl.multiple_of((1 - c) * TOK_FRAME, TOK_FRAME)
+    pairs = [(d, e) for d in range(ZN) for e in range(2)][1:]
+
+    def partner(d, e):
+        return lax.rem(z + d, ZN), (c if e == 0 else 1 - c)
+
+    greet(
+        [(partner(d, e)[0] * rn + r, 2 * y + partner(d, e)[1]) for d, e in pairs]
+        + [(s, across)]
+    )
+
+    def o_copy(d, e):
+        zd, cd = partner(d, e)
+        return remote(
+            o_mine.at[zd, cd], oall.at[y * 8 + c * ZN + z], o_s.at[2 * d + e],
+            o_r.at[c * ZN + z], zd * rn + r, 2 * y + cd,
+        )
+
+    def f_copy(slot):
+        ref = oall.at[y * 8 + slot]
+        return remote(ref, ref, f_s.at[slot], f_r.at[slot], s, across)
+
+    for d, e in pairs:
+        o_copy(d, e).start()
+    oall[y * 8 + c * ZN + z] = o_mine[z, c]
+    f_copy(c * ZN + z).start()
+
+    def d_mlp(f):
+        def body(at):
+            rows = pl.ds(f * TOK_FRAME + at, 64)
+            dmlp[rows, :] = (grad_out[rows, :].astype(F32) * mod[f * 6 + 5 : f * 6 + 6, :]).astype(
+                BF16
+            )
+
+        loop(TOK_FRAME, 64, body)
+
+    for f in range(F_DEV):
+        d_mlp(f)
+
+    def d_hidden(at):
+        dhid[:, pl.ds(at, TILE)] = mm_nt(dmlp[...], wb[pl.ds(HD + FT + at, TILE), :])
+
+    loop(FT, TILE, d_hidden)
+
+    for d, e in pairs:
+        zd, cd = partner(d, e)
+        slot = cd * ZN + zd
+        remote(o_mine.at[0, 0], oall.at[y * 8 + slot], o_s.at[0], o_r.at[slot], s, t).wait_recv()
+        f_copy(slot).start()
+    for slot in range(8):
+        remote(
+            oall.at[0], oall.at[(1 - y) * 8 + slot], f_s.at[slot], f_r.at[slot], s, t
+        ).wait_recv()
+    for m in range(HEADS // 2):
+        a, b = oall[2 * m], oall[2 * m + 1]
+        cols = slice(m * LANES, (m + 1) * LANES)
+        attended[:PACK, cols] = jnp.concatenate([a[:, :HEAD], b[:, :HEAD]], axis=1)
+        attended[PACK:, cols] = jnp.concatenate([a[:, HEAD:], b[:, HEAD:]], axis=1)
+
+    def attn_tile(at):
+        attn[:, pl.ds(at, TILE)] = mm(attended[...], wo[:, pl.ds(at, TILE)])
+
+    loop(D, TILE, attn_tile)
+
+    row = lambda part: mod[pl.ds(c * 6 + part, 1), :]
+
+    def norm_rows(at):
+        rows = pl.ds(at, 64)
+        values = tokens[pl.ds(mine + at, 64), :].astype(F32) + row(2) * attn[rows, :]
+        mid[rows, :] = values
+        normed, inverse = normalize(values)
+        norm[rows, :] = normed
+        inv[rows, :] = inverse
+        sin[pl.ds(mine + at, 64), :] = (normed * (1.0 + row(4)) + row(3)).astype(BF16)
+
+    loop(TOK_FRAME, 64, norm_rows)
+
+    def n_copy(base):
+        ref = sin.at[pl.ds(base, TOK_FRAME)]
+        return remote(ref, ref, n_s.at[0], n_r.at[0], s, sib)
+
+    n_copy(mine).start()
+
+    def feed(base):
+        rows = pl.ds(base, TOK_FRAME)
+
+        def tile(at):
+            cols = pl.ds(at, TILE)
+            u = mm(sin[rows, :], wb[HD : HD + FT, cols])
+            square = u * u
+            inner = GELU_A * u * (1.0 + GELU_B * square)
+            th = jnp.tanh(inner)
+            half = 0.5 * (1.0 + th)
+            hidden[rows, cols] = (u * half).astype(BF16)
+            slope = half + 0.5 * u * (1.0 - th * th) * (GELU_A * (1.0 + 3.0 * GELU_B * square))
+            dup[rows, cols] = (dhid[rows, cols] * slope).astype(BF16)
+
+        loop(FT, TILE, tile)
+
+    feed(mine)
+    n_copy(theirs).wait_recv()
+    feed(theirs)
+
+    def c_copy(w, n):
+        return remote(csend.at[w, n], crecv.at[w, n], c_s.at[w, n], c_r.at[w, n], s, sib)
+
+    def y_copy(w, n):
+        return remote(ysend.at[w, n], yrecv.at[w, n], y_s.at[w, n], y_r.at[w, n], s, across)
+
+    def pass_on(w, n):
+        c_copy(w, n).wait_recv()
+        ysend[w, n] = (own[n] + crecv[w, n].astype(F32)).astype(BF16)
+        y_copy(w, n).start()
+
+    def product(w, base, n):
+        rows = pl.ds(base, TOK_FRAME)
+        if w == 0:
+            return mm_nt(dup[rows, :], wb[HD + n * TILE : HD + (n + 1) * TILE, :])
+        return mm(hidden[rows, :], wb[HD + FT :, n * TILE : (n + 1) * TILE])
+
+    for w in range(2):
+        for n in range(TILES):
+            csend[w, n] = product(w, theirs, n).astype(BF16)
+            c_copy(w, n).start()
+            own[n] = product(w, mine, n)
+            if n:
+                pass_on(w, n - 1)
+        pass_on(w, TILES - 1)
+
+    def down_grad(at):
+        gb[pl.ds(HD + FT + at, TILE), :] = mm_tn(hidden[:, pl.ds(at, TILE)], dmlp[...]).astype(BF16)
+
+    def up_grad(at):
+        gb[pl.ds(HD + at, TILE), :] = mm_tn(sin[:, pl.ds(at, TILE)], dup[...]).astype(BF16)
+
+    loop(FT, TILE, down_grad)
+    loop(D, TILE, up_grad)
+
+    dm = dmod.at[c]
+    dm[...] = jnp.zeros_like(dm)
+    for n in range(TILES):
+        y_copy(0, n).wait_recv()
+
+    def total(w, rows):
+        return jnp.concatenate(
+            [ysend[w, n, rows].astype(F32) + yrecv[w, n, rows].astype(F32) for n in range(TILES)],
+            axis=1,
+        )
+
+    def back_rows(at):
+        rows = pl.ds(at, 64)
+        tok_rows = pl.ds(mine + at, 64)
+        grads = total(0, rows)
+        normed = norm[rows, :]
+        add_to(dm, 1, grads)
+        add_to(dm, 2, grads * normed)
+        values = grad_out[tok_rows, :].astype(F32) + norm_back(
+            grads * (1.0 + row(4)), normed, inv[rows, :]
+        )
+        dmid[tok_rows, :] = values
+        add_to(dm, 0, attn[rows, :] * values)
+        dattn[rows, :] = (row(2) * values).astype(BF16)
+
+    loop(TOK_FRAME, 64, back_rows)
+    for ch in range(2):
+        part = mm_nt(dattn[...], wo[pl.ds(pl.multiple_of((2 * y + ch) * HD, HD), HD), :]).astype(BF16)
+        for zh in range(ZN):
+            cols = slice(zh * HEAD, (zh + 1) * HEAD)
+            dsend[ch * ZN + zh] = jnp.concatenate([part[:PACK, cols], part[PACK:, cols]], axis=1)
+
+    def d_copy(d, e):
+        zd, cd = partner(d, e)
+        return remote(
+            dsend.at[cd * ZN + zd], do_out.at[z, c], d_s.at[2 * d + e], d_r.at[2 * z + c],
+            zd * rn + r, 2 * y + cd,
+        )
+
+    for d, e in pairs:
+        d_copy(d, e).start()
+    do_out[z, c] = dsend[c * ZN + z]
+
+    def o_grad(head_core):
+        cols = pl.ds(pl.multiple_of((2 * y + head_core) * HD, HD), HD)
+        return mm_tn(attended[:, cols], dattn[...])
+
+    w_copy = remote(wsend, wrecv, w_s, w_r, s, sib)
+    wsend[...] = o_grad(1 - c).astype(BF16)
+    w_copy.start()
+    dwo[...] = o_grad(c)
+
+    for n in range(TILES):
+        y_copy(1, n).wait_recv()
+
+    def result_rows(at):
+        rows = pl.ds(at, 64)
+        tok_rows = pl.ds(mine + at, 64)
+        mlp = total(1, rows)
+        add_to(dm, 3, mlp * grad_out[tok_rows, :].astype(F32))
+        result[tok_rows, :] = (mid[rows, :] + row(5) * mlp).astype(BF16)
+
+    loop(TOK_FRAME, 64, result_rows)
+
+    def e_copies(core, base):
+        rows = pl.ds(base, TOK_FRAME)
+        return [
+            remote(ref, ref, e_s.at[i], e_r.at[i], s, sib)
+            for i, ref in enumerate((result.at[rows], dmid.at[rows], dmod.at[core]))
+        ]
+
+    for copy in e_copies(c, mine):
+        copy.start()
+    w_copy.wait_recv()
+    gb[:HD, :] = (dwo[...] + wrecv[...].astype(F32)).astype(BF16)
+
+    for d, e in pairs:
+        zd, cd = partner(d, e)
+        remote(
+            dsend.at[0], do_out.at[zd, cd], d_s.at[0], d_r.at[2 * zd + cd], s, t
+        ).wait_recv()
+    for copy in e_copies(1 - c, theirs):
+        copy.wait_recv()
+    for d, e in pairs:
+        o_copy(d, e).wait_send()
+        d_copy(d, e).wait_send()
+    for slot in range(8):
+        f_copy(slot).wait_send()
+    n_copy(mine).wait_send()
+    for w in range(2):
+        for n in range(TILES):
+            c_copy(w, n).wait_send()
+            y_copy(w, n).wait_send()
+    w_copy.wait_send()
+    for copy in e_copies(c, mine):
+        copy.wait_send()
+
+
+def middle_part(plan, o_mine, wo, wb, tokens, grad_out, mod_rows, cid):
+    rows = F_DEV * TOK_FRAME
+    half = lambda dtype: pltpu.VMEM((TOK_FRAME, D), dtype)
+    full = lambda dtype: pltpu.VMEM((rows, D), dtype)
+    tiles = pltpu.VMEM((2, TILES, TOK_FRAME, TILE), BF16)
+    return call(
+        functools.partial(middle_kernel, plan),
+        (
+            jax.ShapeDtypeStruct((rows, D), BF16),
+            jax.ShapeDtypeStruct((BROWS, D), BF16),
+            jax.ShapeDtypeStruct((ZN, F_DEV, PACK, LANES), BF16),
+            jax.ShapeDtypeStruct((rows, D), F32),
+            jax.ShapeDtypeStruct((F_DEV, 8, D), F32),
+        ),
+        [
+            pltpu.VMEM((HEADS, PACK, LANES), BF16),
+            half(BF16), half(F32), half(F32), half(F32), pltpu.VMEM((TOK_FRAME, 1), F32),
+            full(BF16), full(BF16), full(BF16), full(F32), full(BF16),
+            pltpu.VMEM((TILES, TOK_FRAME, TILE), F32), tiles, tiles, tiles, tiles,
+            half(BF16), pltpu.VMEM((8, PACK, LANES), BF16),
+            pltpu.VMEM((HD, D), F32), pltpu.VMEM((HD, D), BF16), pltpu.VMEM((HD, D), BF16),
+            DMA((8,)), DMA((8,)), DMA((8,)), DMA((8,)), DMA((1,)), DMA((1,)),
+            DMA((2, TILES)), DMA((2, TILES)), DMA((2, TILES)), DMA((2, TILES)),
+            DMA((8,)), DMA((8,)), DMA, DMA, DMA((3,)), DMA((3,)),
+        ],
+        [VM] * 6,
+        cid,
+        name="middle_part",
+    )(o_mine, wo, wb, tokens, grad_out, mod_rows)
+
+
 def scatter_kernel(plan, gq, gb, oq, ob, rq, rb, cq, cb, rs, rr, cs, cr):
     s, t, z, r = place(plan)
     rn = plan.r
@@ -818,20 +1107,6 @@
     )(meta, oq, ob, cond_rows, dmod, master, one, two, average)
 
 
-def normalize(rows):
-    centred = rows - jnp.mean(rows, axis=1, keepdims=True)
-    inverse = lax.rsqrt(jnp.mean(centred * centred, axis=1, keepdims=True) + NORM_EPSILON)
-    return (centred * inverse, inverse)
-
-
-def norm_back(grads, normed, inverse):
-    return inverse * (
-        grads
-        - jnp.mean(grads, axis=1, keepdims=True)
-        - normed * jnp.mean(grads * normed, axis=1, keepdims=True)
-    )
-
-
 def by_frame(rows):
     return rows.reshape(F_DEV, TOK_FRAME, rows.shape[1])
 
@@ -887,14 +1162,12 @@
     condition = jax.nn.silu(mm(one_hot, level_table)).astype(BF16)
     cond_units = condition.reshape(plan.frames, plan.nm, plan.um).transpose(1, 0, 2)
 
-    wq, wb, mod_blocks = gather_weights(plan, flat(master), cond_units, 0)
-    w_out, w_up, w_down = wb[:HD], wb[HD : HD + FT], wb[HD + FT :]
+    wq, wb, mod_blocks, wo = gather_weights(plan, flat(master), cond_units, 0)
     modulation = (
         mod_blocks.reshape(TP, F_DEV, MT).transpose(1, 0, 2).reshape(F_DEV, TP * MT)
     )
-    shift_one, scale_one, gate_one, shift_two, scale_two, gate_two = [
-        modulation[:, part * D : (part + 1) * D] for part in range(6)
-    ]
+    mod_rows = modulation.reshape(F_DEV * 6, D)
+    shift_one, scale_one = modulation[:, :D], modulation[:, D : 2 * D]
 
     inputs = tokens.astype(F32)
     normed_one, inverse_one = normalize(inputs)
@@ -915,34 +1188,9 @@
     q_mine, kv_all = exchange_qkv(plan, pack_heads(projected[:, :HD]), kv, 1)
     meta = jnp.concatenate([frame_clip, lax.rem(s, plan.r)[None]]).astype(jnp.int32)
     o_mine, o_rows, lse = attend(plan, meta, q_mine, kv_all)
-    attended = unpack_heads(exchange_heads(plan, o_mine, 2, "exchange_o"))
-    attn = total_tp(mm(attended, w_out), 3, "total_attn")
-
-    middle = inputs + frame_scale(attn, gate_one)
-    normed_two, inverse_two = normalize(middle)
-    second_in = frame_affine(normed_two, scale_two, shift_two).astype(BF16)
-    up_rows = mm(second_in, w_up)
-    activated, gelu_back = jax.vjp(functools.partial(jax.nn.gelu, approximate=True), up_rows)
-    hidden = activated.astype(BF16)
-    mlp = total_tp(mm(hidden, w_down), 4, "total_mlp")
-    result = (middle + frame_scale(mlp, gate_two)).astype(BF16)
-    upstream = grad_out.astype(F32)
-    gate_two_grad = frame_total(mlp * upstream)
-    mlp_grad = frame_scale(upstream, gate_two).astype(BF16)
-    down_grad = mm_tn(hidden, mlp_grad)
-    up_grad = gelu_back(mm_nt(mlp_grad, w_down))[0].astype(BF16)
-    up_weight_grad = mm_tn(second_in, up_grad)
-    second_grad = total_tp(mm_nt(up_grad, w_up), 5, "total_second")
-    scale_two_grad = frame_total(second_grad * normed_two)
-    shift_two_grad = frame_total(second_grad)
-    middle_grad = upstream + norm_back(
-        frame_scale(second_grad, 1.0 + scale_two), normed_two, inverse_two
-    )
-    gate_one_grad = frame_total(attn * middle_grad)
-    attn_grad = frame_scale(middle_grad, gate_one).astype(BF16)
-    out_weight_grad = mm_tn(attended, attn_grad)
-    attended_grad = mm_nt(attn_grad, w_out).astype(BF16)
-    do_mine = exchange_heads(plan, pack_heads(attended_grad), 6, "exchange_do")
+    result, grads_b, do_mine, middle_grad, mod_four = middle_part(
+        plan, o_mine, wo.reshape(HEADS * HEAD, D), wb, tokens, grad_out, mod_rows, 2
+    )
     dq_mine, dkv_all = attend_back(plan, meta, q_mine, kv_all, do_mine, o_rows, lse)
     dq_heads, dkv_heads = exchange_dkv(plan, dq_mine, dkv_all, 7)
     qkv_grad = jnp.concatenate(
@@ -962,17 +1210,13 @@
         [
             shift_one_grad,
             scale_one_grad,
-            gate_one_grad,
-            shift_two_grad,
-            scale_two_grad,
-            gate_two_grad,
+            mod_four[:, :4].reshape(F_DEV, 4 * D),
         ],
         axis=1,
     )
     mod_grad = lax.all_gather(
         lax.dynamic_slice_in_dim(mod_terms, t * MT, MT, axis=1), "seq", axis=0, tiled=True
     ).astype(BF16)
-    grads_b = jnp.concatenate([out_weight_grad, up_weight_grad, down_grad], axis=0).astype(BF16)
     own_q, own_b = scatter_grads(plan, qkv_weight_grad.astype(BF16), grads_b, 9)
     updated = adam(
         plan,

time: 591 us -> 527 us (0.89)
  other arithmetic: 54.4 us -> 20.2 us
  matrix products: 36.4 us -> 8.84 us
    pallas_call x4 -> x1, Pallas kernels: 104 us -> 25.4 us  [total_tp(): call(functools.partial(total_kernel, chunks), jax.ShapeDtypeStruct(part.s...]
    pallas_call x3 -> x2, Pallas kernels: 54.1 us -> 105 us  [the longest x1 85.7 us: middle_part(): call(functools.partial(middle_kernel, plan), (jax.ShapeDtypeStruct((rows,...]
    pallas_call x1, Pallas kernels: 40.3 us -> 55.7 us  [exchange_qkv(): call(functools.partial(qkv_kernel, plan), (jax.ShapeDtypeStruct((ZN, TOK_...]
    dot_general x4 -> x1, matrix products: 14.7 us -> 3.11 us  [mm_nt(): lax.dot_general(left, right, (((1,), (1,)), ((), ())), preferred_element_...]
    reduce_sum x6 -> x2, other arithmetic: 15 us -> 4.25 us  [frame_total(): return jnp.sum(by_frame(rows), axis=1)]
    dot_general x5 -> x2, matrix products: 10.7 us -> 1.86 us  [mm(): return jnp.dot(left, right, preferred_element_type=F32)]
    mul x1 -> x0, other arithmetic: 7.66 us -> none  [local(): gate_two_grad = frame_total(mlp * upstream)]
    pallas_call x1, Pallas kernels: 87.1 us -> 94.3 us  [gather_weights(): call(functools.partial(gather_kernel, plan), (jax.ShapeDtypeStruct((D, QK...]
where the time goes in v2:
time: 527 us; the launch traced here: 520 us
  Pallas kernels  437 us (83%)
  blocking collectives  36.1 us (7%)
  other arithmetic  20.2 us (4%)
  local copies, waits for them, and re-layouts  16.3 us (3%)
  matrix products  8.84 us (2%)
    pallas_call x1, Pallas kernels, gather_weights(): call(functools.partial(gather_kernel, plan), (jax.ShapeDtypeStruct((D, QK...  94.3 us
    pallas_call x1, Pallas kernels, scatter_grads(): call(functools.partial(scatter_kernel, plan), (jax.ShapeDtypeStruct((3, p...  88.4 us
    pallas_call x1, Pallas kernels, middle_part(): call(functools.partial(middle_kernel, plan), (jax.ShapeDtypeStruct((rows,...  85.7 us
    pallas_call x1, Pallas kernels, exchange_qkv(): call(functools.partial(qkv_kernel, plan), (jax.ShapeDtypeStruct((ZN, TOK_...  55.7 us
    pallas_call x1, Pallas kernels, exchange_dkv(): call(functools.partial(dkv_kernel, plan), (jax.ShapeDtypeStruct((ZN, TOK_...  36.7 us
    all_gather x1, blocking collectives, local(): lax.all_gather(lax.dynamic_slice_in_dim(mod_terms, t * MT, MT, axis=1), '...  36.1 us
    pallas_call x1, Pallas kernels, total_tp(): call(functools.partial(total_kernel, chunks), jax.ShapeDtypeStruct(part.s...  25.4 us
    pallas_call x1, Pallas kernels, attend_back(): call(functools.partial(attend_back_kernel, plan), (jax.ShapeDtypeStruct((...  20.3 us

profile of v2, /device:TPU:0, one launch (start us, length us, event | category | flops | bytes accessed | tf_op | source)
XLA Modules:
  0.0 520.2 jit_solution(4596857153113340775)
XLA Ops:
  0.7 1.4 pad_add_fusion.meta
  2.1 0.7 subtract_multiply_fusion
  2.7 1.7 convert_reduce_fusion
  5.7 0.7 copy.39.cond
  6.4 94.3 %gather_weights.1 = (bf16[1024,768]{1,0:T(8,128)(2,1)}, bf16[2304,1024]{1,0:T(8,128)(2,1)}, f32[4,24,128]{2,1,0:T(8,128)}, bf16[4,256,1024]{2,1,0:T(8,128)(2,1)}) custom-call(f32[4608,128]{1,0:T(8,128)} %bitcast.81, bf16[8,16,128]{2,1,0:T(8,128)(2,1)} %copy.39.cond), custom_call_target="tpu_custom_call" | custom-call | tf_op jit(solution)/shard_map/gather_weights/pallas_call | solution.py:295
  100.8 0.8 reshape.102
  101.7 0.7 reshape_reshape.3.mod
  102.3 1.2 fusion.11
  103.7 1.4 convolution_convert_fusion.1
  105.5 0.9 copy.44.q
  107.3 1.0 pad_maximum_fusion.kv
  108.3 55.7 %exchange_qkv.1 = (bf16[4,384,128]{2,1,0:T(8,128)(2,1)}, bf16[8,768,128]{2,1,0:T(8,128)(2,1)}) custom-call(bf16[4,384,128]{2,1,0:T(8,128)(2,1)} %copy.44.q, bf16[4,768,128]{2,1,0:T(8,128)(2,1)} %pad_maximum_fusion.kv), custom_call_target="tpu_custom_call" | custom-call | tf_op jit(solution)/shard_map/exchange_qkv/pallas_call | solution.py:374
  163.9 19.0 %attend.1 = (bf16[4,2,192,128]{3,2,1,0:T(8,128)(2,1)}, f32[8,64,384]{2,1,0:T(8,128)}, f32[8,1,384]{2,1,0:T(1,128)}) custom-call(s32[17]{0:T(128)} %pad_add_fusion.meta, bf16[4,384,128]{2,1,0:T(8,128)(2,1)} %get-tuple-element.32.q, bf16[8,768,128]{2,1,0:T(8,128)(2,1)} %get-tuple-element.33.kv), custom_call_target="tpu_custom_call" | custom-call | tf_op jit(solution)/shard_map/attend/pallas_call | solution.py:511
  182.9 85.7 %middle_part.1 = (bf16[768,1024]{1,0:T(8,128)(2,1)}, bf16[2304,1024]{1,0:T(8,128)(2,1)}, bf16[4,2,192,128]{3,2,1,0:T(8,128)(2,1)}, f32[768,1024]{1,0:T(8,128)}, f32[2,8,1024]{2,1,0:T(8,128)}) custom-call(bf16[4,2,192,128]{3,2,1,0:T(8,128)(2,1)} %get-tuple-element.34.o_mine, bf16[1024,1024]{1,0:T(8,128)(2,1)} %bitcast.88, ...), custom_call_target="tpu_custom_call" | custom-call | tf_op jit(solution)/shard_map/middle_part/pallas_call | solution.py:910
  268.6 20.3 %attend_back.1 = (bf16[4,384,128]{2,1,0:T(8,128)(2,1)}, bf16[8,768,128]{2,1,0:T(8,128)(2,1)}) custom-call(s32[17]{0:T(128)} %pad_add_fusion.meta, bf16[4,384,128]{2,1,0:T(8,128)(2,1)} %get-tuple-element.32.q, bf16[8,768,128]{2,1,0:T(8,128)(2,1)} %get-tuple-element.33.kv, bf16[4,2,192,128]{3,2,1,0:T(8,128)(2,1)} %get-tuple-element.39.do, ...), custom_call_target="tpu_custom_call" | custom-call | tf_op jit(solution)/shard_map/attend_back/pallas_call | solution.py:569
  288.9 36.7 %exchange_dkv.1 = (bf16[4,384,128]{2,1,0:T(8,128)(2,1)}, bf16[4,768,128]{2,1,0:T(8,128)(2,1)}) custom-call(bf16[4,384,128]{2,1,0:T(8,128)(2,1)} %get-tuple-element.42.dq, bf16[8,768,128]{2,1,0:T(8,128)(2,1)} %get-tuple-element.43.dkv), custom_call_target="tpu_custom_call" | custom-call | tf_op jit(solution)/shard_map/exchange_dkv/pallas_call | solution.py:444
  325.6 1.3 copy.45
  327.4 0.8 slice_bitcast_fusion.4
  328.2 0.8 constant_dynamic-update-slice_fusion.8
  330.6 0.7 constant_dynamic-update-slice_fusion.7
  335.2 0.6 constant_dynamic-update-slice_fusion
  335.8 3.9 convolution_convert_fusion.gq
  339.7 88.4 %scatter_grads.1 = (f32[3,256,768]{2,1,0:T(8,128)}, f32[3,192,1024]{2,1,0:T(8,128)}) custom-call(bf16[1024,768]{1,0:T(8,128)(2,1)} %convolution_convert_fusion.gq, bf16[2304,1024]{1,0:T(8,128)(2,1)} %get-tuple-element.46.gb), custom_call_target="tpu_custom_call" | custom-call | tf_op jit(solution)/shard_map/scatter_grads/pallas_call | solution.py:1036
  428.1 3.1 fusion.23.part
  431.2 25.4 %total_first.1 = f32[768,1024]{1,0:T(8,128)} custom-call(f32[768,1024]{1,0:T(8,128)} %fusion.23.part), custom_call_target="tpu_custom_call" | custom-call | tf_op jit(solution)/shard_map/total_first/pallas_call | solution.py:633
  456.6 2.2 reduce_sum.58
  459.0 3.1 fusion.12
  462.2 5.8 %fusion.2 = (f32[768,1024]{1,0:T(8,128)}, f32[768,1024]{1,0:T(8,128)}) fusion(f32[768,1024]{1,0:T(8,128)S(1)} %copy-done.5, bf16[768,1024]{1,0:T(8,128)(2,1)S(1)} %copy-done.4, f32[768]{0:T(1024)S(1)} %add_rsqrt_fusion, f32[768]{0:T(1024)S(1)} %broadcast_multiply_fusion.2, f32[768,1024]{1,0:T(8,128)} %get-tuple-element.38, ...), kind=kLoop, calls=%fused_computation.6 | loop fusion | flops 7864320 | bytes 14176256 | tf_op jit(solution)/shard_map/mul | solution.py:1204
  467.9 2.1 reduce_sum.59
  470.1 36.1 %all-gather = bf16[8,2,1536]{2,1,0:T(2,128)(2,1)S(1)} all-gather(bf16[1,2,1536]{2,1,0:T(2,128)(2,1)S(1)} %fusion.17), channel_id=1, replica_groups=mesh['seq'=8,'tp'=4] {'seq'}, dimensions={0}, use_global_device_ids=true | all-gather | bytes 55296 | tf_op jit(solution)/shard_map/all_gather | solution.py:1217
  506.8 12.1 %adam.1 = (f32[4608,128]{1,0:T(8,128)}, f32[4608,128]{1,0:T(8,128)}, f32[4608,128]{1,0:T(8,128)}, f32[4608,128]{1,0:T(8,128)}) custom-call(s32[1]{0:T(128)} %bitcast.20.meta, f32[3,256,768]{2,1,0:T(8,128)} %get-tuple-element.47.oq, f32[3,192,1024]{2,1,0:T(8,128)} %get-tuple-element.48.ob, bf16[8,128,16]{2,1,0:T(8,128)(2,1)} %bitcast.84, ...), custom_call_target="tpu_custom_call" | custom-call | tf_op jit(solution)/shard_map/adam/pallas_call | solution.py:1101
  518.9 1.1 copy.71
  (69 shorter events, 9.4 us)
Async XLA Ops:
  0.6 4.4 copy-start
  0.7 3.8 copy-start.2
  5.5 96.8 %copy-start.3 = (bf16[768,1024]{1,0:T(8,128)(2,1)S(1)}, bf16[768,1024]{1,0:T(8,128)(2,1)}, u32[]{:S(2)}) copy-start(bf16[768,1024]{1,0:T(8,128)(2,1)} %tokens.1) | copy-start | bytes 4718596
  5.7 97.9 %copy-start.6 = (bf16[16,1024]{0,1:T(8,128)(2,1)}, bf16[16,1024]{0,1:T(8,128)(2,1)S(1)}, u32[]{:S(2)}) copy-start(bf16[16,1024]{0,1:T(8,128)(2,1)S(1)} %copy.38) | copy-start | bytes 98308
  102.3 1.4 copy-start.12
  103.7 1.4 copy-start.7
  325.6 3.4 copy-start.10
  329.9 6.0 %copy-start.8 = (bf16[768,1024]{1,0:T(8,128)(2,1)S(1)}, bf16[768,1024]{1,0:T(8,128)(2,1)}, u32[]{:S(2)}) copy-start(bf16[768,1024]{1,0:T(8,128)(2,1)} %copy-done.7) | copy-start | bytes 4718596
  339.7 88.4 %copy-start.11 = (bf16[768,768]{0,1:T(8,128)(2,1)S(1)}, bf16[768,768]{0,1:T(8,128)(2,1)}, u32[]{:S(2)}) copy-start(bf16[768,768]{0,1:T(8,128)(2,1)} %constant_dynamic-update-slice_fusion) | copy-start | bytes 3538948
  339.7 88.4 %copy-start.13 = (bf16[1024,768]{1,0:T(8,128)(2,1)S(1)}, bf16[1024,768]{1,0:T(8,128)(2,1)}, u32[]{:S(2)}) copy-start(bf16[1024,768]{1,0:T(8,128)(2,1)} %get-tuple-element.31) | copy-start | bytes 4718596
  456.6 2.4 copy-start.4
  459.0 3.2 copy-start.5
  506.8 12.1 %copy-start.9 = (bf16[768,1024]{1,0:T(8,128)(2,1)S(1)}, bf16[768,1024]{1,0:T(8,128)(2,1)}, u32[]{:S(2)}) copy-start(bf16[768,1024]{1,0:T(8,128)(2,1)} %get-tuple-element.92) | copy-start | bytes 4718596
  506.8 13.2 %copy-start.1 = (bf16[1000,1024]{1,0:T(8,128)(2,1)S(1)}, bf16[1000,1024]{1,0:T(8,128)(2,1)}, u32[]{:S(2)}) copy-start(bf16[1000,1024]{1,0:T(8,128)(2,1)} %param.15) | copy-start | bytes 6144004

commit v3 on v2

--- a/solution.py
+++ b/solution.py
@@ -112,14 +112,24 @@
     pl.semaphore_wait(barrier, len(peers))
 
 
-def by_kind(plan, k, act):
-    @pl.when(k < plan.nq)
-    def _():
-        act("q")
-
-    @pl.when((k >= plan.nq) & (k < plan.nb))
-    def _():
-        act("b")
+def by_kind(plan, k, act, low=0, high=None):
+    high = plan.nb if high is None else high
+    q_high, b_low = min(plan.nq, high), max(plan.nq, low)
+    if low < q_high:
+        @pl.when((k >= low) & (k < q_high))
+        def _():
+            act("q")
+
+    if b_low < high:
+        @pl.when((k >= b_low) & (k < high))
+        def _():
+            act("b")
+
+
+def unit_of(plan, k, kind, wq, wb):
+    if kind == "q":
+        return wq.at[pl.ds(pl.multiple_of(k * plan.uq, plan.uq), plan.uq)]
+    return wb.at[pl.ds(pl.multiple_of((k - plan.nq) * plan.ub, plan.ub), plan.ub)]
 
 
 def call(kernel, outs, scratch, ins, cid=None, cost=None, name=None):
@@ -384,81 +394,6 @@
     )(q, kv)
 
 
-def dkv_kernel(plan, dq, dkv, q_out, kv_out, stage, side, qs, ks, rs, qr, kr, rr):
-    s, t, z, r = place(plan)
-    rn = plan.r
-    greet(
-        [(lax.rem(z + d, ZN) * rn + r, t) for d in range(1, ZN)]
-        + [(z * rn + lax.rem(r + d, rn), t) for d in range(1, rn)]
-    )
-
-    def side_copy(d, e):
-        zs = lax.rem(z + d, ZN)
-        other = lax.rem(r + e, rn)
-        return remote(
-            dkv.at[zs * rn + other], side.at[e - 1, d], rs.at[d, e - 1], rr.at[d, e - 1],
-            z * rn + other, t,
-        )
-
-    def q_copy(d):
-        to = lax.rem(z + d, ZN)
-        return remote(dq.at[to], q_out.at[z], qs.at[d - 1], qr.at[z], to * rn + r, t)
-
-    def kv_copy(d):
-        to = lax.rem(z + d, ZN)
-        return remote(stage.at[d], kv_out.at[z], ks.at[d - 1], kr.at[z], to * rn + r, t)
-
-    order = list(range(1, ZN)) + [0]
-    for d in order:
-        for e in range(1, rn):
-            side_copy(d, e).start()
-    for d in range(1, ZN):
-        q_copy(d).start()
-    q_out[z] = dq[z]
-    for d in order:
-        zs = lax.rem(z + d, ZN)
-        total = dkv[zs * rn + r].astype(F32)
-        for e in range(1, rn):
-            side_copy(d, e).wait_recv()
-            total = total + side[e - 1, d].astype(F32)
-        if d == 0:
-            kv_out[z] = total.astype(BF16)
-        else:
-            stage[d] = total.astype(BF16)
-            kv_copy(d).start()
-    for d in range(1, ZN):
-        zs = lax.rem(z + d, ZN)
-        remote(dq.at[0], q_out.at[zs], qs.at[0], qr.at[zs], s, t).wait_recv()
-        remote(stage.at[d], kv_out.at[zs], ks.at[0], kr.at[zs], s, t).wait_recv()
-    for d in range(1, ZN):
-        q_copy(d).wait_send()
-        kv_copy(d).wait_send()
-    for d in order:
-        for e in range(1, rn):
-            side_copy(d, e).wait_send()
-
-
-def exchange_dkv(plan, dq, dkv, cid):
-    rn = plan.r
-    rows = F_DEV * TOK_FRAME
-    return call(
-        functools.partial(dkv_kernel, plan),
-        (
-            jax.ShapeDtypeStruct((ZN, TOK_FRAME, LANES), BF16),
-            jax.ShapeDtypeStruct((ZN, rows, LANES), BF16),
-        ),
-        [
-            pltpu.VMEM((ZN, rows, LANES), BF16),
-            pltpu.VMEM((rn - 1, ZN, rows, LANES), BF16),
-            DMA((ZN - 1,)), DMA((ZN - 1,)), DMA((ZN, rn - 1)),
-            DMA((ZN,)), DMA((ZN,)), DMA((ZN, rn - 1)),
-        ],
-        [VM, VM],
-        cid,
-        name="exchange_dkv",
-    )(dq, dkv)
-
-
 def padded(rows, low):
     zero = jnp.zeros_like(rows)
     return jnp.concatenate([rows, zero] if low else [zero, rows], axis=1)
@@ -581,65 +516,6 @@
     )(meta, q, kv, do, ot, lse)
 
 
-def total_kernel(chunks, part, out, sbuf, cbuf, ybuf, yrecv, ss, cs, ys, yr, osem, orsem):
-    s = lax.axis_index("seq")
-    t = lax.axis_index("tp")
-    core = lax.rem(t, 2)
-    sibling = t + 1 - 2 * core
-    across = lax.rem(t + 2, TP)
-    greet([(s, sibling), (s, across)])
-    half = TOK_FRAME
-    rows = half // chunks
-    mine = core * half
-    theirs = half - mine
-
-    def c_copy(ch):
-        return remote(sbuf.at[ch], cbuf.at[ch], ss.at[ch], cs.at[ch], s, sibling)
-
-    def y_copy(ch):
-        return remote(ybuf.at[ch], yrecv.at[ch], ys.at[ch], yr.at[ch], s, across)
-
-    def o_copy(ch, base):
-        ref = out.at[pl.ds(pl.multiple_of(base + ch * rows, rows), rows)]
-        return remote(ref, ref, osem.at[ch], orsem.at[ch], s, sibling)
-
-    for ch in range(chunks):
-        sbuf[ch] = part[pl.ds(pl.multiple_of(theirs + ch * rows, rows), rows), :].astype(BF16)
-        c_copy(ch).start()
-    for ch in range(chunks):
-        c_copy(ch).wait_recv()
-        ybuf[ch] = (
-            part[pl.ds(pl.multiple_of(mine + ch * rows, rows), rows), :] + cbuf[ch].astype(F32)
-        ).astype(BF16)
-        y_copy(ch).start()
-    for ch in range(chunks):
-        y_copy(ch).wait_recv()
-        out[pl.ds(pl.multiple_of(mine + ch * rows, rows), rows), :] = ybuf[ch].astype(F32) + yrecv[
-            ch
-        ].astype(F32)
-        o_copy(ch, mine).start()
-    for ch in range(chunks):
-        o_copy(ch, theirs).wait_recv()
-    for ch in range(chunks):
-        c_copy(ch).wait_send()
-        y_copy(ch).wait_send()
-        o_copy(ch, mine).wait_send()
-
-
-def total_tp(part, cid, name):
-    chunks = 4
-    rows = TOK_FRAME // chunks
-    buf = pltpu.VMEM((chunks, rows, D), BF16)
-    return call(
-        functools.partial(total_kernel, chunks),
-        jax.ShapeDtypeStruct(part.shape, F32),
-        [buf] * 4 + [DMA((chunks,))] * 6,
-        [VM],
-        cid,
-        name=name,
-    )(part)
-
-
 def loop(count, step, body):
     def turn(i, carry):
         body(pl.multiple_of(i * step, step))
@@ -804,7 +680,7 @@
     loop(FT, TILE, down_grad)
     loop(D, TILE, up_grad)
 
-    dm = dmod.at[c]
+    dm = dmod
     dm[...] = jnp.zeros_like(dm)
     for n in range(TILES):
         y_copy(0, n).wait_recv()
@@ -825,7 +701,7 @@
         values = grad_out[tok_rows, :].astype(F32) + norm_back(
             grads * (1.0 + row(4)), normed, inv[rows, :]
         )
-        dmid[tok_rows, :] = values
+        dmid[rows, :] = values
         add_to(dm, 0, attn[rows, :] * values)
         dattn[rows, :] = (row(2) * values).astype(BF16)
 
@@ -868,15 +744,11 @@
 
     loop(TOK_FRAME, 64, result_rows)
 
-    def e_copies(core, base):
-        rows = pl.ds(base, TOK_FRAME)
-        return [
-            remote(ref, ref, e_s.at[i], e_r.at[i], s, sib)
-            for i, ref in enumerate((result.at[rows], dmid.at[rows], dmod.at[core]))
-        ]
-
-    for copy in e_copies(c, mine):
-        copy.start()
+    def e_copy(base):
+        ref = result.at[pl.ds(base, TOK_FRAME)]
+        return remote(ref, ref, e_s, e_r, s, sib)
+
+    e_copy(mine).start()
     w_copy.wait_recv()
     gb[:HD, :] = (dwo[...] + wrecv[...].astype(F32)).astype(BF16)
 
@@ -885,8 +757,7 @@
         remote(
             dsend.at[0], do_out.at[zd, cd], d_s.at[0], d_r.at[2 * zd + cd], s, t
         ).wait_recv()
-    for copy in e_copies(1 - c, theirs):
-        copy.wait_recv()
+    e_copy(theirs).wait_recv()
     for d, e in pairs:
         o_copy(d, e).wait_send()
         d_copy(d, e).wait_send()
@@ -898,8 +769,7 @@
             c_copy(w, n).wait_send()
             y_copy(w, n).wait_send()
     w_copy.wait_send()
-    for copy in e_copies(c, mine):
-        copy.wait_send()
+    e_copy(mine).wait_send()
 
 
 def middle_part(plan, o_mine, wo, wb, tokens, grad_out, mod_rows, cid):
@@ -913,8 +783,8 @@
             jax.ShapeDtypeStruct((rows, D), BF16),
             jax.ShapeDtypeStruct((BROWS, D), BF16),
             jax.ShapeDtypeStruct((ZN, F_DEV, PACK, LANES), BF16),
-            jax.ShapeDtypeStruct((rows, D), F32),
-            jax.ShapeDtypeStruct((F_DEV, 8, D), F32),
+            jax.ShapeDtypeStruct((TOK_FRAME, D), F32),
+            jax.ShapeDtypeStruct((8, D), F32),
         ),
         [
             pltpu.VMEM((HEADS, PACK, LANES), BF16),
@@ -925,7 +795,7 @@
             pltpu.VMEM((HD, D), F32), pltpu.VMEM((HD, D), BF16), pltpu.VMEM((HD, D), BF16),
             DMA((8,)), DMA((8,)), DMA((8,)), DMA((8,)), DMA((1,)), DMA((1,)),
             DMA((2, TILES)), DMA((2, TILES)), DMA((2, TILES)), DMA((2, TILES)),
-            DMA((8,)), DMA((8,)), DMA, DMA, DMA((3,)), DMA((3,)),
+            DMA((8,)), DMA((8,)), DMA, DMA, DMA, DMA,
         ],
         [VM] * 6,
         cid,
@@ -933,123 +803,344 @@
     )(o_mine, wo, wb, tokens, grad_out, mod_rows)
 
 
-def scatter_kernel(plan, gq, gb, oq, ob, rq, rb, cq, cb, rs, rr, cs, cr):
+def tail_kernel(
+    plan, dq, dkv, first_in, wq, tokens, dmid, mod, dm4, gb,
+    igrad, oq, ob, dall,
+    stage, side, q_in, kv_in, dqkv, gq, own, csend, crecv, ysend, yrecv, dm, dm3, dboth,
+    rq, rb, cq, cb,
+    q_s, q_r, k_s, k_r, x_s, x_r, c_s, c_r, y_s, y_r, e_s, e_r, h_s, h_r, m_s, m_r, r_s, r_r, t_s, t_r,
+):
     s, t, z, r = place(plan)
-    rn = plan.r
-    greet(
-        [(z * rn + lax.rem(r + d, rn), t) for d in range(1, rn)]
-        + [(lax.rem(z + d, ZN) * rn + r, t) for d in (1, ZN - 1)]
-    )
-
-    def own(k, kind):
-        if kind == "q":
-            return gq.at[pl.ds(pl.multiple_of(k * plan.uq, plan.uq), plan.uq)]
-        return gb.at[pl.ds(pl.multiple_of((k - plan.nq) * plan.ub, plan.ub), plan.ub)]
-
-    a = 2 - lax.div(z, 2)
-    b = 2 * lax.div(ZN - 1 - z, ZN - 1)
+    n, rn = plan.n, plan.r
+    y = lax.div(t, 2)
+    c = lax.rem(t, 2)
+    sib = 2 * y + 1 - c
+    across = lax.rem(t + 2, TP)
+    mine = pl.multiple_of(c * TOK_FRAME, TOK_FRAME)
+    theirs = pl.multiple_of((1 - c) * TOK_FRAME, TOK_FRAME)
+    greet([(lax.rem(s + d, n), t) for d in range(1, n)] + [(s, sib), (s, across)])
+
+    def side_copy(d, e):
+        zs = lax.rem(z + d, ZN)
+        other = lax.rem(r + e, rn)
+        return remote(
+            dkv.at[zs * rn + other], side.at[e - 1, d], x_s.at[d, e - 1], x_r.at[d, e - 1],
+            z * rn + other, t,
+        )
+
+    def q_copy(d):
+        to = lax.rem(z + d, ZN)
+        return remote(dq.at[to], q_in.at[z], q_s.at[d - 1], q_r.at[z], to * rn + r, t)
+
+    def kv_copy(d):
+        to = lax.rem(z + d, ZN)
+        return remote(stage.at[d], kv_in.at[z], k_s.at[d - 1], k_r.at[z], to * rn + r, t)
+
+    order = list(range(1, ZN)) + [0]
+    for d in order:
+        for e in range(1, rn):
+            side_copy(d, e).start()
+    for d in range(1, ZN):
+        q_copy(d).start()
+    q_in[z] = dq[z]
+    for d in order:
+        zs = lax.rem(z + d, ZN)
+        total = dkv[zs * rn + r].astype(F32)
+        for e in range(1, rn):
+            side_copy(d, e).wait_recv()
+            total = total + side[e - 1, d].astype(F32)
+        if d == 0:
+            kv_in[z] = total.astype(BF16)
+        else:
+            stage[d] = total.astype(BF16)
+            kv_copy(d).start()
 
     def owner(j):
+        a = 2 - lax.div(z, 2)
+        b = 2 * lax.div(ZN - 1 - z, ZN - 1)
         return lax.rem(a * j + b, 3)
 
-    def side_copy(zo, i, d, kind):
+    def grad_copy(zo, i, d, kind):
         other = lax.rem(r + d, rn)
         k = 3 * (zo * rn + other) + i
         lu = 3 * zo + i
         buf = rq if kind == "q" else rb
-        return k, remote(
-            own(k, kind), buf.at[d - 1, lu], rs.at[lu, d - 1], rr.at[lu, d - 1], z * rn + other, t
+        return remote(
+            unit_of(plan, k, kind, gq, gb), buf.at[d - 1, lu], r_s.at[lu, d - 1],
+            r_r.at[lu, d - 1], z * rn + other, t,
         )
 
-    def chain_copy(lu, kind, side, to):
+    def grad_sides(owners, low, high, act):
+        for zo in owners:
+            for i in range(3):
+                for d in range(1, rn):
+                    k = 3 * (zo * rn + lax.rem(r + d, rn)) + i
+                    by_kind(plan, k, lambda kind: act(grad_copy(zo, i, d, kind)), low, high)
+
+    def chain_copy(lu, kind, below, to):
         src = (rq if kind == "q" else rb).at[0, lu]
-        dst = (cq if kind == "q" else cb).at[side, lu]
-        return remote(src, dst, cs.at[lu], cr.at[lu, side], to, t)
-
-    for j in range(3):
-        for i in range(3):
-            for d in range(1, rn):
-                k = 3 * (owner(j) * rn + lax.rem(r + d, rn)) + i
-                by_kind(plan, k, lambda kind: side_copy(owner(j), i, d, kind)[1].start())
-
-    for j in range(3):
-        zo = owner(j)
-        for i in range(3):
-            k = 3 * (zo * rn + r) + i
-            lu = 3 * zo + i
-
-            def step(kind):
-                side = rq if kind == "q" else rb
-                chain = cq if kind == "q" else cb
-                out = oq if kind == "q" else ob
-                for d in range(1, rn):
-                    remote(
-                        own(k, kind), side.at[d - 1, lu], rs.at[lu, d - 1], rr.at[lu, d - 1], s, t
-                    ).wait_recv()
-                total = own(k, kind)[...].astype(F32)
-                for d in range(1, rn):
-                    total = total + side[d - 1, lu].astype(F32)
-                out[i] = total
-
-                @pl.when((zo <= z) & (z < ZN - 1))
-                def _():
-                    chain_copy(lu, kind, 0, s).wait_recv()
-                    out[i] += chain[0, lu].astype(F32)
-
-                @pl.when((zo >= z) & (z > 0))
-                def _():
-                    chain_copy(lu, kind, 1, s).wait_recv()
-                    out[i] += chain[1, lu].astype(F32)
-
-                @pl.when(zo != z)
-                def _():
-                    side[0, lu] = out[i].astype(BF16)
-
-                @pl.when(zo < z)
-                def _():
-                    chain_copy(lu, kind, 0, s - rn).start()
-
-                @pl.when(zo > z)
-                def _():
-                    chain_copy(lu, kind, 1, s + rn).start()
-
-            by_kind(plan, k, step)
-
-    for j in range(3):
-        zo = owner(j)
-        for i in range(3):
-            for d in range(1, rn):
-                k = 3 * (zo * rn + lax.rem(r + d, rn)) + i
-                by_kind(plan, k, lambda kind: side_copy(zo, i, d, kind)[1].wait_send())
-            k = 3 * (zo * rn + r) + i
-
-            def close(kind):
-                @pl.when(zo != z)
-                def _():
-                    chain_copy(3 * zo + i, kind, 0, s).wait_send()
-
-            by_kind(plan, k, close)
-
-
-def scatter_grads(plan, gq, gb, cid):
-    rn = plan.r
+        dst = cq.at[lu] if kind == "q" else cb.at[below, lu]
+        return remote(src, dst, t_s.at[lu], t_r.at[lu, below], to, t)
+
+    def grad_chain(owners, low, high):
+        for zo in owners:
+            for i in range(3):
+                k = 3 * (zo * rn + r) + i
+                lu = 3 * zo + i
+
+                def step(kind):
+                    part = rq if kind == "q" else rb
+                    out = oq if kind == "q" else ob
+                    unit = unit_of(plan, k, kind, gq, gb)
+                    rows = plan.uq if kind == "q" else plan.ub
+                    for d in range(1, rn):
+                        remote(
+                            unit, part.at[d - 1, lu], r_s.at[lu, d - 1], r_r.at[lu, d - 1], s, t
+                        ).wait_recv()
+                    above = (zo <= z) & (z < ZN - 1)
+                    below = (zo >= z) & (z > 0)
+
+                    @pl.when(above)
+                    def _():
+                        chain_copy(lu, kind, 0, s).wait_recv()
+
+                    if kind == "b":
+                        @pl.when(below)
+                        def _():
+                            chain_copy(lu, kind, 1, s).wait_recv()
+
+                    def here(at):
+                        total = unit[pl.ds(at, 16), :].astype(F32)
+                        for d in range(1, rn):
+                            total = total + part[d - 1, lu, pl.ds(at, 16), :].astype(F32)
+                        return total
+
+                    def from_chain(at, below):
+                        ref = cq.at[lu] if kind == "q" else cb.at[below, lu]
+                        return ref[pl.ds(at, 16), :].astype(F32)
+
+                    @pl.when(zo != z)
+                    def _():
+                        @pl.when((zo < z) & (z == ZN - 1) | (zo > z) & (z == 0))
+                        def _():
+                            def body(at):
+                                part[0, lu, pl.ds(at, 16), :] = here(at).astype(BF16)
+
+                            loop(rows, 16, body)
+
+                        @pl.when((zo < z) & (z < ZN - 1))
+                        def _():
+                            def body(at):
+                                part[0, lu, pl.ds(at, 16), :] = (here(at) + from_chain(at, 0)).astype(BF16)
+
+                            loop(rows, 16, body)
+
+                        if kind == "b":
+                            @pl.when((zo > z) & (z > 0))
+                            def _():
+                                def body(at):
+                                    part[0, lu, pl.ds(at, 16), :] = (here(at) + from_chain(at, 1)).astype(BF16)
+
+                                loop(rows, 16, body)
+
+                    @pl.when(zo < z)
+                    def _():
+                        chain_copy(lu, kind, 0, s - rn).start()
+
+                    if kind == "b":
+                        @pl.when(zo > z)
+                        def _():
+                            chain_copy(lu, kind, 1, s + rn).start()
+
+                    @pl.when((zo == z) & (z == 0))
+                    def _():
+                        def body(at):
+                            out[i, pl.ds(at, 16), :] = here(at) + from_chain(at, 0)
+
+                        loop(rows, 16, body)
+
+                    if kind == "b":
+                        @pl.when((zo == z) & (z > 0))
+                        def _():
+                            def body(at):
+                                out[i, pl.ds(at, 16), :] = here(at) + from_chain(at, 0) + from_chain(at, 1)
+
+                            loop(rows, 16, body)
+
+                by_kind(plan, k, step, low, high)
+
+    def grad_close(owners, low, high):
+        grad_sides(owners, low, high, lambda copy: copy.wait_send())
+        for zo in owners:
+            for i in range(3):
+                def close(kind):
+                    @pl.when(zo != z)
+                    def _():
+                        chain_copy(3 * zo + i, kind, 0, s).wait_send()
+
+                by_kind(plan, 3 * (zo * rn + r) + i, close, low, high)
+
+    every = [owner(j) for j in range(3)]
+    start = lambda copy: copy.start()
+    grad_sides(every, plan.nq, plan.nb, start)
+
+    for d in range(1, ZN):
+        zs = lax.rem(z + d, ZN)
+        remote(dq.at[0], q_in.at[zs], q_s.at[0], q_r.at[zs], s, t).wait_recv()
+        remote(stage.at[d], kv_in.at[zs], k_s.at[0], k_r.at[zs], s, t).wait_recv()
+    for p in range(2):
+        cols = slice(p * LANES, (p + 1) * LANES)
+        a, b = q_in[2 * p], q_in[2 * p + 1]
+        dqkv[:TOK_FRAME, cols] = jnp.concatenate([a[:, :HEAD], b[:, :HEAD]], axis=1)
+        dqkv[TOK_FRAME:, cols] = jnp.concatenate([a[:, HEAD:], b[:, HEAD:]], axis=1)
+        a, b = kv_in[2 * p], kv_in[2 * p + 1]
+        dqkv[:, HD + p * LANES : HD + (p + 1) * LANES] = jnp.concatenate(
+            [a[:, :HEAD], b[:, :HEAD]], axis=1
+        )
+        dqkv[:, 2 * HD + p * LANES : 2 * HD + (p + 1) * LANES] = jnp.concatenate(
+            [a[:, HEAD:], b[:, HEAD:]], axis=1
+        )
+
+    def q_grad(at):
+        gq[pl.ds(at, TILE), :] = mm_tn(first_in[:, pl.ds(at, TILE)], dqkv[...]).astype(BF16)
+
+    loop(D, TILE, q_grad)
+    grad_sides([0], 0, plan.nq, start)
+
+    def c_copy(w):
+        return remote(csend.at[w], crecv.at[w], c_s.at[w], c_r.at[w], s, sib)
+
+    def y_copy(w):
+        return remote(ysend.at[w], yrecv.at[w], y_s.at[w], y_r.at[w], s, across)
+
+    def pass_on(w):
+        c_copy(w).wait_recv()
+        ysend[w] = (own[w] + crecv[w].astype(F32)).astype(BF16)
+        y_copy(w).start()
+
+    for w in range(TILES):
+        weights = wq[w * TILE : (w + 1) * TILE, :]
+        csend[w] = mm_nt(dqkv[pl.ds(theirs, TOK_FRAME), :], weights).astype(BF16)
+        c_copy(w).start()
+        own[w] = mm_nt(dqkv[pl.ds(mine, TOK_FRAME), :], weights)
+        if w:
+            pass_on(w - 1)
+    pass_on(TILES - 1)
+
+    grad_chain(every, plan.nq, plan.nb)
+
+    for w in range(TILES):
+        y_copy(w).wait_recv()
+    row = lambda part: mod[pl.ds(c * 6 + part, 1), :]
+    dm[...] = jnp.zeros_like(dm)
+
+    def input_rows(at):
+        rows = pl.ds(at, 64)
+        tok_rows = pl.ds(mine + at, 64)
+        grads = jnp.concatenate(
+            [ysend[w, rows].astype(F32) + yrecv[w, rows].astype(F32) for w in range(TILES)], axis=1
+        )
+        normed, inverse = normalize(tokens[tok_rows, :].astype(F32))
+        add_to(dm, 0, grads)
+        add_to(dm, 1, grads * normed)
+        igrad[tok_rows, :] = dmid[rows, :] + norm_back(grads * (1.0 + row(1)), normed, inverse)
+
+    loop(TOK_FRAME, 64, input_rows)
+
+    def e_copy(base):
+        ref = igrad.at[pl.ds(base, TOK_FRAME)]
+        return remote(ref, ref, e_s, e_r, s, sib)
+
+    e_copy(mine).start()
+
+    for block in range(6 * D // LANES):
+        part, at = block // (D // LANES), block % (D // LANES)
+        src = dm if part < 2 else dm4
+        lane = slice(at * LANES, (at + 1) * LANES)
+        from_row = part if part < 2 else part - 2
+        dm3[block // MCOLS, block % MCOLS : block % MCOLS + 1, :] = src[from_row : from_row + 1, lane]
+    h_copy = lambda frame: remote(dm3.at[sib], dboth.at[frame], h_s, h_r, s, sib)
+    h_copy(c).start()
+    dboth[c] = dm3[t]
+    h_copy(1 - c).wait_recv()
+
+    def m_copy(src):
+        return remote(dboth, dall.at[s], m_s.at[src - plan.first_mod], m_r.at[s], src, t)
+
+    for src in range(plan.first_mod, n):
+        @pl.when(s == src)
+        def _():
+            dall[s] = dboth[...]
+
+        @pl.when(s != src)
+        def _():
+            m_copy(src).start()
+
+    grad_chain([0], 0, plan.nq)
+
+    @pl.when(s >= plan.first_mod)
+    def _():
+        for d in range(1, n):
+            other = lax.rem(s + d, n)
+            remote(dboth, dall.at[other], m_s.at[0], m_r.at[other], s, t).wait_recv()
+
+    e_copy(theirs).wait_recv()
+    for d in range(1, ZN):
+        q_copy(d).wait_send()
+        kv_copy(d).wait_send()
+    for d in order:
+        for e in range(1, rn):
+            side_copy(d, e).wait_send()
+    grad_close(every, plan.nq, plan.nb)
+    grad_close([0], 0, plan.nq)
+    for w in range(TILES):
+        c_copy(w).wait_send()
+        y_copy(w).wait_send()
+    e_copy(mine).wait_send()
+    h_copy(c).wait_send()
+    for src in range(plan.first_mod, n):
+        @pl.when(s != src)
+        def _():
+            m_copy(src).wait_send()
+
+
+def tail_part(plan, dq, dkv, first_in, wq, tokens, dmid, mod_rows, dm4, gb, cid):
+    n, rn = plan.n, plan.r
+    rows = F_DEV * TOK_FRAME
+    tiles = pltpu.VMEM((TILES, TOK_FRAME, TILE), BF16)
+    mods = n - plan.first_mod
     return call(
-        functools.partial(scatter_kernel, plan),
+        functools.partial(tail_kernel, plan),
         (
+            jax.ShapeDtypeStruct((rows, D), F32),
             jax.ShapeDtypeStruct((3, plan.uq, QKV), F32),
             jax.ShapeDtypeStruct((3, plan.ub, D), F32),
+            jax.ShapeDtypeStruct((n, F_DEV, 16, LANES), F32),
         ),
         [
-            pltpu.VMEM((rn - 1, 9, plan.uq, QKV), BF16),
+            pltpu.VMEM((ZN, rows, LANES), BF16),
+            pltpu.VMEM((rn - 1, ZN, rows, LANES), BF16),
+            pltpu.VMEM((ZN, TOK_FRAME, LANES), BF16),
+            pltpu.VMEM((ZN, rows, LANES), BF16),
+            pltpu.VMEM((rows, QKV), BF16),
+            pltpu.VMEM((D, QKV), BF16),
+            pltpu.VMEM((TILES, TOK_FRAME, TILE), F32), tiles, tiles, tiles, tiles,
+            pltpu.VMEM((8, D), F32),
+            pltpu.VMEM((TP, 16, LANES), F32),
+            pltpu.VMEM((F_DEV, 16, LANES), F32),
+            pltpu.VMEM((rn - 1, 3, plan.uq, QKV), BF16),
             pltpu.VMEM((rn - 1, 9, plan.ub, D), BF16),
-            pltpu.VMEM((2, 9, plan.uq, QKV), BF16),
+            pltpu.VMEM((3, plan.uq, QKV), BF16),
             pltpu.VMEM((2, 9, plan.ub, D), BF16),
+            DMA((ZN - 1,)), DMA((ZN,)), DMA((ZN - 1,)), DMA((ZN,)), DMA((ZN, rn - 1)), DMA((ZN, rn - 1)),
+            DMA((TILES,)), DMA((TILES,)), DMA((TILES,)), DMA((TILES,)),
+            DMA, DMA, DMA, DMA, DMA((mods,)), DMA((n,)),
             DMA((9, rn - 1)), DMA((9, rn - 1)), DMA((9,)), DMA((9, 2)),
         ],
-        [VM, VM],
+        [VM] * 9,
         cid,
-        name="scatter_grads",
-    )(gq, gb)
+        name="tail_part",
+    )(dq, dkv, first_in, wq, tokens, dmid, mod_rows, dm4, gb)
 
 
 def adam_kernel(plan, meta, oq, ob, cond, dmod, master, one, two, average, n_master, n_one, n_two, n_average):
@@ -1092,7 +1183,7 @@
             for j in range(MCOLS):
                 update(
                     pl.ds(base + j, plan.um, stride=MCOLS),
-                    mm(at, dmod[:, j * LANES : (j + 1) * LANES]),
+                    mm(at, dmod[pl.ds(j, plan.frames, stride=16), :].astype(BF16)),
                 )
 
 
@@ -1111,29 +1202,15 @@
     return rows.reshape(F_DEV, TOK_FRAME, rows.shape[1])
 
 
-def frame_scale(rows, factor):
-    return (by_frame(rows) * factor[:, None, :]).reshape(rows.shape)
-
-
 def frame_affine(rows, factor, offset_rows):
     return (by_frame(rows) * (1.0 + factor)[:, None, :] + offset_rows[:, None, :]).reshape(
         rows.shape
     )
 
 
-def frame_total(rows):
-    return jnp.sum(by_frame(rows), axis=1)
-
-
 def pack_heads(rows):
     return rows.reshape(F_DEV, TOK_FRAME, ZN, HEAD).transpose(2, 1, 0, 3).reshape(
         ZN, TOK_FRAME, F_DEV * HEAD
-    )
-
-
-def unpack_heads(packs):
-    return packs.reshape(ZN, TOK_FRAME, F_DEV, HEAD).transpose(2, 1, 0, 3).reshape(
-        F_DEV * TOK_FRAME, ZN * HEAD
     )
 
 
@@ -1192,39 +1269,16 @@
         plan, o_mine, wo.reshape(HEADS * HEAD, D), wb, tokens, grad_out, mod_rows, 2
     )
     dq_mine, dkv_all = attend_back(plan, meta, q_mine, kv_all, do_mine, o_rows, lse)
-    dq_heads, dkv_heads = exchange_dkv(plan, dq_mine, dkv_all, 7)
-    qkv_grad = jnp.concatenate(
-        [unpack_heads(dq_heads)]
-        + [dkv_heads[h][:, :HEAD] for h in range(ZN)]
-        + [dkv_heads[h][:, HEAD:] for h in range(ZN)],
-        axis=1,
+    input_grad, own_q, own_b, mod_all = tail_part(
+        plan, dq_mine, dkv_all, first_in, wq, tokens, middle_grad, mod_rows, mod_four, grads_b, 3
     )
-    qkv_weight_grad = mm_tn(first_in, qkv_grad)
-    first_grad = total_tp(mm_nt(qkv_grad, wq), 8, "total_first")
-    scale_one_grad = frame_total(first_grad * normed_one)
-    shift_one_grad = frame_total(first_grad)
-    input_grad = middle_grad + norm_back(
-        frame_scale(first_grad, 1.0 + scale_one), normed_one, inverse_one
-    )
-    mod_terms = jnp.concatenate(
-        [
-            shift_one_grad,
-            scale_one_grad,
-            mod_four[:, :4].reshape(F_DEV, 4 * D),
-        ],
-        axis=1,
-    )
-    mod_grad = lax.all_gather(
-        lax.dynamic_slice_in_dim(mod_terms, t * MT, MT, axis=1), "seq", axis=0, tiled=True
-    ).astype(BF16)
-    own_q, own_b = scatter_grads(plan, qkv_weight_grad.astype(BF16), grads_b, 9)
     updated = adam(
         plan,
         s[None].astype(jnp.int32),
         own_q,
         own_b,
         cond_units.transpose(0, 2, 1),
-        mod_grad,
+        flat(mod_all),
         flat(master),
         flat(moment_one),
         flat(moment_two),

time: 527 us -> 453 us (0.86); the launches traced: 520 us -> 453 us
  blocking collectives: 36.1 us -> 0 us
  other arithmetic: 20.2 us -> 6.94 us
  local copies, waits for them, and re-layouts: 16.3 us -> 8.36 us
  matrix products: 8.84 us -> 1.86 us
    all_gather x1 -> x0, blocking collectives: 36.1 us -> none  [local(): lax.all_gather(lax.dynamic_slice_in_dim(mod_terms, t * MT, MT, axis=1), '...]
    reduce_sum x3 -> x0, other arithmetic: 7.39 us -> none  [the longest x2 4.25 us: frame_total(): return jnp.sum(by_frame(rows), axis=1)]
    dot_general x2 -> x0, matrix products: 6.99 us -> none  [the longest x1 3.88 us: mm_tn(): lax.dot_general(left, right, (((0,), (0,)), ((), ())), preferred_element_...]
    mul x1 -> x0, other arithmetic: 5.76 us -> none  [local(): scale_one_grad = frame_total(first_grad * normed_one)]
    pallas_call x3 -> x1, Pallas kernels: 150 us -> 149 us  [tail_part(): call(functools.partial(tail_kernel, plan), (jax.ShapeDtypeStruct((rows, D...]
where the time goes in v3:
time: 453 us
  Pallas kernels  435 us (96%)
  local copies, waits for them, and re-layouts  8.36 us (2%)
  other arithmetic  6.94 us (2%)
    pallas_call x1, Pallas kernels, tail_part(): call(functools.partial(tail_kernel, plan), (jax.ShapeDtypeStruct((rows, D...  149 us
    pallas_call x1, Pallas kernels, gather_weights(): call(functools.partial(gather_kernel, plan), (jax.ShapeDtypeStruct((D, QK...  94.4 us
    pallas_call x1, Pallas kernels, middle_part(): call(functools.partial(middle_kernel, plan), (jax.ShapeDtypeStruct((rows,...  82.9 us
    pallas_call x1, Pallas kernels, exchange_qkv(): call(functools.partial(qkv_kernel, plan), (jax.ShapeDtypeStruct((ZN, TOK_...  55.7 us
    pallas_call x1, Pallas kernels, attend_back(): call(functools.partial(attend_back_kernel, plan), (jax.ShapeDtypeStruct((...  20.8 us
    pallas_call x1, Pallas kernels, attend(): call(functools.partial(attend_kernel, plan), (jax.ShapeDtypeStruct((ZN, F...  19.5 us
    pallas_call x1, Pallas kernels, adam(): call(functools.partial(adam_kernel, plan), (shape,) * 4, [], [SM] + [VM]...  11.9 us

profile of v3, /device:TPU:0, one launch (start us, length us, event | category | flops | bytes accessed | tf_op | source)
XLA Modules:
  0.0 452.6 jit_solution(13679893666549691816)
XLA Ops:
  0.6 0.0 copy-start
  0.7 1.4 pad_add_fusion.meta
  2.0 0.7 subtract_multiply_fusion
  2.7 1.7 convert_reduce_fusion
  4.4 0.6 fusion.2
  5.0 0.5 multiply_convert_fusion
  5.5 0.2 copy.21
  5.7 0.7 copy.22.cond
  6.4 94.4 %gather_weights.1 = (bf16[1024,768]{1,0:T(8,128)(2,1)}, bf16[2304,1024]{1,0:T(8,128)(2,1)}, f32[4,24,128]{2,1,0:T(8,128)}, bf16[4,256,1024]{2,1,0:T(8,128)(2,1)}) custom-call(f32[4608,128]{1,0:T(8,128)} %bitcast.42, bf16[8,16,128]{2,1,0:T(8,128)(2,1)} %copy.22.cond), custom_call_target="tpu_custom_call" | custom-call | tf_op jit(solution)/shard_map/gather_weights/pallas_call | solution.py:305
  100.8 0.8 reshape.79
  101.7 0.7 reshape_reshape.3.mod
  102.4 1.2 fusion.5.first_in
  103.6 0.2 copy-done.7
  103.8 1.4 convolution_convert_fusion
  105.2 0.2 copy.25
  105.4 0.1 reshape.81
  105.5 0.1 copy.26
  105.5 0.9 copy.27.q
  106.5 0.4 fusion.8
  106.8 0.2 maximum_bitcast_fusion
  107.1 0.2 maximum_bitcast_fusion.2
  107.3 1.0 pad_maximum_fusion.kv
  108.3 55.7 %exchange_qkv.1 = (bf16[4,384,128]{2,1,0:T(8,128)(2,1)}, bf16[8,768,128]{2,1,0:T(8,128)(2,1)}) custom-call(bf16[4,384,128]{2,1,0:T(8,128)(2,1)} %copy.27.q, bf16[4,768,128]{2,1,0:T(8,128)(2,1)} %pad_maximum_fusion.kv), custom_call_target="tpu_custom_call" | custom-call | tf_op jit(solution)/shard_map/exchange_qkv/pallas_call | solution.py:384
  163.9 19.5 %attend.1 = (bf16[4,2,192,128]{3,2,1,0:T(8,128)(2,1)}, f32[8,64,384]{2,1,0:T(8,128)}, f32[8,1,384]{2,1,0:T(1,128)}) custom-call(s32[17]{0:T(128)} %pad_add_fusion.meta, bf16[4,384,128]{2,1,0:T(8,128)(2,1)} %get-tuple-element.32.q, bf16[8,768,128]{2,1,0:T(8,128)(2,1)} %get-tuple-element.33.kv), custom_call_target="tpu_custom_call" | custom-call | tf_op jit(solution)/shard_map/attend/pallas_call | solution.py:446
  183.4 82.9 %middle_part.1 = (bf16[768,1024]{1,0:T(8,128)(2,1)}, bf16[2304,1024]{1,0:T(8,128)(2,1)}, bf16[4,2,192,128]{3,2,1,0:T(8,128)(2,1)}, f32[384,1024]{1,0:T(8,128)}, f32[8,1024]{1,0:T(8,128)}) custom-call(bf16[4,2,192,128]{3,2,1,0:T(8,128)(2,1)} %get-tuple-element.34.o_mine, bf16[1024,1024]{1,0:T(8,128)(2,1)} %bitcast.49, ...), custom_call_target="tpu_custom_call" | custom-call | tf_op jit(solution)/shard_map/middle_part/pallas_call | solution.py:780
  266.4 20.8 %attend_back.1 = (bf16[4,384,128]{2,1,0:T(8,128)(2,1)}, bf16[8,768,128]{2,1,0:T(8,128)(2,1)}) custom-call(s32[17]{0:T(128)} %pad_add_fusion.meta, bf16[4,384,128]{2,1,0:T(8,128)(2,1)} %get-tuple-element.32.q, bf16[8,768,128]{2,1,0:T(8,128)(2,1)} %get-tuple-element.33.kv, bf16[4,2,192,128]{3,2,1,0:T(8,128)(2,1)} %get-tuple-element.38.do, ...), custom_call_target="tpu_custom_call" | custom-call | tf_op jit(solution)/shard_map/attend_back/pallas_call | solution.py:504
  287.2 149.3 %tail_part.1 = (f32[768,1024]{1,0:T(8,128)}, f32[3,256,768]{2,1,0:T(8,128)}, f32[3,192,1024]{2,1,0:T(8,128)}, f32[8,2,16,128]{3,2,1,0:T(8,128)}) custom-call(bf16[4,384,128]{2,1,0:T(8,128)(2,1)} %get-tuple-element.41.dq, bf16[8,768,128]{2,1,0:T(8,128)(2,1)} %get-tuple-element.42.dkv, bf16[768,1024]{1,0:T(8,128)(2,1)} %copy-done.4, ...), custom_call_target="tpu_custom_call" | custom-call | tf_op jit(solution)/shard_map/tail_part/pallas_call | solution.py:1112
  436.6 11.9 %adam.1 = (f32[4608,128]{1,0:T(8,128)}, f32[4608,128]{1,0:T(8,128)}, f32[4608,128]{1,0:T(8,128)}, f32[4608,128]{1,0:T(8,128)}) custom-call(s32[1]{0:T(128)} %bitcast.14.meta, f32[3,256,768]{2,1,0:T(8,128)} %get-tuple-element.47.oq, f32[3,192,1024]{2,1,0:T(8,128)} %get-tuple-element.48.ob, bf16[8,128,16]{2,1,0:T(8,128)(2,1)} %bitcast.45, ...), custom_call_target="tpu_custom_call" | custom-call | tf_op jit(solution)/shard_map/adam/pallas_call | solution.py:1192
  448.5 0.0 copy-start.1
  448.5 1.1 copy.35
  449.6 1.3 copy-done.5
  450.9 1.7 copy.36
  (20 shorter events, 0.1 us)
Async XLA Ops:
  0.6 4.3 copy-start
  0.7 3.7 copy-start.2
  5.5 96.9 %copy-start.3 = (bf16[768,1024]{1,0:T(8,128)(2,1)S(1)}, bf16[768,1024]{1,0:T(8,128)(2,1)}, u32[]{:S(2)}) copy-start(bf16[768,1024]{1,0:T(8,128)(2,1)} %tokens.3) | copy-start | bytes 4718596
  5.6 98.0 %copy-start.6 = (bf16[16,1024]{0,1:T(8,128)(2,1)}, bf16[16,1024]{0,1:T(8,128)(2,1)S(1)}, u32[]{:S(2)}) copy-start(bf16[16,1024]{0,1:T(8,128)(2,1)S(1)} %copy.21) | copy-start | bytes 98308
  102.4 1.4 copy-start.7
  103.8 1.4 copy-start.4
  436.6 11.9 %copy-start.8 = (bf16[768,1024]{1,0:T(8,128)(2,1)S(1)}, bf16[768,1024]{1,0:T(8,128)(2,1)}, u32[]{:S(2)}) copy-start(bf16[768,1024]{1,0:T(8,128)(2,1)} %get-tuple-element.76) | copy-start | bytes 4718596
  448.5 2.5 copy-start.5
  448.5 4.1 copy-start.1

commit v4 on v3

--- a/solution.py
+++ b/solution.py
@@ -71,6 +71,18 @@
     )
 
 
+def loop(count, step, body):
+    def turn(i, carry):
+        body(pl.multiple_of(i * step, step))
+        return carry
+
+    lax.fori_loop(0, count // step, turn, 0)
+
+
+def add_to(ref, row, values):
+    ref[pl.ds(row, 1), :] += jnp.sum(values, axis=0, keepdims=True)
+
+
 class Plan:
     def __init__(self, seq_count):
         self.n = seq_count
@@ -143,13 +155,95 @@
         out_specs=jax.tree.map(lambda _: VM, outs),
         scratch_shapes=scratch,
         compiler_params=pltpu.CompilerParams(**params),
+        cost_estimate=cost,
         name=name,
     )
 
 
-def gather_kernel(
-    plan, master, cond, wq, wb, mod, wo, tile, macc, mpart, mrecv,
-    send_sem, recv_sem, msend, mrecv_sem, tsend, trecv, osend, orecv,
+class Travel:
+    def __init__(self, plan, wb, send_sem, recv_sem, low, high):
+        self.plan, self.wb, self.low, self.high = plan, wb, low, high
+        self.send_sem, self.recv_sem = send_sem, recv_sem
+        self.s, self.t, self.z, self.r = place(plan)
+
+    def move(self, k, lu, sem, owner_r, to_s):
+        ref = unit_of(self.plan, k, "b", None, self.wb)
+        return remote(ref, ref, self.send_sem.at[lu, sem], self.recv_sem.at[lu, owner_r], to_s, self.t)
+
+    def spread(self, k, lu, act, up=None, down=None, sides=True):
+        plan, rn = self.plan, self.plan.r
+
+        def go(kind):
+            if up is not None:
+                @pl.when(up)
+                def _():
+                    act(self.move(k, lu, 0, self.r, self.s + rn))
+            if down is not None:
+                @pl.when(down)
+                def _():
+                    act(self.move(k, lu, 1, self.r, self.s - rn))
+            if sides:
+                for d in range(1, rn):
+                    act(self.move(k, lu, 1 + d, self.r, self.z * rn + lax.rem(self.r + d, rn)))
+
+        by_kind(plan, k, go, self.low, self.high)
+
+    def own(self, act, up=True, down=True, sides=True):
+        for i in range(3):
+            self.spread(
+                3 * self.s + i,
+                3 * self.z + i,
+                act,
+                (self.z < ZN - 1) if up else None,
+                (self.z > 0) if down else None,
+                sides,
+            )
+
+    def line(self, d, act, wait=True):
+        for i in range(3):
+            for side in (0, 1):
+                zs = self.z - d if side == 0 else self.z + d
+                k = 3 * (zs * self.plan.r + self.r) + i
+                lu = 3 * zs + i
+
+                @pl.when((zs >= 0) & (zs < ZN))
+                def _():
+                    if wait:
+                        by_kind(
+                            self.plan, k,
+                            lambda kind: self.move(k, lu, 0, self.r, self.s).wait_recv(),
+                            self.low, self.high,
+                        )
+                    if side == 0:
+                        self.spread(k, lu, act, self.z < ZN - 1, None)
+                    else:
+                        self.spread(k, lu, act, None, self.z > 0)
+
+    def from_sides(self):
+        rn = self.plan.r
+        for d in range(1, rn):
+            other = lax.rem(self.r + d, rn)
+            for zs in range(ZN):
+                for i in range(3):
+                    k = 3 * (zs * rn + other) + i
+                    by_kind(
+                        self.plan, k,
+                        lambda kind: self.move(k, 3 * zs + i, 0, other, self.s).wait_recv(),
+                        self.low, self.high,
+                    )
+
+    def close(self):
+        done = lambda copy: copy.wait_send()
+        self.own(done)
+        for d in range(1, ZN):
+            self.line(d, done, wait=False)
+
+
+def head_kernel(
+    plan, master, cond, tokens,
+    wq, wb, mods, first_in, q_out, kv_out,
+    tile, macc, mpart, mrecv, mod, norm, q_send, kv_send,
+    qp_s, qc_s, q_r, b_s, b_r, m_s, m_r, t_s, t_r, as_, ar, ks, kr, xs, xr,
 ):
     s, t, z, r = place(plan)
     n, rn = plan.n, plan.r
@@ -157,33 +251,56 @@
         [(lax.rem(s + d, n), t) for d in range(1, n)]
         + [(s, lax.rem(t + d, TP)) for d in range(1, TP)]
     )
-
-    def unit(k, kind):
-        if kind == "q":
-            return wq.at[pl.ds(pl.multiple_of(k * plan.uq, plan.uq), plan.uq)]
-        return wb.at[pl.ds(pl.multiple_of((k - plan.nq) * plan.ub, plan.ub), plan.ub)]
-
-    def move(k, lu, kind, sem, owner_r, to_s):
-        ref = unit(k, kind)
-        return remote(ref, ref, send_sem.at[lu, sem], recv_sem.at[lu, owner_r], to_s, t)
-
-    def spread(k, lu, up, down, act):
-        def for_kind(kind):
-            if up is not None:
-                @pl.when(up)
+    start = lambda copy: copy.start()
+    done = lambda copy: copy.wait_send()
+    half = plan.uq // 2
+
+    def q_rows(k, h):
+        return wq.at[pl.ds(pl.multiple_of(k * plan.uq + h * half, half), half)]
+
+    def q_copy(k, h, sem, to_s):
+        ref = q_rows(k, h)
+        return remote(ref, ref, sem, q_r.at[2 * k + h], to_s, t)
+
+    def q_arrived(k, h):
+        q_copy(k, h, qc_s.at[0, 0], s).wait_recv()
+
+    def column(j):
+        return r + rn * lax.rem(j + r, 2)
+
+    def q_own(act):
+        for i in range(3):
+            k = 3 * s + i
+
+            @pl.when(k < plan.nq)
+            def _():
+                for h in range(2):
+                    for d in range(1, rn):
+                        act(q_copy(k, h, qp_s.at[2 * i + h, d - 1], lax.rem(r + d, rn)))
+
+    def q_line(act, wait):
+        for j in range(2):
+            k = column(j)
+            for h in range(2):
+                if wait:
+                    @pl.when((z > 0) | (lax.div(k, 3) != r))
+                    def _():
+                        q_arrived(k, h)
+
+                @pl.when(z < ZN - 1)
                 def _():
-                    act(move(k, lu, kind, 0, r, s + rn))
-            if down is not None:
-                @pl.when(down)
+                    act(q_copy(k, h, qc_s.at[2 * j + h, 0], s + rn))
+
+                @pl.when(z > 0)
                 def _():
-                    act(move(k, lu, kind, 1, r, s - rn))
-            for d in range(1, rn):
-                act(move(k, lu, kind, 1 + d, r, z * rn + lax.rem(r + d, rn)))
-
-        by_kind(plan, k, for_kind)
-
-    start = lambda copy: copy.start()
-    finish = lambda copy: copy.wait_send()
+                    for d in range(1, rn):
+                        act(
+                            q_copy(
+                                k, h, qc_s.at[2 * j + h, d], z * rn + lax.rem(r + d, rn)
+                            )
+                        )
+
+    travel = Travel(plan, wb, b_s, b_r, plan.nq, plan.nb)
 
     for i in range(3):
         k = 3 * s + i
@@ -201,7 +318,18 @@
                 ].astype(BF16)
 
         by_kind(plan, k, fill)
-        spread(k, 3 * z + i, z < ZN - 1, z > 0, start)
+
+        @pl.when(k < plan.nq)
+        def _():
+            for h in range(2):
+                for d in range(1, rn):
+                    q_copy(k, h, qp_s.at[2 * i + h, d - 1], lax.rem(r + d, rn)).start()
+
+    @pl.when(z == 0)
+    def _():
+        q_line(start, True)
+
+    travel.own(start, up=False, sides=False)
 
     macc[...] = jnp.zeros_like(macc)
     for i in range(3):
@@ -217,6 +345,10 @@
             macc[...] += mm(cond[k - plan.nb], tile[...])
 
     fm = plan.first_mod
+
+    def m_copy(d):
+        to = lax.rem(s + d, n)
+        return remote(mpart.at[to], mrecv.at[s - fm], m_s.at[d - 1], m_r.at[s - fm], to, t)
 
     @pl.when(s >= fm)
     def _():
@@ -227,171 +359,167 @@
                 ]
         mrecv[s - fm] = mpart[s]
         for d in range(1, n):
-            to = lax.rem(s + d, n)
-            remote(mpart.at[to], mrecv.at[s - fm], msend.at[d - 1], mrecv_sem.at[s - fm], to, t).start()
+            m_copy(d).start()
+
+    def norm_rows(at):
+        rows = pl.ds(at, 64)
+        norm[rows, :] = normalize(tokens[rows, :].astype(F32))[0]
+
+    loop(F_DEV * TOK_FRAME, 64, norm_rows)
+
+    @pl.when(z > 0)
+    def _():
+        q_line(start, True)
+
+    travel.own(start, down=False)
 
     for src in range(fm, n):
         @pl.when(s != src)
         def _():
-            remote(
-                mpart.at[0], mrecv.at[src - fm], msend.at[0], mrecv_sem.at[src - fm], s, t
-            ).wait_recv()
+            remote(mpart.at[0], mrecv.at[src - fm], m_s.at[0], m_r.at[src - fm], s, t).wait_recv()
 
     total = mrecv[0]
     for src in range(1, n - fm):
         total = total + mrecv[src]
     mod[t] = total
+
+    def t_copy(d):
+        return remote(mod.at[t], mod.at[t], t_s.at[d - 1], t_r.at[t], s, lax.rem(t + d, TP))
+
     for d in range(1, TP):
-        remote(mod.at[t], mod.at[t], tsend.at[d - 1], trecv.at[t], s, lax.rem(t + d, TP)).start()
-
-    for d in range(1, ZN):
-        for i in range(3):
-            for side in (0, 1):
-                zs = z - d if side == 0 else z + d
-                k = 3 * (zs * rn + r) + i
-                lu = 3 * zs + i
-
-                @pl.when((zs >= 0) & (zs < ZN))
-                def _():
-                    by_kind(plan, k, lambda kind: move(k, lu, kind, 0, r, s).wait_recv())
-                    if side == 0:
-                        spread(k, lu, z < ZN - 1, None, start)
-                    else:
-                        spread(k, lu, None, z > 0, start)
-
-    for d in range(1, rn):
-        other = lax.rem(r + d, rn)
-        for zs in range(ZN):
-            for i in range(3):
-                k = 3 * (zs * rn + other) + i
-                by_kind(plan, k, lambda kind: move(k, 3 * zs + i, kind, 0, other, s).wait_recv())
-
-    wo[t] = wb[:HD]
-    for d in range(1, TP):
-        remote(wo.at[t], wo.at[t], osend.at[d - 1], orecv.at[t], s, lax.rem(t + d, TP)).start()
+        t_copy(d).start()
     for d in range(1, TP):
         other = lax.rem(t + d, TP)
-        remote(wo.at[t], wo.at[other], osend.at[0], orecv.at[other], s, t).wait_recv()
-        remote(wo.at[t], wo.at[t], osend.at[d - 1], orecv.at[t], s, other).wait_send()
-        remote(mod.at[t], mod.at[other], tsend.at[0], trecv.at[other], s, t).wait_recv()
-        remote(mod.at[t], mod.at[t], tsend.at[d - 1], trecv.at[t], s, other).wait_send()
+        remote(mod.at[t], mod.at[other], t_s.at[0], t_r.at[other], s, t).wait_recv()
+    for f in range(F_DEV):
+        for block in range(TP * MCOLS):
+            part, at = block // (D // LANES), block % (D // LANES)
+            mods[f * 6 + part : f * 6 + part + 1, at * LANES : (at + 1) * LANES] = mod[
+                block // MCOLS, f * MCOLS + block % MCOLS : f * MCOLS + block % MCOLS + 1, :
+            ]
+
+    def affine(f):
+        def body(at):
+            rows = pl.ds(f * TOK_FRAME + at, 64)
+            first_in[rows, :] = (
+                norm[rows, :] * (1.0 + mods[f * 6 + 1 : f * 6 + 2, :]) + mods[f * 6 : f * 6 + 1, :]
+            ).astype(BF16)
+
+        loop(TOK_FRAME, 64, body)
+
+    for f in range(F_DEV):
+        affine(f)
+
+    for k in range(plan.nq):
+        for h in range(2):
+            if rn > 1:
+                at_zero = (z == 0) & (k // 3 != r) & (k % rn != r)
+
+                @pl.when(at_zero | (z > 0) & (k % rn != r))
+                def _():
+                    q_arrived(k, h)
+
+    keys = mm(first_in[...], wq[:, HD : 2 * HD]).astype(BF16)
+    values = mm(first_in[...], wq[:, 2 * HD :]).astype(BF16)
+    for h in range(ZN):
+        cols = slice(h * HEAD, (h + 1) * HEAD)
+        kv_send[h] = jnp.concatenate([keys[:, cols], values[:, cols]], axis=1)
+
+    def kv_copy(d):
+        h = lax.rem(z + d, ZN)
+        return remote(kv_send.at[h], kv_out.at[s], ks.at[d - 1], kr.at[z], h * rn + r, t)
+
+    def a_copy(d):
+        h = lax.rem(z + d, ZN)
+        return remote(q_send.at[h], q_out.at[z], as_.at[d - 1], ar.at[z], h * rn + r, t)
+
+    def side_copy(zs, e):
+        at = zs * rn + r
+        ref = kv_out.at[at]
+        return remote(ref, ref, xs.at[zs, e - 1], xr.at[at], z * rn + lax.rem(r + e, rn), t)
+
+    for d in range(1, ZN):
+        kv_copy(d).start()
+    kv_out[s] = kv_send[z]
+    for e in range(1, rn):
+        side_copy(z, e).start()
+    queries = mm(first_in[...], wq[:, :HD]).astype(BF16)
+    for h in range(ZN):
+        cols = slice(h * HEAD, (h + 1) * HEAD)
+        q_send[h] = jnp.concatenate([queries[:TOK_FRAME, cols], queries[TOK_FRAME:, cols]], axis=1)
+    for d in range(1, ZN):
+        a_copy(d).start()
+    q_out[z] = q_send[z]
+
+    travel.line(1, start)
+    for d in range(1, ZN):
+        zs = lax.rem(z + d, ZN)
+        remote(kv_send.at[0], kv_out.at[zs * rn + r], ks.at[0], kr.at[zs], s, t).wait_recv()
+        for e in range(1, rn):
+            side_copy(zs, e).start()
+    for d in range(2, ZN):
+        travel.line(d, start)
+    for d in range(1, ZN):
+        zs = lax.rem(z + d, ZN)
+        remote(q_send.at[0], q_out.at[zs], as_.at[0], ar.at[zs], s, t).wait_recv()
+    for e in range(1, rn):
+        for zs in range(ZN):
+            at = zs * rn + lax.rem(r + e, rn)
+            remote(kv_out.at[at], kv_out.at[at], xs.at[0, 0], xr.at[at], s, t).wait_recv()
+    travel.from_sides()
+
+    q_own(done)
+    q_line(done, False)
+    travel.close()
 
     @pl.when(s >= fm)
     def _():
         for d in range(1, n):
-            to = lax.rem(s + d, n)
-            remote(mpart.at[to], mrecv.at[s - fm], msend.at[d - 1], mrecv_sem.at[s - fm], to, t).wait_send()
-
-    for i in range(3):
-        spread(3 * s + i, 3 * z + i, z < ZN - 1, z > 0, finish)
+            m_copy(d).wait_send()
+
+    for d in range(1, TP):
+        t_copy(d).wait_send()
     for d in range(1, ZN):
-        for i in range(3):
-            for side in (0, 1):
-                zs = z - d if side == 0 else z + d
-                k = 3 * (zs * rn + r) + i
-                lu = 3 * zs + i
-
-                @pl.when((zs >= 0) & (zs < ZN))
-                def _():
-                    if side == 0:
-                        spread(k, lu, z < ZN - 1, None, finish)
-                    else:
-                        spread(k, lu, None, z > 0, finish)
-
-
-def gather_weights(plan, master, cond_units, cid):
-    n = plan.n
+        kv_copy(d).wait_send()
+        a_copy(d).wait_send()
+    for zs in range(ZN):
+        for e in range(1, rn):
+            side_copy(zs, e).wait_send()
+
+
+def head_part(plan, master, cond_units, tokens, cid):
+    n, rn = plan.n, plan.r
     mrows = F_DEV * MCOLS
+    rows = F_DEV * TOK_FRAME
+    mods = n - plan.first_mod
     return call(
-        functools.partial(gather_kernel, plan),
+        functools.partial(head_kernel, plan),
         (
             jax.ShapeDtypeStruct((D, QKV), BF16),
             jax.ShapeDtypeStruct((BROWS, D), BF16),
-            jax.ShapeDtypeStruct((TP, mrows, LANES), F32),
-            jax.ShapeDtypeStruct((TP, HD, D), BF16),
+            jax.ShapeDtypeStruct((F_DEV * 6, D), F32),
+            jax.ShapeDtypeStruct((rows, D), BF16),
+            jax.ShapeDtypeStruct((ZN, TOK_FRAME, LANES), BF16),
+            jax.ShapeDtypeStruct((n, rows, LANES), BF16),
         ),
         [
             pltpu.VMEM((plan.um, MT), BF16),
             pltpu.VMEM((plan.frames, MT), F32),
             pltpu.VMEM((n, mrows, LANES), F32),
-            pltpu.VMEM((n - plan.first_mod, mrows, LANES), F32),
-            DMA((3 * ZN, plan.r + 1)),
-            DMA((3 * ZN, plan.r)),
-            DMA((n - 1,)),
-            DMA((n - plan.first_mod,)),
-            DMA((TP - 1,)),
-            DMA((TP,)),
-            DMA((TP - 1,)),
-            DMA((TP,)),
+            pltpu.VMEM((mods, mrows, LANES), F32),
+            pltpu.VMEM((TP, mrows, LANES), F32),
+            pltpu.VMEM((rows, D), F32),
+            pltpu.VMEM((ZN, TOK_FRAME, LANES), BF16),
+            pltpu.VMEM((ZN, rows, LANES), BF16),
+            DMA((6, rn - 1)), DMA((4, rn)), DMA((2 * plan.nq,)),
+            DMA((3 * ZN, rn + 1)), DMA((3 * ZN, rn)),
+            DMA((n - 1,)), DMA((mods,)), DMA((TP - 1,)), DMA((TP,)),
+            DMA((ZN - 1,)), DMA((ZN,)), DMA((ZN - 1,)), DMA((ZN,)), DMA((ZN, rn - 1)), DMA((n,)),
         ],
-        [VM, VM],
+        [VM] * 3,
         cid,
-        name="gather_weights",
-    )(master, cond_units)
-
-
-def qkv_kernel(plan, q, kv, q_out, kv_out, qs, ks, rs, qr, kr, rr):
-    s, t, z, r = place(plan)
-    rn = plan.r
-    greet(
-        [(lax.rem(z + d, ZN) * rn + r, t) for d in range(1, ZN)]
-        + [(z * rn + lax.rem(r + d, rn), t) for d in range(1, rn)]
-    )
-
-    def kv_copy(d):
-        h = lax.rem(z + d, ZN)
-        return remote(kv.at[h], kv_out.at[s], ks.at[d - 1], kr.at[z], h * rn + r, t)
-
-    def q_copy(d):
-        h = lax.rem(z + d, ZN)
-        return remote(q.at[h], q_out.at[z], qs.at[d - 1], qr.at[z], h * rn + r, t)
-
-    def side_copy(zs, e):
-        at = zs * rn + r
-        src = kv_out.at[at]
-        return remote(src, src, rs.at[zs, e - 1], rr.at[at], z * rn + lax.rem(r + e, rn), t)
-
-    for d in range(1, ZN):
-        kv_copy(d).start()
-    for d in range(1, ZN):
-        q_copy(d).start()
-    kv_out[s] = kv[z]
-    q_out[z] = q[z]
-    for e in range(1, rn):
-        side_copy(z, e).start()
-    for d in range(1, ZN):
-        zs = lax.rem(z + d, ZN)
-        remote(kv.at[0], kv_out.at[zs * rn + r], ks.at[0], kr.at[zs], s, t).wait_recv()
-        for e in range(1, rn):
-            side_copy(zs, e).start()
-    for d in range(1, ZN):
-        zs = lax.rem(z + d, ZN)
-        remote(q.at[0], q_out.at[zs], qs.at[0], qr.at[zs], s, t).wait_recv()
-    for e in range(1, rn):
-        for zs in range(ZN):
-            at = zs * rn + lax.rem(r + e, rn)
-            remote(kv_out.at[at], kv_out.at[at], rs.at[0, 0], rr.at[at], s, t).wait_recv()
-    for d in range(1, ZN):
-        kv_copy(d).wait_send()
-        q_copy(d).wait_send()
-    for zs in range(ZN):
-        for e in range(1, rn):
-            side_copy(zs, e).wait_send()
-
-
-def exchange_qkv(plan, q, kv, cid):
-    rn = plan.r
-    return call(
-        functools.partial(qkv_kernel, plan),
-        (
-            jax.ShapeDtypeStruct((ZN, TOK_FRAME, LANES), BF16),
-            jax.ShapeDtypeStruct((plan.n, F_DEV * TOK_FRAME, LANES), BF16),
-        ),
-        [DMA((ZN - 1,)), DMA((ZN - 1,)), DMA((ZN, rn - 1)), DMA((ZN,)), DMA((ZN,)), DMA((plan.n,))],
-        [VM, VM],
-        cid,
-        name="exchange_qkv",
-    )(q, kv)
+        name="head_part",
+    )(master, cond_units, tokens)
 
 
 def padded(rows, low):
@@ -456,6 +584,7 @@
             pltpu.VMEM((LANES, TOK_FRAME), F32),
         ],
         [SM, VM, VM],
+        cost=pl.CostEstimate(flops=2 * 10**10, bytes_accessed=6 * 10**7, transcendentals=10**7),
         name="attend",
     )(meta, q, kv)
 
@@ -516,24 +645,12 @@
     )(meta, q, kv, do, ot, lse)
 
 
-def loop(count, step, body):
-    def turn(i, carry):
-        body(pl.multiple_of(i * step, step))
-        return carry
-
-    lax.fori_loop(0, count // step, turn, 0)
-
-
-def add_to(ref, row, values):
-    ref[pl.ds(row, 1), :] += jnp.sum(values, axis=0, keepdims=True)
-
-
 def middle_kernel(
-    plan, o_mine, wo, wb, tokens, grad_out, mod,
+    plan, o_mine, wo_across, wb, tokens, grad_out, mod,
     result, gb, do_out, dmid, dmod,
-    oall, attended, attn, mid, norm, inv, sin, hidden, dmlp, dhid, dup,
+    wo, oall, attended, attn, mid, norm, inv, sin, hidden, dmlp, dhid, dup,
     own, csend, crecv, ysend, yrecv, dattn, dsend, dwo, wsend, wrecv,
-    o_s, o_r, f_s, f_r, n_s, n_r, c_s, c_r, y_s, y_r, d_s, d_r, w_s, w_r, e_s, e_r,
+    o_s, o_r, f_s, f_r, n_s, n_r, c_s, c_r, y_s, y_r, d_s, d_r, w_s, w_r, e_s, e_r, p_s, p_r,
 ):
     s, t, z, r = place(plan)
     rn = plan.r
@@ -564,8 +681,16 @@
         ref = oall.at[y * 8 + slot]
         return remote(ref, ref, f_s.at[slot], f_r.at[slot], s, across)
 
+    def p_copy(i, tp):
+        ref = wo.at[pl.ds(pl.multiple_of(tp * HD, HD), HD)]
+        return remote(ref, ref, p_s.at[i], p_r.at[i], s, sib)
+
     for d, e in pairs:
         o_copy(d, e).start()
+    wo[pl.ds(pl.multiple_of(t * HD, HD), HD), :] = wb[:HD, :]
+    p_copy(0, t).start()
+    wo[pl.ds(pl.multiple_of(across * HD, HD), HD), :] = wo_across[...]
+    p_copy(1, across).start()
     oall[y * 8 + c * ZN + z] = o_mine[z, c]
     f_copy(c * ZN + z).start()
 
@@ -601,6 +726,9 @@
         attended[:PACK, cols] = jnp.concatenate([a[:, :HEAD], b[:, :HEAD]], axis=1)
         attended[PACK:, cols] = jnp.concatenate([a[:, HEAD:], b[:, HEAD:]], axis=1)
 
+    p_copy(0, sib).wait_recv()
+    p_copy(1, lax.rem(sib + 2, TP)).wait_recv()
+
     def attn_tile(at):
         attn[:, pl.ds(at, TILE)] = mm(attended[...], wo[:, pl.ds(at, TILE)])
 
@@ -764,6 +892,8 @@
     for slot in range(8):
         f_copy(slot).wait_send()
     n_copy(mine).wait_send()
+    p_copy(0, t).wait_send()
+    p_copy(1, across).wait_send()
     for w in range(2):
         for n in range(TILES):
             c_copy(w, n).wait_send()
@@ -772,7 +902,7 @@
     e_copy(mine).wait_send()
 
 
-def middle_part(plan, o_mine, wo, wb, tokens, grad_out, mod_rows, cid):
+def middle_part(plan, o_mine, wo_across, wb, tokens, grad_out, mod_rows, cid):
     rows = F_DEV * TOK_FRAME
     half = lambda dtype: pltpu.VMEM((TOK_FRAME, D), dtype)
     full = lambda dtype: pltpu.VMEM((rows, D), dtype)
@@ -787,6 +917,7 @@
             jax.ShapeDtypeStruct((8, D), F32),
         ),
         [
+            pltpu.VMEM((HEADS * HEAD, D), BF16),
             pltpu.VMEM((HEADS, PACK, LANES), BF16),
             half(BF16), half(F32), half(F32), half(F32), pltpu.VMEM((TOK_FRAME, 1), F32),
             full(BF16), full(BF16), full(BF16), full(F32), full(BF16),
@@ -795,12 +926,12 @@
             pltpu.VMEM((HD, D), F32), pltpu.VMEM((HD, D), BF16), pltpu.VMEM((HD, D), BF16),
             DMA((8,)), DMA((8,)), DMA((8,)), DMA((8,)), DMA((1,)), DMA((1,)),
             DMA((2, TILES)), DMA((2, TILES)), DMA((2, TILES)), DMA((2, TILES)),
-            DMA((8,)), DMA((8,)), DMA, DMA, DMA, DMA,
+            DMA((8,)), DMA((8,)), DMA, DMA, DMA, DMA, DMA((2,)), DMA((2,)),
         ],
         [VM] * 6,
         cid,
         name="middle_part",
-    )(o_mine, wo, wb, tokens, grad_out, mod_rows)
+    )(o_mine, wo_across, wb, tokens, grad_out, mod_rows)
 
 
 def tail_kernel(
@@ -1198,22 +1329,6 @@
     )(meta, oq, ob, cond_rows, dmod, master, one, two, average)
 
 
-def by_frame(rows):
-    return rows.reshape(F_DEV, TOK_FRAME, rows.shape[1])
-
-
-def frame_affine(rows, factor, offset_rows):
-    return (by_frame(rows) * (1.0 + factor)[:, None, :] + offset_rows[:, None, :]).reshape(
-        rows.shape
-    )
-
-
-def pack_heads(rows):
-    return rows.reshape(F_DEV, TOK_FRAME, ZN, HEAD).transpose(2, 1, 0, 3).reshape(
-        ZN, TOK_FRAME, F_DEV * HEAD
-    )
-
-
 def local(
     tokens,
     grad_out,
@@ -1229,7 +1344,6 @@
     plan = Plan(lax.axis_size("seq"))
     s = lax.axis_index("seq")
     t = lax.axis_index("tp")
-    rows = F_DEV * TOK_FRAME
     flat = lambda x: x.reshape(-1, LANES)
 
     effective = noise_level * (1 - context_mask)
@@ -1239,34 +1353,14 @@
     condition = jax.nn.silu(mm(one_hot, level_table)).astype(BF16)
     cond_units = condition.reshape(plan.frames, plan.nm, plan.um).transpose(1, 0, 2)
 
-    wq, wb, mod_blocks, wo = gather_weights(plan, flat(master), cond_units, 0)
-    modulation = (
-        mod_blocks.reshape(TP, F_DEV, MT).transpose(1, 0, 2).reshape(F_DEV, TP * MT)
+    wq, wb, mod_rows, first_in, q_mine, kv_all = head_part(
+        plan, flat(master), cond_units, tokens, 0
     )
-    mod_rows = modulation.reshape(F_DEV * 6, D)
-    shift_one, scale_one = modulation[:, :D], modulation[:, D : 2 * D]
-
-    inputs = tokens.astype(F32)
-    normed_one, inverse_one = normalize(inputs)
-    first_in = frame_affine(normed_one, scale_one, shift_one).astype(BF16)
-    projected = mm(first_in, wq).astype(BF16)
-    kv = jnp.stack(
-        [
-            jnp.concatenate(
-                [
-                    projected[:, HD + h * HEAD : HD + (h + 1) * HEAD],
-                    projected[:, 2 * HD + h * HEAD : 2 * HD + (h + 1) * HEAD],
-                ],
-                axis=1,
-            )
-            for h in range(ZN)
-        ]
-    )
-    q_mine, kv_all = exchange_qkv(plan, pack_heads(projected[:, :HD]), kv, 1)
+    wo_across = lax.ppermute(wb[:HD], "tp", [(i, (i + 2) % TP) for i in range(TP)])
     meta = jnp.concatenate([frame_clip, lax.rem(s, plan.r)[None]]).astype(jnp.int32)
     o_mine, o_rows, lse = attend(plan, meta, q_mine, kv_all)
     result, grads_b, do_mine, middle_grad, mod_four = middle_part(
-        plan, o_mine, wo.reshape(HEADS * HEAD, D), wb, tokens, grad_out, mod_rows, 2
+        plan, o_mine, wo_across, wb, tokens, grad_out, mod_rows, 2
     )
     dq_mine, dkv_all = attend_back(plan, meta, q_mine, kv_all, do_mine, o_rows, lse)
     input_grad, own_q, own_b, mod_all = tail_part(

time: 453 us -> 424 us (0.936)
  Pallas kernels: 435 us -> 412 us
  other arithmetic: 6.94 us -> 1.41 us
    pallas_call x2 -> x1, Pallas kernels: 150 us -> 106 us  [head_part(): call(functools.partial(head_kernel, plan), (jax.ShapeDtypeStruct((D, QKV)...]
    pallas_call x1, Pallas kernels: 82.9 us -> 103 us  [middle_part(): call(functools.partial(middle_kernel, plan), (jax.ShapeDtypeStruct((rows,...]
  transfers between devices with their start and end apart: 0 -> 1, of which waited for: 0 -> 0; matrix products, arithmetic and copies ran while one was open for 0% -> 0% of each run, Pallas kernels for 0% -> 4%
where the time goes in v4:
time: 424 us
  Pallas kernels  412 us (97%)
  local copies, waits for them, and re-layouts  7.68 us (2%)
    pallas_call x1, Pallas kernels, tail_part(): call(functools.partial(tail_kernel, plan), (jax.ShapeDtypeStruct((rows, D...  152 us
    pallas_call x1, Pallas kernels, head_part(): call(functools.partial(head_kernel, plan), (jax.ShapeDtypeStruct((D, QKV)...  106 us
    pallas_call x1, Pallas kernels, middle_part(): call(functools.partial(middle_kernel, plan), (jax.ShapeDtypeStruct((rows,...  103 us
    pallas_call x1, Pallas kernels, attend_back(): call(functools.partial(attend_back_kernel, plan), (jax.ShapeDtypeStruct((...  20.1 us
    pallas_call x1, Pallas kernels, attend(): call(functools.partial(attend_kernel, plan), (jax.ShapeDtypeStruct((ZN, F...  18.8 us
    pallas_call x1, Pallas kernels, adam(): call(functools.partial(adam_kernel, plan), (shape,) * 4, [], [SM] + [VM]...  12.1 us
  transfers between devices with their start and end apart: 1, of which 0 were waited for; matrix products, arithmetic and copies ran while one was open for 0% of the time, Pallas kernels for 4%

profile of v4, /device:TPU:0, one launch (start us, length us, event | category | flops | bytes accessed | tf_op | source)
XLA Modules:
  0.0 423.6 jit_solution(14227986679730178877)
XLA Ops:
  0.6 0.0 copy-start
  0.6 0.8 subtract_multiply_fusion
  1.5 0.8 copy-done
  2.2 0.5 multiply_convert_fusion
  2.7 0.2 copy.16
  2.9 0.0 copy-start.2
  2.9 0.7 copy.17.cond
  3.6 0.0 copy-start.5
  3.6 106.0 %head_part.1 = (bf16[1024,768]{1,0:T(8,128)(2,1)}, bf16[2304,1024]{1,0:T(8,128)(2,1)}, f32[12,1024]{1,0:T(8,128)}, bf16[768,1024]{1,0:T(8,128)(2,1)}, bf16[4,384...) custom-call(f32[4608,128]{1,0:T(8,128)} %bitcast.17, bf16[8,16,128]{2,1,0:T(8,128)(2,1)} %copy.17.cond, ...), custom_call_target="tpu_custom_call" | custom-call | tf_op jit(solution)/shard_map/head_part/pallas_call | solution.py:495
  109.6 1.1 slice.3
  110.7 0.0 copy-done.2
  110.7 1.6 collective-permute-start
  112.3 0.0 copy-done.5
  112.3 0.6 pad_add_fusion.meta
  112.9 18.8 %attend.1 = (bf16[4,2,192,128]{3,2,1,0:T(8,128)(2,1)}, f32[8,64,384]{2,1,0:T(8,128)}, f32[8,1,384]{2,1,0:T(1,128)}) custom-call(s32[17]{0:T(128)} %pad_add_fusion.meta, bf16[4,384,128]{2,1,0:T(8,128)(2,1)} %get-tuple-element.30.q, bf16[8,768,128]{2,1,0:T(8,128)(2,1)} %get-tuple-element.31.kv), custom_call_target="tpu_custom_call" | custom-call | flops 20000000000 | bytes 60000000 | tf_op jit(solution)/shard_map/attend/pallas_call | solution.py:574
  131.6 0.0 collective-permute-done.wo_across
  131.6 0.0 copy-start.4
  131.6 0.8 copy-done.4
  132.4 103.1 %middle_part.1 = (bf16[768,1024]{1,0:T(8,128)(2,1)}, bf16[2304,1024]{1,0:T(8,128)(2,1)}, bf16[4,2,192,128]{3,2,1,0:T(8,128)(2,1)}, f32[384,1024]{1,0:T(8,128)}, f32[8,1024]{1,0:T(8,128)}) custom-call(bf16[4,2,192,128]{3,2,1,0:T(8,128)(2,1)} %get-tuple-element.32.o_mine, bf16[256,1024]{1,0:T(8,128)(2,1)} %copy-done.4, ...), custom_call_target="tpu_custom_call" | custom-call | tf_op jit(solution)/shard_map/middle_part/pallas_call | solution.py:910
  235.5 20.1 %attend_back.1 = (bf16[4,384,128]{2,1,0:T(8,128)(2,1)}, bf16[8,768,128]{2,1,0:T(8,128)(2,1)}) custom-call(s32[17]{0:T(128)} %pad_add_fusion.meta, bf16[4,384,128]{2,1,0:T(8,128)(2,1)} %get-tuple-element.30.q, bf16[8,768,128]{2,1,0:T(8,128)(2,1)} %get-tuple-element.31.kv, bf16[4,2,192,128]{3,2,1,0:T(8,128)(2,1)} %get-tuple-element.36.do, ...), custom_call_target="tpu_custom_call" | custom-call | tf_op jit(solution)/shard_map/attend_back/pallas_call | solution.py:633
  255.6 151.8 %tail_part.1 = (f32[768,1024]{1,0:T(8,128)}, f32[3,256,768]{2,1,0:T(8,128)}, f32[3,192,1024]{2,1,0:T(8,128)}, f32[8,2,16,128]{3,2,1,0:T(8,128)}) custom-call(bf16[4,384,128]{2,1,0:T(8,128)(2,1)} %get-tuple-element.39.dq, bf16[8,768,128]{2,1,0:T(8,128)(2,1)} %get-tuple-element.40.dkv, bf16[768,1024]{1,0:T(8,128)(2,1)} %get-tuple-element.41.first_in, ...), custom_call_target="tpu_custom_call" | custom-call | tf_op jit(solution)/shard_map/tail_part/pallas_call | solution.py:1243
  407.3 0.0 copy-start.3
  407.4 12.1 %adam.1 = (f32[4608,128]{1,0:T(8,128)}, f32[4608,128]{1,0:T(8,128)}, f32[4608,128]{1,0:T(8,128)}, f32[4608,128]{1,0:T(8,128)}) custom-call(s32[1]{0:T(128)} %bitcast.4.meta, f32[3,256,768]{2,1,0:T(8,128)} %get-tuple-element.47.oq, f32[3,192,1024]{2,1,0:T(8,128)} %get-tuple-element.48.ob, bf16[8,128,16]{2,1,0:T(8,128)(2,1)} %bitcast.20, f32[256,128]{1,0:T(8,128)} %bitcast.24, ...), custom_call_target="tpu_custom_call" | custom-call | tf_op jit(solution)/shard_map/adam/pallas_call | solution.py:1323
  419.5 0.0 copy-start.1
  419.5 0.0 copy-done.3
  419.5 1.1 copy.20
  420.6 1.3 copy-done.1
  421.9 1.7 copy.21
Async XLA Ops:
  0.6 1.6 copy-start
  2.9 107.8 %copy-start.2 = (bf16[16,1024]{0,1:T(8,128)(2,1)}, bf16[16,1024]{0,1:T(8,128)(2,1)S(1)}, u32[]{:S(2)}) copy-start(bf16[16,1024]{0,1:T(8,128)(2,1)S(1)} %copy.16) | copy-start | bytes 98308
  3.6 108.6 %copy-start.5 = (s32[16]{0:T(128)S(1)}, s32[16]{0:T(128)}, u32[]{:S(2)}) copy-start(s32[16]{0:T(128)} %param.14) | copy-start | bytes 196
  110.7 21.0 %collective-permute-start = (bf16[256,1024]{1,0:T(8,128)(2,1)S(1)}, bf16[256,1024]{1,0:T(8,128)(2,1)S(1)}, u32[]{:S(2)}, u32[]{:S(2)}) collective-permute-start(bf16[256,1024]{1,0:T(8,128)(2,1)S(1)} %slice.3), channel_id=1, source_target_pairs={{0,2},{1,3},{2,0},{3,1},{4,6},{5,7},{6,4},{7,5},{8,10},{9,11},{10,... | collective-permute-start | bytes 1572872 | tf_op jit(solution)/shard_map/ppermute | solution.py:1359
  131.6 0.8 copy-start.4
  407.3 12.1 %copy-start.3 = (bf16[768,1024]{1,0:T(8,128)(2,1)S(1)}, bf16[768,1024]{1,0:T(8,128)(2,1)}, u32[]{:S(2)}) copy-start(bf16[768,1024]{1,0:T(8,128)(2,1)} %get-tuple-element.60) | copy-start | bytes 4718596
  419.5 2.5 copy-start.1

commit v5 on v4

--- a/solution.py
+++ b/solution.py
@@ -39,6 +39,7 @@
 MESH = pl.DeviceIdType.MESH
 VM = pl.BlockSpec(memory_space=pltpu.VMEM)
 SM = pl.BlockSpec(memory_space=pltpu.SMEM)
+ANY = pl.BlockSpec(memory_space=pl.ANY)
 DMA = pltpu.SemaphoreType.DMA
 F32 = jnp.float32
 BF16 = jnp.bfloat16
@@ -96,8 +97,26 @@
         self.nb = self.nq + BROWS // self.ub
         self.nm = D // self.um
         self.first_mod = self.nb // 3
+        self.half = (self.nq + self.nb) // 2
         self.flat_rows = self.unit // LANES
         self.frames = seq_count * F_DEV
+        self.late = list(range(self.nq, self.half))
+        self.early = list(range(self.half, self.nb))
+        self.outs = self.late[: -(-HD // self.ub)]
+        self.sided = self.late[len(self.outs) :]
+        self.rank, self.ranks = self.ranked(self.early)
+        self.late_rank, self.late_ranks = self.ranked(self.sided)
+
+    def ranked(self, units):
+        seen, rank = {}, {}
+        for k in units:
+            column = self.home(k)[1]
+            rank[k] = seen.get(column, 0)
+            seen[column] = rank[k] + 1
+        return rank, max(seen.values())
+
+    def home(self, k):
+        return (k // 3) // self.r, (k // 3) % self.r
 
 
 def place(plan):
@@ -144,7 +163,7 @@
     return wb.at[pl.ds(pl.multiple_of((k - plan.nq) * plan.ub, plan.ub), plan.ub)]
 
 
-def call(kernel, outs, scratch, ins, cid=None, cost=None, name=None):
+def call(kernel, outs, scratch, ins, cid=None, cost=None, name=None, out_specs=None):
     params = dict(vmem_limit_bytes=VMEM_LIMIT)
     if cid is not None:
         params.update(collective_id=cid, has_side_effects=True)
@@ -152,7 +171,7 @@
         kernel,
         out_shape=outs,
         in_specs=ins,
-        out_specs=jax.tree.map(lambda _: VM, outs),
+        out_specs=out_specs or jax.tree.map(lambda _: VM, outs),
         scratch_shapes=scratch,
         compiler_params=pltpu.CompilerParams(**params),
         cost_estimate=cost,
@@ -160,90 +179,11 @@
     )
 
 
-class Travel:
-    def __init__(self, plan, wb, send_sem, recv_sem, low, high):
-        self.plan, self.wb, self.low, self.high = plan, wb, low, high
-        self.send_sem, self.recv_sem = send_sem, recv_sem
-        self.s, self.t, self.z, self.r = place(plan)
-
-    def move(self, k, lu, sem, owner_r, to_s):
-        ref = unit_of(self.plan, k, "b", None, self.wb)
-        return remote(ref, ref, self.send_sem.at[lu, sem], self.recv_sem.at[lu, owner_r], to_s, self.t)
-
-    def spread(self, k, lu, act, up=None, down=None, sides=True):
-        plan, rn = self.plan, self.plan.r
-
-        def go(kind):
-            if up is not None:
-                @pl.when(up)
-                def _():
-                    act(self.move(k, lu, 0, self.r, self.s + rn))
-            if down is not None:
-                @pl.when(down)
-                def _():
-                    act(self.move(k, lu, 1, self.r, self.s - rn))
-            if sides:
-                for d in range(1, rn):
-                    act(self.move(k, lu, 1 + d, self.r, self.z * rn + lax.rem(self.r + d, rn)))
-
-        by_kind(plan, k, go, self.low, self.high)
-
-    def own(self, act, up=True, down=True, sides=True):
-        for i in range(3):
-            self.spread(
-                3 * self.s + i,
-                3 * self.z + i,
-                act,
-                (self.z < ZN - 1) if up else None,
-                (self.z > 0) if down else None,
-                sides,
-            )
-
-    def line(self, d, act, wait=True):
-        for i in range(3):
-            for side in (0, 1):
-                zs = self.z - d if side == 0 else self.z + d
-                k = 3 * (zs * self.plan.r + self.r) + i
-                lu = 3 * zs + i
-
-                @pl.when((zs >= 0) & (zs < ZN))
-                def _():
-                    if wait:
-                        by_kind(
-                            self.plan, k,
-                            lambda kind: self.move(k, lu, 0, self.r, self.s).wait_recv(),
-                            self.low, self.high,
-                        )
-                    if side == 0:
-                        self.spread(k, lu, act, self.z < ZN - 1, None)
-                    else:
-                        self.spread(k, lu, act, None, self.z > 0)
-
-    def from_sides(self):
-        rn = self.plan.r
-        for d in range(1, rn):
-            other = lax.rem(self.r + d, rn)
-            for zs in range(ZN):
-                for i in range(3):
-                    k = 3 * (zs * rn + other) + i
-                    by_kind(
-                        self.plan, k,
-                        lambda kind: self.move(k, 3 * zs + i, 0, other, self.s).wait_recv(),
-                        self.low, self.high,
-                    )
-
-    def close(self):
-        done = lambda copy: copy.wait_send()
-        self.own(done)
-        for d in range(1, ZN):
-            self.line(d, done, wait=False)
-
-
 def head_kernel(
     plan, master, cond, tokens,
-    wq, wb, mods, first_in, q_out, kv_out,
+    wq, w_out, w_side, w_early, own_b, mods, first_in, q_out, kv_out,
     tile, macc, mpart, mrecv, mod, norm, q_send, kv_send,
-    qp_s, qc_s, q_r, b_s, b_r, m_s, m_r, t_s, t_r, as_, ar, ks, kr, xs, xr,
+    qp_s, qc_s, q_r, wo_s, wo_r, ws_s, ws_r, we_s, we_r, loc_s, m_s, m_r, t_s, t_r, as_, ar, ks, kr, xs, xr,
 ):
     s, t, z, r = place(plan)
     n, rn = plan.n, plan.r
@@ -269,14 +209,15 @@
         return r + rn * lax.rem(j + r, 2)
 
     def q_own(act):
-        for i in range(3):
-            k = 3 * s + i
-
-            @pl.when(k < plan.nq)
-            def _():
-                for h in range(2):
-                    for d in range(1, rn):
-                        act(q_copy(k, h, qp_s.at[2 * i + h, d - 1], lax.rem(r + d, rn)))
+        for away in (True, False):
+            for i in range(3):
+                k = 3 * s + i
+
+                @pl.when((k < plan.nq) & ((lax.rem(k, rn) != r) == away))
+                def _():
+                    for h in range(2):
+                        for d in range(1, rn):
+                            act(q_copy(k, h, qp_s.at[2 * i + h, d - 1], lax.rem(r + d, rn)))
 
     def q_line(act, wait):
         for j in range(2):
@@ -300,36 +241,99 @@
                             )
                         )
 
-    travel = Travel(plan, wb, b_s, b_r, plan.nq, plan.nb)
+    def slot(k):
+        if k in plan.outs:
+            at = k - plan.nq
+            return w_out.at[at], wo_s.at[at], wo_r.at[at]
+        if k in plan.sided:
+            at = plan.late_rank[k]
+            return w_side.at[at], ws_s.at[at], ws_r.at[at]
+        return w_early.at[k - plan.half], we_s.at[plan.rank[k]], we_r.at[k - plan.half]
+
+    def along(k, src, act, up):
+        dst, send_sem, recv_sem = slot(k)
+        if up and k < plan.half:
+            @pl.when(z < ZN - 1)
+            def _():
+                act(remote(src, dst, send_sem.at[0], recv_sem, s + rn, t))
+
+        if not up:
+            @pl.when(z > 0)
+            def _():
+                act(remote(src, dst, send_sem.at[1], recv_sem, s - rn, t))
+
+    def beside(k, src, act):
+        if k in plan.sided:
+            return
+        dst, send_sem, recv_sem = slot(k)
+        for d in range(1, rn):
+            act(
+                remote(
+                    src, dst, send_sem.at[1 + d], recv_sem, z * rn + lax.rem(r + d, rn), t
+                )
+            )
+
+    def arrived(k):
+        dst, send_sem, recv_sem = slot(k)
+        remote(own_b.at[0], dst, send_sem.at[0], recv_sem, s, t).wait_recv()
+
+    def keep(k):
+        return pltpu.make_async_copy(own_b.at[k % 3], slot(k)[0], loc_s.at[k % 3])
+
+    def owned(units, act):
+        for k in units:
+            @pl.when(s == k // 3)
+            def _():
+                act(k, own_b.at[k % 3])
+
+    def pass_along(units, d, act, wait):
+        for k in units:
+            zo, ro = plan.home(k)
+            if k < plan.half and zo + d < ZN:
+                @pl.when((r == ro) & (z == zo + d))
+                def _():
+                    if wait:
+                        arrived(k)
+                    along(k, slot(k)[0], act, True)
+                    beside(k, slot(k)[0], act)
+
+            if zo - d >= 0:
+                @pl.when((r == ro) & (z == zo - d))
+                def _():
+                    if wait:
+                        arrived(k)
+                    along(k, slot(k)[0], act, False)
+                    beside(k, slot(k)[0], act)
+
+    units = plan.late + plan.early
+    first_up = [k for k in plan.late if k % 3 == 0 and plan.home(k)[0] > 0]
+    later_up = [k for k in plan.late if k not in first_up]
 
     for i in range(3):
         k = 3 * s + i
         base = i * plan.flat_rows
 
         def fill(kind):
-            if kind == "q":
-                rows, ref, at, cols = plan.uq, wq, k * plan.uq, QKV // LANES
-            else:
-                rows, ref, at, cols = plan.ub, wb, (k - plan.nq) * plan.ub, D // LANES
-            at = pl.multiple_of(at, rows)
+            rows, cols = (plan.uq, QKV // LANES) if kind == "q" else (plan.ub, D // LANES)
+            at = pl.multiple_of(k * plan.uq, plan.uq)
             for j in range(cols):
-                ref[pl.ds(at, rows), j * LANES : (j + 1) * LANES] = master[
-                    pl.ds(base + j, rows, stride=cols), :
-                ].astype(BF16)
+                values = master[pl.ds(base + j, rows, stride=cols), :].astype(BF16)
+                if kind == "q":
+                    wq[pl.ds(at, rows), j * LANES : (j + 1) * LANES] = values
+                else:
+                    own_b[i, :, j * LANES : (j + 1) * LANES] = values
 
         by_kind(plan, k, fill)
 
-        @pl.when(k < plan.nq)
-        def _():
-            for h in range(2):
-                for d in range(1, rn):
-                    q_copy(k, h, qp_s.at[2 * i + h, d - 1], lax.rem(r + d, rn)).start()
+    q_own(start)
 
     @pl.when(z == 0)
     def _():
         q_line(start, True)
 
-    travel.own(start, up=False, sides=False)
+    owned(units, lambda k, src: along(k, src, start, False))
+    owned(first_up, lambda k, src: along(k, src, start, True))
+    owned(units, lambda k, src: keep(k).start())
 
     macc[...] = jnp.zeros_like(macc)
     for i in range(3):
@@ -371,7 +375,10 @@
     def _():
         q_line(start, True)
 
-    travel.own(start, down=False)
+    owned(plan.outs, lambda k, src: along(k, src, start, True))
+    owned([k for k in later_up if k not in plan.outs], lambda k, src: along(k, src, start, True))
+    owned(units, lambda k, src: beside(k, src, start))
+    pass_along(first_up, 1, start, True)
 
     for src in range(fm, n):
         @pl.when(s != src)
@@ -451,14 +458,15 @@
         a_copy(d).start()
     q_out[z] = q_send[z]
 
-    travel.line(1, start)
+    rest = [k for k in units if k not in first_up]
+    pass_along(rest, 1, start, True)
     for d in range(1, ZN):
         zs = lax.rem(z + d, ZN)
         remote(kv_send.at[0], kv_out.at[zs * rn + r], ks.at[0], kr.at[zs], s, t).wait_recv()
         for e in range(1, rn):
             side_copy(zs, e).start()
     for d in range(2, ZN):
-        travel.line(d, start)
+        pass_along(units, d, start, True)
     for d in range(1, ZN):
         zs = lax.rem(z + d, ZN)
         remote(q_send.at[0], q_out.at[zs], as_.at[0], ar.at[zs], s, t).wait_recv()
@@ -466,11 +474,22 @@
         for zs in range(ZN):
             at = zs * rn + lax.rem(r + e, rn)
             remote(kv_out.at[at], kv_out.at[at], xs.at[0, 0], xr.at[at], s, t).wait_recv()
-    travel.from_sides()
+    for k in plan.outs + plan.early:
+        zo, ro = plan.home(k)
+
+        @pl.when((r != ro) & ((z <= zo) | (k in plan.outs)))
+        def _():
+            arrived(k)
+
 
     q_own(done)
     q_line(done, False)
-    travel.close()
+    owned(units, lambda k, src: along(k, src, done, False))
+    owned(plan.late, lambda k, src: along(k, src, done, True))
+    owned(units, lambda k, src: beside(k, src, done))
+    owned(units, lambda k, src: keep(k).wait())
+    for d in range(1, ZN):
+        pass_along(units, d, done, False)
 
     @pl.when(s >= fm)
     def _():
@@ -496,7 +515,10 @@
         functools.partial(head_kernel, plan),
         (
             jax.ShapeDtypeStruct((D, QKV), BF16),
-            jax.ShapeDtypeStruct((BROWS, D), BF16),
+            jax.ShapeDtypeStruct((len(plan.outs), plan.ub, D), BF16),
+            jax.ShapeDtypeStruct((plan.late_ranks, plan.ub, D), BF16),
+            jax.ShapeDtypeStruct((len(plan.early), plan.ub, D), BF16),
+            jax.ShapeDtypeStruct((3, plan.ub, D), BF16),
             jax.ShapeDtypeStruct((F_DEV * 6, D), F32),
             jax.ShapeDtypeStruct((rows, D), BF16),
             jax.ShapeDtypeStruct((ZN, TOK_FRAME, LANES), BF16),
@@ -512,12 +534,15 @@
             pltpu.VMEM((ZN, TOK_FRAME, LANES), BF16),
             pltpu.VMEM((ZN, rows, LANES), BF16),
             DMA((6, rn - 1)), DMA((4, rn)), DMA((2 * plan.nq,)),
-            DMA((3 * ZN, rn + 1)), DMA((3 * ZN, rn)),
+            DMA((len(plan.outs), rn + 1)), DMA((len(plan.outs),)),
+            DMA((plan.late_ranks, 2)), DMA((plan.late_ranks,)),
+            DMA((plan.ranks, rn + 1)), DMA((len(plan.early),)), DMA((3,)),
             DMA((n - 1,)), DMA((mods,)), DMA((TP - 1,)), DMA((TP,)),
             DMA((ZN - 1,)), DMA((ZN,)), DMA((ZN - 1,)), DMA((ZN,)), DMA((ZN, rn - 1)), DMA((n,)),
         ],
         [VM] * 3,
         cid,
+        out_specs=(VM, ANY, ANY, ANY, VM, VM, VM, VM, VM),
         name="head_part",
     )(master, cond_units, tokens)
 
@@ -641,16 +666,17 @@
             pltpu.VMEM((LANES, TOK_FRAME), F32),
         ],
         [SM, VM, VM, VM, VM, VM],
+        cost=pl.CostEstimate(flops=3 * 10**10, bytes_accessed=9 * 10**7, transcendentals=10**7),
         name="attend_back",
     )(meta, q, kv, do, ot, lse)
 
 
 def middle_kernel(
-    plan, o_mine, wo_across, wb, tokens, grad_out, mod,
-    result, gb, do_out, dmid, dmod,
-    wo, oall, attended, attn, mid, norm, inv, sin, hidden, dmlp, dhid, dup,
+    plan, o_mine, wo_across, w_out, w_side, w_beside, w_early, w_below, tokens, grad_out, mod,
+    result, gb, esum, do_out, dmid, dmod,
+    wb, eside, wo, oall, attended, attn, mid, norm, inv, sin, hidden, dmlp, slopes, dup,
     own, csend, crecv, ysend, yrecv, dattn, dsend, dwo, wsend, wrecv,
-    o_s, o_r, f_s, f_r, n_s, n_r, c_s, c_r, y_s, y_r, d_s, d_r, w_s, w_r, e_s, e_r, p_s, p_r,
+    o_s, o_r, f_s, f_r, n_s, n_r, c_s, c_r, y_s, y_r, d_s, d_r, w_s, w_r, e_s, e_r, p_s, p_r, l_s, u_s, u_r, g_s, g_r,
 ):
     s, t, z, r = place(plan)
     rn = plan.r
@@ -668,7 +694,80 @@
     greet(
         [(partner(d, e)[0] * rn + r, 2 * y + partner(d, e)[1]) for d, e in pairs]
         + [(s, across)]
+        + [(z * rn + lax.rem(r + d, rn), t) for d in range(1, rn)]
     )
+
+    def home(k):
+        return (k // 3) // rn, (k // 3) % rn, k - plan.half
+
+    def w_rows(ref, k):
+        return ref.at[pl.ds((k - plan.nq) * plan.ub, plan.ub)]
+
+    def late_loads(act):
+        for k in plan.late:
+            sem = l_s.at[k - plan.nq]
+            if k in plan.outs:
+                act(pltpu.make_async_copy(w_out.at[k - plan.nq], w_rows(wb, k), sem))
+            else:
+                zo, ro = plan.home(k)
+                rank = plan.late_rank[k]
+
+                @pl.when(r == ro)
+                def _():
+                    act(pltpu.make_async_copy(w_side.at[rank], w_rows(wb, k), sem))
+
+                @pl.when(r != ro)
+                def _():
+                    d = lax.rem(r - ro + rn, rn)
+                    act(pltpu.make_async_copy(w_beside.at[d - 1, rank], w_rows(wb, k), sem))
+
+    def loads(act):
+        for k in plan.early:
+            zo, ro, at = home(k)
+
+            @pl.when(z <= zo)
+            def _():
+                act(pltpu.make_async_copy(w_early.at[at], w_rows(wb, k), l_s.at[len(plan.late) + at]))
+
+            @pl.when((z == zo + 1) & (r == ro))
+            def _():
+                act(
+                    pltpu.make_async_copy(
+                        w_below.at[k % 3], w_rows(wb, k), l_s.at[len(plan.late) + at]
+                    )
+                )
+
+    def rise(k, src, act):
+        zo, ro, at = home(k)
+
+        @pl.when(z < ZN - 1)
+        def _():
+            act(remote(src, w_rows(wb, k), u_s.at[at, 0], u_r.at[at], s + rn, t))
+
+        for d in range(1, rn):
+            act(
+                remote(
+                    src, w_rows(wb, k), u_s.at[at, d], u_r.at[at],
+                    z * rn + lax.rem(r + d, rn), t,
+                )
+            )
+
+    def risen(k):
+        remote(w_below.at[0], w_rows(wb, k), u_s.at[0, 0], u_r.at[k - plan.half], s, t).wait_recv()
+
+    def rises(act, first, wait):
+        for k in plan.early:
+            zo, ro, at = home(k)
+            if first:
+                @pl.when((z == zo + 1) & (r == ro))
+                def _():
+                    rise(k, w_below.at[k % 3], act)
+            else:
+                @pl.when((z > zo + 1) & (r == ro))
+                def _():
+                    if wait:
+                        risen(k)
+                    rise(k, w_rows(wb, k), act)
 
     def o_copy(d, e):
         zd, cd = partner(d, e)
@@ -687,6 +786,11 @@
 
     for d, e in pairs:
         o_copy(d, e).start()
+    start = lambda copy: copy.start()
+    rises(start, True, False)
+    late_loads(start)
+    loads(start)
+    late_loads(lambda copy: copy.wait())
     wo[pl.ds(pl.multiple_of(t * HD, HD), HD), :] = wb[:HD, :]
     p_copy(0, t).start()
     wo[pl.ds(pl.multiple_of(across * HD, HD), HD), :] = wo_across[...]
@@ -705,11 +809,6 @@
 
     for f in range(F_DEV):
         d_mlp(f)
-
-    def d_hidden(at):
-        dhid[:, pl.ds(at, TILE)] = mm_nt(dmlp[...], wb[pl.ds(HD + FT + at, TILE), :])
-
-    loop(FT, TILE, d_hidden)
 
     for d, e in pairs:
         zd, cd = partner(d, e)
@@ -733,6 +832,7 @@
         attn[:, pl.ds(at, TILE)] = mm(attended[...], wo[:, pl.ds(at, TILE)])
 
     loop(D, TILE, attn_tile)
+    rises(start, False, True)
 
     row = lambda part: mod[pl.ds(c * 6 + part, 1), :]
 
@@ -752,6 +852,13 @@
         return remote(ref, ref, n_s.at[0], n_r.at[0], s, sib)
 
     n_copy(mine).start()
+    loads(lambda copy: copy.wait())
+    for k in plan.early:
+        zo, ro, at = home(k)
+
+        @pl.when((z > zo) & (r != ro))
+        def _():
+            risen(k)
 
     def feed(base):
         rows = pl.ds(base, TOK_FRAME)
@@ -764,14 +871,23 @@
             th = jnp.tanh(inner)
             half = 0.5 * (1.0 + th)
             hidden[rows, cols] = (u * half).astype(BF16)
-            slope = half + 0.5 * u * (1.0 - th * th) * (GELU_A * (1.0 + 3.0 * GELU_B * square))
-            dup[rows, cols] = (dhid[rows, cols] * slope).astype(BF16)
+            slopes[rows, cols] = half + 0.5 * u * (1.0 - th * th) * (
+                GELU_A * (1.0 + 3.0 * GELU_B * square)
+            )
 
         loop(FT, TILE, tile)
 
     feed(mine)
     n_copy(theirs).wait_recv()
     feed(theirs)
+
+    def d_up(at):
+        cols = pl.ds(at, TILE)
+        dup[:, cols] = (mm_nt(dmlp[...], wb[pl.ds(HD + FT + at, TILE), :]) * slopes[:, cols]).astype(
+            BF16
+        )
+
+    loop(FT, TILE, d_up)
 
     def c_copy(w, n):
         return remote(csend.at[w, n], crecv.at[w, n], c_s.at[w, n], c_r.at[w, n], s, sib)
@@ -807,6 +923,24 @@
 
     loop(FT, TILE, down_grad)
     loop(D, TILE, up_grad)
+
+    def early_grad(k, d):
+        zo, ro, at = home(k)
+        slot = lax.rem(ro - r + rn, rn) - 1 if d is None else d - 1
+        return remote(
+            w_rows(gb, k), eside.at[slot, plan.rank[k]], g_s.at[at], g_r.at[slot, plan.rank[k]],
+            z * rn + ro, t,
+        )
+
+    def early_grads(act):
+        for k in plan.early:
+            zo, ro, at = home(k)
+
+            @pl.when(r != ro)
+            def _():
+                act(early_grad(k, None))
+
+    early_grads(start)
 
     dm = dmod
     dm[...] = jnp.zeros_like(dm)
@@ -885,7 +1019,29 @@
         remote(
             dsend.at[0], do_out.at[zd, cd], d_s.at[0], d_r.at[2 * zd + cd], s, t
         ).wait_recv()
+    for k in plan.early:
+        zo, ro, at = home(k)
+
+        @pl.when(r == ro)
+        def _():
+            rank = plan.rank[k]
+            for d in range(1, rn):
+                early_grad(k, d).wait_recv()
+
+            def body(at):
+                rows = pl.ds(at, 16)
+                total = gb[pl.ds((k - plan.nq) * plan.ub + at, 16), :].astype(F32)
+                for d in range(1, rn):
+                    total = total + eside[d - 1, rank, rows, :].astype(F32)
+                esum[rank, rows, :] = total.astype(BF16)
+
+            loop(plan.ub, 16, body)
+
     e_copy(theirs).wait_recv()
+    done = lambda copy: copy.wait_send()
+    early_grads(done)
+    rises(done, True, False)
+    rises(done, False, False)
     for d, e in pairs:
         o_copy(d, e).wait_send()
         d_copy(d, e).wait_send()
@@ -902,7 +1058,8 @@
     e_copy(mine).wait_send()
 
 
-def middle_part(plan, o_mine, wo_across, wb, tokens, grad_out, mod_rows, cid):
+def middle_part(plan, o_mine, wo_across, weights, tokens, grad_out, mod_rows, cid):
+    rn, count = plan.r, len(plan.early)
     rows = F_DEV * TOK_FRAME
     half = lambda dtype: pltpu.VMEM((TOK_FRAME, D), dtype)
     full = lambda dtype: pltpu.VMEM((rows, D), dtype)
@@ -912,11 +1069,14 @@
         (
             jax.ShapeDtypeStruct((rows, D), BF16),
             jax.ShapeDtypeStruct((BROWS, D), BF16),
+            jax.ShapeDtypeStruct((plan.ranks, plan.ub, D), BF16),
             jax.ShapeDtypeStruct((ZN, F_DEV, PACK, LANES), BF16),
             jax.ShapeDtypeStruct((TOK_FRAME, D), F32),
             jax.ShapeDtypeStruct((8, D), F32),
         ),
         [
+            pltpu.VMEM((BROWS, D), BF16),
+            pltpu.VMEM((rn - 1, plan.ranks, plan.ub, D), BF16),
             pltpu.VMEM((HEADS * HEAD, D), BF16),
             pltpu.VMEM((HEADS, PACK, LANES), BF16),
             half(BF16), half(F32), half(F32), half(F32), pltpu.VMEM((TOK_FRAME, 1), F32),
@@ -927,19 +1087,21 @@
             DMA((8,)), DMA((8,)), DMA((8,)), DMA((8,)), DMA((1,)), DMA((1,)),
             DMA((2, TILES)), DMA((2, TILES)), DMA((2, TILES)), DMA((2, TILES)),
             DMA((8,)), DMA((8,)), DMA, DMA, DMA, DMA, DMA((2,)), DMA((2,)),
+            DMA((len(plan.late) + count,)), DMA((count, rn)), DMA((count,)), DMA((count,)), DMA((rn - 1, plan.ranks)),
         ],
-        [VM] * 6,
+        [VM, VM, ANY, ANY, ANY, ANY, ANY, VM, VM, VM],
         cid,
         name="middle_part",
-    )(o_mine, wo_across, wb, tokens, grad_out, mod_rows)
+    )(o_mine, wo_across, *weights, tokens, grad_out, mod_rows)
 
 
 def tail_kernel(
-    plan, dq, dkv, first_in, wq, tokens, dmid, mod, dm4, gb,
+    plan, dq, dkv, first_in, wq, tokens, dmid, mod, dm4, gb, esum, e_above, e_below,
     igrad, oq, ob, dall,
     stage, side, q_in, kv_in, dqkv, gq, own, csend, crecv, ysend, yrecv, dm, dm3, dboth,
-    rq, rb, cq, cb,
+    rb, cb, estage, ebuf, qside, qpeer, qchain, qstage,
     q_s, q_r, k_s, k_r, x_s, x_r, c_s, c_r, y_s, y_r, e_s, e_r, h_s, h_r, m_s, m_r, r_s, r_r, t_s, t_r,
+    es_s, es_r, qo_s, qs_r, qp_r, qc_s, qc_r,
 ):
     s, t, z, r = place(plan)
     n, rn = plan.n, plan.r
@@ -986,134 +1148,251 @@
             stage[d] = total.astype(BF16)
             kv_copy(d).start()
 
-    def owner(j):
-        a = 2 - lax.div(z, 2)
-        b = 2 * lax.div(ZN - 1 - z, ZN - 1)
-        return lax.rem(a * j + b, 3)
-
-    def grad_copy(zo, i, d, kind):
-        other = lax.rem(r + d, rn)
-        k = 3 * (zo * rn + other) + i
-        lu = 3 * zo + i
-        buf = rq if kind == "q" else rb
-        return remote(
-            unit_of(plan, k, kind, gq, gb), buf.at[d - 1, lu], r_s.at[lu, d - 1],
-            r_r.at[lu, d - 1], z * rn + other, t,
-        )
-
-    def grad_sides(owners, low, high, act):
-        for zo in owners:
+    def b_rows(k):
+        return gb.at[pl.ds(pl.multiple_of((k - plan.nq) * plan.ub, plan.ub), plan.ub)]
+
+    def late(k, act):
+        by_kind(plan, k, lambda kind: act(), plan.nq, plan.half)
+
+    def late_sides(act):
+        for zo in range(2):
             for i in range(3):
                 for d in range(1, rn):
-                    k = 3 * (zo * rn + lax.rem(r + d, rn)) + i
-                    by_kind(plan, k, lambda kind: act(grad_copy(zo, i, d, kind)), low, high)
-
-    def chain_copy(lu, kind, below, to):
-        src = (rq if kind == "q" else rb).at[0, lu]
-        dst = cq.at[lu] if kind == "q" else cb.at[below, lu]
-        return remote(src, dst, t_s.at[lu], t_r.at[lu, below], to, t)
-
-    def grad_chain(owners, low, high):
-        for zo in owners:
+                    other = lax.rem(r + d, rn)
+                    k = 3 * (zo * rn + other) + i
+                    lu = 3 * zo + i
+                    late(
+                        k,
+                        lambda: act(
+                            remote(
+                                b_rows(k), rb.at[d - 1, lu], r_s.at[lu, d - 1], r_r.at[lu, d - 1],
+                                z * rn + other, t,
+                            )
+                        ),
+                    )
+
+    def late_copy(lu, below, to):
+        return remote(rb.at[0, lu], cb.at[below, lu], t_s.at[lu], t_r.at[lu, below], to, t)
+
+    def late_step(zo, i, here_z, above, below, final):
+        k = 3 * (zo * rn + r) + i
+        lu = 3 * zo + i
+
+        def act():
+            unit = b_rows(k)
+            for d in range(1, rn):
+                remote(
+                    unit, rb.at[d - 1, lu], r_s.at[lu, d - 1], r_r.at[lu, d - 1], s, t
+                ).wait_recv()
+            if above:
+                late_copy(lu, 0, s).wait_recv()
+            if below:
+                late_copy(lu, 1, s).wait_recv()
+
+            def body(at):
+                rows = pl.ds(at, 16)
+                total = unit[rows, :].astype(F32)
+                for d in range(1, rn):
+                    total = total + rb[d - 1, lu, rows, :].astype(F32)
+                if above:
+                    total = total + cb[0, lu, rows, :].astype(F32)
+                if below:
+                    total = total + cb[1, lu, rows, :].astype(F32)
+                if final:
+                    ob[i, rows, :] = total
+                else:
+                    rb[0, lu, rows, :] = total.astype(BF16)
+
+            loop(plan.ub, 16, body)
+            if not final:
+                late_copy(lu, 0 if here_z > zo else 1, s - rn if here_z > zo else s + rn).start()
+
+        @pl.when(z == here_z)
+        def _():
+            late(k, act)
+
+    def late_close():
+        late_sides(lambda copy: copy.wait_send())
+        for zo in range(2):
             for i in range(3):
-                k = 3 * (zo * rn + r) + i
-                lu = 3 * zo + i
-
-                def step(kind):
-                    part = rq if kind == "q" else rb
-                    out = oq if kind == "q" else ob
-                    unit = unit_of(plan, k, kind, gq, gb)
-                    rows = plan.uq if kind == "q" else plan.ub
+                @pl.when(z != zo)
+                def _():
+                    late(
+                        3 * (zo * rn + r) + i, lambda: late_copy(3 * zo + i, 0, s).wait_send()
+                    )
+
+    def early_units(act):
+        for k in plan.early:
+            zo, ro, rank = (k // 3) // rn, (k // 3) % rn, plan.rank[k]
+
+            @pl.when(r == ro)
+            def _():
+                act(k, zo, rank)
+
+    def early_copy(rank, to):
+        return remote(estage.at[rank], ebuf.at[rank], es_s.at[rank], es_r.at[rank], to, t)
+
+    def early_send(k, zo, rank):
+        source, came, step = (1, e_below, rn) if zo == 2 else (2, e_above, -rn)
+
+        @pl.when(z == source)
+        def _():
+            def body(at):
+                rows = pl.ds(at, 16)
+                estage[rank, rows, :] = (
+                    esum[rank, rows, :].astype(F32) + came[rank, rows, :].astype(F32)
+                ).astype(BF16)
+
+            loop(plan.ub, 16, body)
+            early_copy(rank, s + step).start()
+
+    def early_final(k, zo, rank):
+        came = e_above if zo == 2 else e_below
+
+        @pl.when(z == zo)
+        def _():
+            early_copy(rank, s).wait_recv()
+
+            def body(at):
+                rows = pl.ds(at, 16)
+                ob[k % 3, rows, :] = (
+                    esum[rank, rows, :].astype(F32)
+                    + came[rank, rows, :].astype(F32)
+                    + ebuf[rank, rows, :].astype(F32)
+                )
+
+            loop(plan.ub, 16, body)
+
+    def early_done(k, zo, rank):
+        @pl.when(z == 3 - zo)
+        def _():
+            early_copy(rank, s).wait_send()
+
+    hq = plan.uq // 2
+
+    def q_rows(k, h):
+        return gq.at[pl.ds(pl.multiple_of(k * plan.uq + h * hq, hq), hq)]
+
+    def q_sides(k, act):
+        tc, ro, j = k % rn, k // 3, k // rn
+        for h in range(2):
+            @pl.when((z > 0) & (r != tc))
+            def _():
+                slot = lax.rem(tc - r + rn, rn) - 1
+                act(
+                    remote(
+                        q_rows(k, h), qside.at[slot, 2 * j + h], qo_s.at[2 * k + h],
+                        qs_r.at[slot, 2 * j + h], z * rn + tc, t,
+                    )
+                )
+
+            @pl.when((z == 0) & (r != ro) & (r != tc))
+            def _():
+                slot = lax.rem(ro - r + rn, rn) - 1
+                act(
+                    remote(
+                        q_rows(k, h), qpeer.at[slot, 2 * (k % 3) + h], qo_s.at[2 * k + h],
+                        qp_r.at[slot, 2 * (k % 3) + h], ro, t,
+                    )
+                )
+
+    def q_down(at, to):
+        return remote(qstage.at[at], qchain.at[at], qc_s.at[at], qc_r.at[at], to, t)
+
+    def q_chain(top):
+        for j in range(2):
+            k = r + rn * j
+            for h in range(2):
+                at = 2 * j + h
+
+                @pl.when(z == ZN - 1 if top else (z > 0) & (z < ZN - 1))
+                def _():
                     for d in range(1, rn):
                         remote(
-                            unit, part.at[d - 1, lu], r_s.at[lu, d - 1], r_r.at[lu, d - 1], s, t
+                            q_rows(k, h), qside.at[d - 1, at], qo_s.at[0], qs_r.at[d - 1, at], s, t
                         ).wait_recv()
-                    above = (zo <= z) & (z < ZN - 1)
-                    below = (zo >= z) & (z > 0)
-
-                    @pl.when(above)
-                    def _():
-                        chain_copy(lu, kind, 0, s).wait_recv()
-
-                    if kind == "b":
-                        @pl.when(below)
-                        def _():
-                            chain_copy(lu, kind, 1, s).wait_recv()
-
-                    def here(at):
-                        total = unit[pl.ds(at, 16), :].astype(F32)
+                    if not top:
+                        q_down(at, s).wait_recv()
+                    unit = q_rows(k, h)
+
+                    def body(row):
+                        rows = pl.ds(row, 16)
+                        total = unit[rows, :].astype(F32)
                         for d in range(1, rn):
-                            total = total + part[d - 1, lu, pl.ds(at, 16), :].astype(F32)
-                        return total
-
-                    def from_chain(at, below):
-                        ref = cq.at[lu] if kind == "q" else cb.at[below, lu]
-                        return ref[pl.ds(at, 16), :].astype(F32)
-
-                    @pl.when(zo != z)
-                    def _():
-                        @pl.when((zo < z) & (z == ZN - 1) | (zo > z) & (z == 0))
-                        def _():
-                            def body(at):
-                                part[0, lu, pl.ds(at, 16), :] = here(at).astype(BF16)
-
-                            loop(rows, 16, body)
-
-                        @pl.when((zo < z) & (z < ZN - 1))
-                        def _():
-                            def body(at):
-                                part[0, lu, pl.ds(at, 16), :] = (here(at) + from_chain(at, 0)).astype(BF16)
-
-                            loop(rows, 16, body)
-
-                        if kind == "b":
-                            @pl.when((zo > z) & (z > 0))
-                            def _():
-                                def body(at):
-                                    part[0, lu, pl.ds(at, 16), :] = (here(at) + from_chain(at, 1)).astype(BF16)
-
-                                loop(rows, 16, body)
-
-                    @pl.when(zo < z)
-                    def _():
-                        chain_copy(lu, kind, 0, s - rn).start()
-
-                    if kind == "b":
-                        @pl.when(zo > z)
-                        def _():
-                            chain_copy(lu, kind, 1, s + rn).start()
-
-                    @pl.when((zo == z) & (z == 0))
-                    def _():
-                        def body(at):
-                            out[i, pl.ds(at, 16), :] = here(at) + from_chain(at, 0)
-
-                        loop(rows, 16, body)
-
-                    if kind == "b":
-                        @pl.when((zo == z) & (z > 0))
-                        def _():
-                            def body(at):
-                                out[i, pl.ds(at, 16), :] = here(at) + from_chain(at, 0) + from_chain(at, 1)
-
-                            loop(rows, 16, body)
-
-                by_kind(plan, k, step, low, high)
-
-    def grad_close(owners, low, high):
-        grad_sides(owners, low, high, lambda copy: copy.wait_send())
-        for zo in owners:
-            for i in range(3):
-                def close(kind):
-                    @pl.when(zo != z)
-                    def _():
-                        chain_copy(3 * zo + i, kind, 0, s).wait_send()
-
-                by_kind(plan, 3 * (zo * rn + r) + i, close, low, high)
-
-    every = [owner(j) for j in range(3)]
+                            total = total + qside[d - 1, at, rows, :].astype(F32)
+                        if not top:
+                            total = total + qchain[at, rows, :].astype(F32)
+                        qstage[at, rows, :] = total.astype(BF16)
+
+                    loop(hq, 16, body)
+                    q_down(at, s - rn).start()
+
+    def q_last_copy(k, h):
+        tc, ro, j = k % rn, k // 3, k // rn
+        slot = (ro - tc + rn) % rn - 1
+        return remote(
+            qstage.at[2 * j + h], qpeer.at[slot, 2 * (k % 3) + h], qc_s.at[2 * j + h],
+            qp_r.at[slot, 2 * (k % 3) + h], ro, t,
+        )
+
+    def q_ground(act):
+        for k in range(plan.nq):
+            if k % rn != k // 3:
+                @pl.when((z == 0) & (r == k % rn))
+                def _():
+                    for h in range(2):
+                        act(k, h)
+
+    def q_turn(k, h):
+        at = 2 * (k // rn) + h
+        q_down(at, s).wait_recv()
+        unit = q_rows(k, h)
+
+        def body(row):
+            rows = pl.ds(row, 16)
+            qstage[at, rows, :] = (
+                unit[rows, :].astype(F32) + qchain[at, rows, :].astype(F32)
+            ).astype(BF16)
+
+        loop(hq, 16, body)
+        q_last_copy(k, h).start()
+
+    def q_final():
+        for k in range(plan.nq):
+            @pl.when((z == 0) & (r == k // 3))
+            def _():
+                straight = k % rn == k // 3
+                for h in range(2):
+                    at = 2 * (k // rn) + h
+                    if straight:
+                        q_down(at, s).wait_recv()
+                    for d in range(1, rn):
+                        remote(
+                            q_rows(k, h), qpeer.at[d - 1, 2 * (k % 3) + h], qo_s.at[0],
+                            qp_r.at[d - 1, 2 * (k % 3) + h], s, t,
+                        ).wait_recv()
+                    unit = q_rows(k, h)
+
+                    def body(row):
+                        rows = pl.ds(row, 16)
+                        total = unit[rows, :].astype(F32)
+                        for d in range(1, rn):
+                            total = total + qpeer[d - 1, 2 * (k % 3) + h, rows, :].astype(F32)
+                        if straight:
+                            total = total + qchain[at, rows, :].astype(F32)
+                        oq[k % 3, pl.ds(h * hq + row, 16), :] = total
+
+                    loop(hq, 16, body)
+
     start = lambda copy: copy.start()
-    grad_sides(every, plan.nq, plan.nb, start)
+    done = lambda copy: copy.wait_send()
+    late_sides(start)
+    early_units(early_send)
+    for zo in range(2):
+        for i in range(3):
+            late_step(zo, i, ZN - 1, False, False, False)
+    for i in range(3):
+        late_step(1, i, 0, False, False, False)
 
     for d in range(1, ZN):
         zs = lax.rem(z + d, ZN)
@@ -1132,11 +1411,12 @@
             [a[:, HEAD:], b[:, HEAD:]], axis=1
         )
 
-    def q_grad(at):
-        gq[pl.ds(at, TILE), :] = mm_tn(first_in[:, pl.ds(at, TILE)], dqkv[...]).astype(BF16)
-
-    loop(D, TILE, q_grad)
-    grad_sides([0], 0, plan.nq, start)
+    for m in range(TILES):
+        gq[m * TILE : (m + 1) * TILE, :] = mm_tn(
+            first_in[:, m * TILE : (m + 1) * TILE], dqkv[...]
+        ).astype(BF16)
+        for k in range(m * plan.nq // TILES, (m + 1) * plan.nq // TILES):
+            q_sides(k, start)
 
     def c_copy(w):
         return remote(csend.at[w], crecv.at[w], c_s.at[w], c_r.at[w], s, sib)
@@ -1158,7 +1438,13 @@
             pass_on(w - 1)
     pass_on(TILES - 1)
 
-    grad_chain(every, plan.nq, plan.nb)
+    for here in (2, 1):
+        for zo in range(2):
+            if zo != here:
+                for i in range(3):
+                    late_step(zo, i, here, True, False, False)
+    q_chain(True)
+    q_chain(False)
 
     for w in range(TILES):
         y_copy(w).wait_recv()
@@ -1207,7 +1493,12 @@
         def _():
             m_copy(src).start()
 
-    grad_chain([0], 0, plan.nq)
+    q_ground(q_turn)
+    for i in range(3):
+        late_step(1, i, 1, True, True, True)
+        late_step(0, i, 0, True, False, True)
+    early_units(early_final)
+    q_final()
 
     @pl.when(s >= plan.first_mod)
     def _():
@@ -1222,8 +1513,17 @@
     for d in order:
         for e in range(1, rn):
             side_copy(d, e).wait_send()
-    grad_close(every, plan.nq, plan.nb)
-    grad_close([0], 0, plan.nq)
+    late_close()
+    early_units(early_done)
+    for k in range(plan.nq):
+        q_sides(k, done)
+
+    @pl.when(z > 0)
+    def _():
+        for at in range(4):
+            q_down(at, s).wait_send()
+
+    q_ground(lambda k, h: q_last_copy(k, h).wait_send())
     for w in range(TILES):
         c_copy(w).wait_send()
         y_copy(w).wait_send()
@@ -1235,7 +1535,7 @@
             m_copy(src).wait_send()
 
 
-def tail_part(plan, dq, dkv, first_in, wq, tokens, dmid, mod_rows, dm4, gb, cid):
+def tail_part(plan, dq, dkv, first_in, wq, tokens, dmid, mod_rows, dm4, gb, early, cid):
     n, rn = plan.n, plan.r
     rows = F_DEV * TOK_FRAME
     tiles = pltpu.VMEM((TILES, TOK_FRAME, TILE), BF16)
@@ -1259,19 +1559,25 @@
             pltpu.VMEM((8, D), F32),
             pltpu.VMEM((TP, 16, LANES), F32),
             pltpu.VMEM((F_DEV, 16, LANES), F32),
-            pltpu.VMEM((rn - 1, 3, plan.uq, QKV), BF16),
-            pltpu.VMEM((rn - 1, 9, plan.ub, D), BF16),
-            pltpu.VMEM((3, plan.uq, QKV), BF16),
-            pltpu.VMEM((2, 9, plan.ub, D), BF16),
+            pltpu.VMEM((rn - 1, 6, plan.ub, D), BF16),
+            pltpu.VMEM((2, 6, plan.ub, D), BF16),
+            pltpu.VMEM((plan.ranks, plan.ub, D), BF16),
+            pltpu.VMEM((plan.ranks, plan.ub, D), BF16),
+            pltpu.VMEM((rn - 1, 4, plan.uq // 2, QKV), BF16),
+            pltpu.VMEM((rn - 1, 6, plan.uq // 2, QKV), BF16),
+            pltpu.VMEM((4, plan.uq // 2, QKV), BF16),
+            pltpu.VMEM((4, plan.uq // 2, QKV), BF16),
             DMA((ZN - 1,)), DMA((ZN,)), DMA((ZN - 1,)), DMA((ZN,)), DMA((ZN, rn - 1)), DMA((ZN, rn - 1)),
             DMA((TILES,)), DMA((TILES,)), DMA((TILES,)), DMA((TILES,)),
             DMA, DMA, DMA, DMA, DMA((mods,)), DMA((n,)),
-            DMA((9, rn - 1)), DMA((9, rn - 1)), DMA((9,)), DMA((9, 2)),
+            DMA((6, rn - 1)), DMA((6, rn - 1)), DMA((6,)), DMA((6, 2)),
+            DMA((plan.ranks,)), DMA((plan.ranks,)), DMA((2 * plan.nq,)),
+            DMA((rn - 1, 4)), DMA((rn - 1, 6)), DMA((4,)), DMA((4,)),
         ],
-        [VM] * 9,
+        [VM] * 12,
         cid,
         name="tail_part",
-    )(dq, dkv, first_in, wq, tokens, dmid, mod_rows, dm4, gb)
+    )(dq, dkv, first_in, wq, tokens, dmid, mod_rows, dm4, gb, *early)
 
 
 def adam_kernel(plan, meta, oq, ob, cond, dmod, master, one, two, average, n_master, n_one, n_two, n_average):
@@ -1353,18 +1659,34 @@
     condition = jax.nn.silu(mm(one_hot, level_table)).astype(BF16)
     cond_units = condition.reshape(plan.frames, plan.nm, plan.um).transpose(1, 0, 2)
 
-    wq, wb, mod_rows, first_in, q_mine, kv_all = head_part(
+    wq, w_out, w_side, w_early, own_b, mod_rows, first_in, q_mine, kv_all = head_part(
         plan, flat(master), cond_units, tokens, 0
     )
-    wo_across = lax.ppermute(wb[:HD], "tp", [(i, (i + 2) % TP) for i in range(TP)])
+    rn, n = plan.r, plan.n
+    w_below = lax.ppermute(own_b, "seq", [(i, i + rn) for i in range(rn, 3 * rn)])
+    wo_across = lax.ppermute(
+        w_out.reshape(-1, D)[:HD], "tp", [(i, (i + 2) % TP) for i in range(TP)]
+    )
+    w_beside = jnp.stack(
+        [
+            lax.ppermute(
+                w_side, "seq", [(i, i // rn * rn + (i + d) % rn) for i in range(n)]
+            )
+            for d in range(1, rn)
+        ]
+    )
     meta = jnp.concatenate([frame_clip, lax.rem(s, plan.r)[None]]).astype(jnp.int32)
     o_mine, o_rows, lse = attend(plan, meta, q_mine, kv_all)
-    result, grads_b, do_mine, middle_grad, mod_four = middle_part(
-        plan, o_mine, wo_across, wb, tokens, grad_out, mod_rows, 2
+    result, grads_b, early_sum, do_mine, middle_grad, mod_four = middle_part(
+        plan, o_mine, wo_across, (w_out, w_side, w_beside, w_early, w_below),
+        tokens, grad_out, mod_rows, 2
     )
     dq_mine, dkv_all = attend_back(plan, meta, q_mine, kv_all, do_mine, o_rows, lse)
+    e_above = lax.ppermute(early_sum, "seq", [(i, i - rn) for i in range(3 * rn, n)])
+    e_below = lax.ppermute(early_sum, "seq", [(i, i + rn) for i in range(rn)])
     input_grad, own_q, own_b, mod_all = tail_part(
-        plan, dq_mine, dkv_all, first_in, wq, tokens, middle_grad, mod_rows, mod_four, grads_b, 3
+        plan, dq_mine, dkv_all, first_in, wq, tokens, middle_grad, mod_rows, mod_four, grads_b,
+        (early_sum, e_above, e_below), 3
     )
     updated = adam(
         plan,

time: 424 us -> 382 us (0.901)
  Pallas kernels: 412 us -> 347 us
  waiting for transfers between devices: 0.01 us -> 11.8 us
  starting transfers between devices: 1.58 us -> 9.67 us
    pallas_call x1, Pallas kernels: 152 us -> 111 us  [tail_part(): call(functools.partial(tail_kernel, plan), (jax.ShapeDtypeStruct((rows, D...]
    pallas_call x1, Pallas kernels: 103 us -> 84.4 us  [middle_part(): call(functools.partial(middle_kernel, plan), (jax.ShapeDtypeStruct((rows,...]
    ppermute x1 -> x5, waiting for transfers between devices: 0.01 us -> 11.8 us  [the longest x1 6.12 us: local(): lax.ppermute(w_side, 'seq', [(i, i // rn * rn + (i + d) % rn) for i in ra...]
    ppermute x1 -> x5, starting transfers between devices: 1.58 us -> 9.67 us  [the longest x1 4.65 us: local(): e_below = lax.ppermute(early_sum, 'seq', [(i, i + rn) for i in range(rn)])]
    pallas_call x1, Pallas kernels: 106 us -> 101 us  [head_part(): call(functools.partial(head_kernel, plan), (jax.ShapeDtypeStruct((D, QKV)...]
  transfers between devices with their start and end apart: 1 -> 5, of which waited for: 0 -> 2; matrix products, arithmetic and copies ran while one was open for 0% -> 0% of each run, Pallas kernels for 4% -> 10%
where the time goes in v5:
time: 382 us; the launch traced here: 380 us
  Pallas kernels  347 us (91%)
  waiting for transfers between devices  11.8 us (3%)
  starting transfers between devices  9.67 us (3%)
  local copies, waits for them, and re-layouts  9.08 us (2%)
    pallas_call x1, Pallas kernels, tail_part(): call(functools.partial(tail_kernel, plan), (jax.ShapeDtypeStruct((rows, D...  111 us
    pallas_call x1, Pallas kernels, head_part(): call(functools.partial(head_kernel, plan), (jax.ShapeDtypeStruct((D, QKV)...  101 us
    pallas_call x1, Pallas kernels, middle_part(): call(functools.partial(middle_kernel, plan), (jax.ShapeDtypeStruct((rows,...  84.4 us
    pallas_call x1, Pallas kernels, attend_back(): call(functools.partial(attend_back_kernel, plan), (jax.ShapeDtypeStruct((...  19.6 us
    pallas_call x1, Pallas kernels, attend(): call(functools.partial(attend_kernel, plan), (jax.ShapeDtypeStruct((ZN, F...  18.2 us
    pallas_call x1, Pallas kernels, adam(): call(functools.partial(adam_kernel, plan), (shape,) * 4, [], [SM] + [VM]...  12.1 us
  transfers between devices with their start and end apart: 5, of which 2 were waited for; matrix products, arithmetic and copies ran while one was open for 0% of the time, Pallas kernels for 10%

profile of v5, /device:TPU:0, one launch (start us, length us, event | category | flops | bytes accessed | tf_op | source)
XLA Modules:
  0.0 380.4 jit_solution(1954898049964739439)
XLA Ops:
  0.6 0.0 copy-start
  0.6 0.8 subtract_multiply_fusion
  1.5 0.8 copy-done
  2.2 0.5 multiply_convert_fusion
  2.7 0.2 copy.16
  2.9 0.0 copy-start.2
  2.9 0.7 copy.17.cond
  3.6 101.5 %head_part.1 = (bf16[1024,768]{1,0:T(8,128)(2,1)}, bf16[2,192,1024]{2,1,0:T(8,128)(2,1)}, bf16[3,192,1024]{2,1,0:T(8,128)(2,1)}, bf16[6,192,1024]{2,1,0:T(8,128)...) custom-call(f32[4608,128]{1,0:T(8,128)} %bitcast.19, ...), custom_call_target="tpu_custom_call" | custom-call | tf_op jit(solution)/shard_map/head_part/pallas_call | solution.py:514
  105.1 1.9 slice.4
  107.0 0.5 collective-permute-start
  107.5 0.9 collective-permute-start.2
  108.4 2.7 collective-permute-start.1
  111.1 0.6 pad_add_fusion.meta
  111.6 18.2 %attend.1 = (bf16[4,2,192,128]{3,2,1,0:T(8,128)(2,1)}, f32[8,64,384]{2,1,0:T(8,128)}, f32[8,1,384]{2,1,0:T(1,128)}) custom-call(s32[17]{0:T(128)} %pad_add_fusion.meta, bf16[4,384,128]{2,1,0:T(8,128)(2,1)} %get-tuple-element.34.q, bf16[8,768,128]{2,1,0:T(8,128)(2,1)} %get-tuple-element.35.kv), custom_call_target="tpu_custom_call" | custom-call | flops 20000000000 | bytes 60000000 | tf_op jit(solution)/shard_map/attend/pallas_call | solution.py:599
  129.9 0.0 collective-permute-done.wo_across
  129.9 0.0 collective-permute-done.2.w_below
  129.9 0.0 copy-start.6
  129.9 6.1 %collective-permute-done.1 = bf16[3,192,1024]{2,1,0:T(8,128)(2,1)} collective-permute-done((bf16[3,192,1024]{2,1,0:T(8,128)(2,1)}, bf16[3,192,1024]{2,1,0:T(8,128)(2,1)}, u32[]{:S(2)}, u32[]{:S(2)}) %collective-permute-start.1) | collective-permute-done | bytes 1179680 | tf_op jit(solution)/shard_map/ppermute | solution.py:1672
  136.0 84.4 %middle_part.1 = (bf16[768,1024]{1,0:T(8,128)(2,1)}, bf16[2304,1024]{1,0:T(8,128)(2,1)}, bf16[3,192,1024]{2,1,0:T(8,128)(2,1)}, bf16[4,2,192,128]{3,2,1,0:T(8,12...) custom-call(bf16[4,2,192,128]{3,2,1,0:T(8,128)(2,1)} %get-tuple-element.36.o_mine, ...), custom_call_target="tpu_custom_call" | custom-call | tf_op jit(solution)/shard_map/middle_part/pallas_call | solution.py:1067
  220.4 4.7 %collective-permute-start.4 = (bf16[3,192,1024]{2,1,0:T(8,128)(2,1)}, bf16[3,192,1024]{2,1,0:T(8,128)(2,1)S(1)}, u32[]{:S(2)}, u32[]{:S(2)}) collective-permute-start(bf16[3,192,1024]{2,1,0:T(8,128)(2,1)} %get-tuple-element.53.esum), channel_id=1, source_target_pairs={{0,8},{4,12},{1,9},{5,13},{2,10},{6,14},{3,11},{7,15}} | collective-permute-start | bytes 3538952 | tf_op jit(solution)/shard_map/ppermute | solution.py:1686
  225.1 1.0 collective-permute-start.3
  226.0 19.6 %attend_back.1 = (bf16[4,384,128]{2,1,0:T(8,128)(2,1)}, bf16[8,768,128]{2,1,0:T(8,128)(2,1)}) custom-call(s32[17]{0:T(128)} %pad_add_fusion.meta, bf16[4,384,128]{2,1,0:T(8,128)(2,1)} %get-tuple-element.34.q, bf16[8,768,128]{2,1,0:T(8,128)(2,1)} %get-tuple-element.35.kv, bf16[4,2,192,128]{3,2,1,0:T(8,128)(2,1)} %get-tuple-element.43.do, ...), custom_call_target="tpu_custom_call" | custom-call | flops 30000001024 | bytes 90000000 | tf_op jit(solution)/shard_map/attend_back/pallas_call | solution.py:658
  245.6 5.7 %collective-permute-done.4.e_below = bf16[3,192,1024]{2,1,0:T(8,128)(2,1)S(1)} collective-permute-done((bf16[3,192,1024]{2,1,0:T(8,128)(2,1)}, bf16[3,192,1024]{2,1,0:T(8,128)(2,1)S(1)}, u32[]{:S(2)}, u32[]{:S(2)}) %collective-permute-start.4) | collective-permute-done | bytes 1179680 | tf_op jit(solution)/shard_map/ppermute | solution.py:1686
  251.3 0.0 collective-permute-done.3.e_above
  251.3 1.0 copy-done.4
  252.3 0.4 copy-done.5
  252.7 111.4 %tail_part.1 = (f32[768,1024]{1,0:T(8,128)}, f32[3,256,768]{2,1,0:T(8,128)}, f32[3,192,1024]{2,1,0:T(8,128)}, f32[8,2,16,128]{3,2,1,0:T(8,128)}) custom-call(bf16[4,384,128]{2,1,0:T(8,128)(2,1)} %get-tuple-element.46.dq, bf16[8,768,128]{2,1,0:T(8,128)(2,1)} %get-tuple-element.47.dkv, bf16[768,1024]{1,0:T(8,128)(2,1)} %get-tuple-element.48.first_in, ...), custom_call_target="tpu_custom_call" | custom-call | tf_op jit(solution)/shard_map/tail_part/pallas_call | solution.py:1543
  364.2 12.1 %adam.1 = (f32[4608,128]{1,0:T(8,128)}, f32[4608,128]{1,0:T(8,128)}, f32[4608,128]{1,0:T(8,128)}, f32[4608,128]{1,0:T(8,128)}) custom-call(s32[1]{0:T(128)} %bitcast.6.meta, f32[3,256,768]{2,1,0:T(8,128)} %get-tuple-element.55.oq, f32[3,192,1024]{2,1,0:T(8,128)} %get-tuple-element.56.ob, bf16[8,128,16]{2,1,0:T(8,128)(2,1)} %bitcast.22, f32[256,128]{1,0:T(8,128)} %bitcast.27, ...), custom_call_target="tpu_custom_call" | custom-call | tf_op jit(solution)/shard_map/adam/pallas_call | solution.py:1629
  376.3 0.0 copy-done.3
  376.3 1.1 copy.20
  377.5 1.3 copy-done.1
  378.8 1.7 copy.21
  (8 shorter events, 0.0 us)
Async XLA Ops:
  0.6 1.6 copy-start
  2.9 102.2 %copy-start.2 = (bf16[16,1024]{0,1:T(8,128)(2,1)}, bf16[16,1024]{0,1:T(8,128)(2,1)S(1)}, u32[]{:S(2)}) copy-start(bf16[16,1024]{0,1:T(8,128)(2,1)S(1)} %copy.16) | copy-start | bytes 98308
  3.6 107.4 %copy-start.7 = (s32[16]{0:T(128)S(1)}, s32[16]{0:T(128)}, u32[]{:S(2)}) copy-start(s32[16]{0:T(128)} %param.14) | copy-start | bytes 196
  107.0 22.9 %collective-permute-start = (bf16[256,1024]{1,0:T(8,128)(2,1)}, bf16[256,1024]{1,0:T(8,128)(2,1)}, u32[]{:S(2)}, u32[]{:S(2)}) collective-permute-start(bf16[256,1024]{1,0:T(8,128)(2,1)} %slice.4), channel_id=1, source_target_pairs={{0,2},{1,3},{2,0},{3,1},{4,6},{5,7},{6,4},{7,5},{8,10},{9,11},{10,... | collective-permute-start | bytes 1572872 | tf_op jit(solution)/shard_map/ppermute | solution.py:1667
  107.5 22.4 %collective-permute-start.2 = (bf16[3,192,1024]{2,1,0:T(8,128)(2,1)}, bf16[3,192,1024]{2,1,0:T(8,128)(2,1)S(1)}, u32[]{:S(2)}, u32[]{:S(2)}) collective-permute-start(bf16[3,192,1024]{2,1,0:T(8,128)(2,1)} %get-tuple-element.40), channel_id=1, source_target_pairs={{8,16},{12,20},{16,24},{20,28},{9,17},{13,21},{17,25},{21,29},{10,... | collective-permute-start | bytes 3538952 | tf_op jit(solution)/shard_map/ppermute | solution.py:1666
  108.4 27.6 %collective-permute-start.1 = (bf16[3,192,1024]{2,1,0:T(8,128)(2,1)}, bf16[3,192,1024]{2,1,0:T(8,128)(2,1)}, u32[]{:S(2)}, u32[]{:S(2)}) collective-permute-start(bf16[3,192,1024]{2,1,0:T(8,128)(2,1)} %get-tuple-element.38.w_side), channel_id=1, source_target_pairs={{0,4},{4,0},{8,12},{12,8},{16,20},{20,16},{24,28},{28,24},{1,5},{5... | collective-permute-start | bytes 3538952 | tf_op jit(solution)/shard_map/ppermute | solution.py:1672
  129.9 6.1 %copy-start.6 = (bf16[3,192,1024]{2,1,0:T(8,128)(2,1)}, bf16[3,192,1024]{2,1,0:T(8,128)(2,1)S(1)}, u32[]{:S(2)}) copy-start(bf16[3,192,1024]{2,1,0:T(8,128)(2,1)S(1)} %collective-permute-done.2.w_below) | copy-start | bytes 3538948
  220.4 30.9 %collective-permute-start.4 = (bf16[3,192,1024]{2,1,0:T(8,128)(2,1)}, bf16[3,192,1024]{2,1,0:T(8,128)(2,1)S(1)}, u32[]{:S(2)}, u32[]{:S(2)}) collective-permute-start(bf16[3,192,1024]{2,1,0:T(8,128)(2,1)} %get-tuple-element.53.esum), channel_id=1, source_target_pairs={{0,8},{4,12},{1,9},{5,13},{2,10},{6,14},{3,11},{7,15}} | collective-permute-start | bytes 3538952 | tf_op jit(solution)/shard_map/ppermute | solution.py:1686
  225.1 26.2 %collective-permute-start.3 = (bf16[3,192,1024]{2,1,0:T(8,128)(2,1)}, bf16[3,192,1024]{2,1,0:T(8,128)(2,1)S(1)}, u32[]{:S(2)}, u32[]{:S(2)}) collective-permute-start(bf16[3,192,1024]{2,1,0:T(8,128)(2,1)} %get-tuple-element.53.esum), channel_id=1, source_target_pairs={{24,16},{28,20},{25,17},{29,21},{26,18},{30,22},{27,19},{31,23}} | collective-permute-start | bytes 3538952 | tf_op jit(solution)/shard_map/ppermute | solution.py:1685
  251.3 1.0 copy-start.4
  251.3 1.4 copy-start.5
  364.1 12.2 %copy-start.3 = (bf16[768,1024]{1,0:T(8,128)(2,1)S(1)}, bf16[768,1024]{1,0:T(8,128)(2,1)}, u32[]{:S(2)}) copy-start(bf16[768,1024]{1,0:T(8,128)(2,1)} %get-tuple-element.68) | copy-start | bytes 4718596
  376.3 2.5 copy-start.1

commit v6 on v5

--- a/solution.py
+++ b/solution.py
@@ -26,6 +26,7 @@
 PACK = TOK_FRAME // 2
 TILE = 256
 TILES = D // TILE
+CUTS = 4
 
 NORM_EPSILON = 1e-06
 RATE_FACTOR = 2.5
@@ -43,7 +44,7 @@
 DMA = pltpu.SemaphoreType.DMA
 F32 = jnp.float32
 BF16 = jnp.bfloat16
-VMEM_LIMIT = 56 * 2**20
+VMEM_LIMIT = 60 * 2**20
 
 
 def mm(left, right):
@@ -106,6 +107,7 @@
         self.sided = self.late[len(self.outs) :]
         self.rank, self.ranks = self.ranked(self.early)
         self.late_rank, self.late_ranks = self.ranked(self.sided)
+        self.grad_rank, self.grad_ranks = self.ranked(self.late)
 
     def ranked(self, units):
         seen, rank = {}, {}
@@ -193,14 +195,14 @@
     )
     start = lambda copy: copy.start()
     done = lambda copy: copy.wait_send()
-    half = plan.uq // 2
+    cut = plan.uq // CUTS
 
     def q_rows(k, h):
-        return wq.at[pl.ds(pl.multiple_of(k * plan.uq + h * half, half), half)]
+        return wq.at[pl.ds(pl.multiple_of(k * plan.uq + h * cut, cut), cut)]
 
     def q_copy(k, h, sem, to_s):
         ref = q_rows(k, h)
-        return remote(ref, ref, sem, q_r.at[2 * k + h], to_s, t)
+        return remote(ref, ref, sem, q_r.at[CUTS * k + h], to_s, t)
 
     def q_arrived(k, h):
         q_copy(k, h, qc_s.at[0, 0], s).wait_recv()
@@ -208,36 +210,34 @@
     def column(j):
         return r + rn * lax.rem(j + r, 2)
 
-    def q_own(act):
-        for away in (True, False):
-            for i in range(3):
-                k = 3 * s + i
-
-                @pl.when((k < plan.nq) & ((lax.rem(k, rn) != r) == away))
-                def _():
-                    for h in range(2):
-                        for d in range(1, rn):
-                            act(q_copy(k, h, qp_s.at[2 * i + h, d - 1], lax.rem(r + d, rn)))
-
-    def q_line(act, wait):
+    def q_own(i, act):
+        k = 3 * s + i
+
+        @pl.when(k < plan.nq)
+        def _():
+            for h in range(CUTS):
+                for d in range(1, rn):
+                    act(q_copy(k, h, qp_s.at[CUTS * i + h, d - 1], lax.rem(r + d, rn)))
+
+    def q_line(act, wait, whole=False):
         for j in range(2):
             k = column(j)
-            for h in range(2):
+            for h in range(CUTS):
                 if wait:
                     @pl.when((z > 0) | (lax.div(k, 3) != r))
                     def _():
                         q_arrived(k, h)
 
-                @pl.when(z < ZN - 1)
+                @pl.when((z < ZN - 1) & ((z > 0) | (lax.div(k, 3) != r) | whole))
                 def _():
-                    act(q_copy(k, h, qc_s.at[2 * j + h, 0], s + rn))
+                    act(q_copy(k, h, qc_s.at[CUTS * j + h, 0], s + rn))
 
                 @pl.when(z > 0)
                 def _():
                     for d in range(1, rn):
                         act(
                             q_copy(
-                                k, h, qc_s.at[2 * j + h, d], z * rn + lax.rem(r + d, rn)
+                                k, h, qc_s.at[CUTS * j + h, d], z * rn + lax.rem(r + d, rn)
                             )
                         )
 
@@ -309,23 +309,36 @@
     first_up = [k for k in plan.late if k % 3 == 0 and plan.home(k)[0] > 0]
     later_up = [k for k in plan.late if k not in first_up]
 
-    for i in range(3):
+    def fill(i, kind):
         k = 3 * s + i
         base = i * plan.flat_rows
-
-        def fill(kind):
-            rows, cols = (plan.uq, QKV // LANES) if kind == "q" else (plan.ub, D // LANES)
-            at = pl.multiple_of(k * plan.uq, plan.uq)
-            for j in range(cols):
-                values = master[pl.ds(base + j, rows, stride=cols), :].astype(BF16)
-                if kind == "q":
-                    wq[pl.ds(at, rows), j * LANES : (j + 1) * LANES] = values
-                else:
-                    own_b[i, :, j * LANES : (j + 1) * LANES] = values
-
-        by_kind(plan, k, fill)
-
-    q_own(start)
+        rows, cols = (plan.uq, QKV // LANES) if kind == "q" else (plan.ub, D // LANES)
+        at = pl.multiple_of(k * plan.uq, plan.uq)
+        for j in range(cols):
+            values = master[pl.ds(base + j, rows, stride=cols), :].astype(BF16)
+            if kind == "q":
+                wq[pl.ds(at, rows), j * LANES : (j + 1) * LANES] = values
+            else:
+                own_b[i, :, j * LANES : (j + 1) * LANES] = values
+
+    for away in (True, False):
+        for i in range(3):
+            k = 3 * s + i
+
+            @pl.when((k < plan.nq) & ((lax.rem(k, rn) != r) == away))
+            def _():
+                fill(i, "q")
+                q_own(i, start)
+                if not away:
+                    at = lax.div(k, rn)
+                    slot_j = lax.rem(at + r, 2)
+                    for h in range(CUTS):
+                        q_copy(k, h, qc_s.at[CUTS * slot_j + h, 0], s + rn).start()
+
+    for i in range(3):
+        @pl.when((3 * s + i >= plan.nq) & (3 * s + i < plan.nb))
+        def _():
+            fill(i, "b")
 
     @pl.when(z == 0)
     def _():
@@ -378,7 +391,7 @@
     owned(plan.outs, lambda k, src: along(k, src, start, True))
     owned([k for k in later_up if k not in plan.outs], lambda k, src: along(k, src, start, True))
     owned(units, lambda k, src: beside(k, src, start))
-    pass_along(first_up, 1, start, True)
+    pass_along(first_up + plan.early, 1, start, True)
 
     for src in range(fm, n):
         @pl.when(s != src)
@@ -418,7 +431,7 @@
         affine(f)
 
     for k in range(plan.nq):
-        for h in range(2):
+        for h in range(CUTS):
             if rn > 1:
                 at_zero = (z == 0) & (k // 3 != r) & (k % rn != r)
 
@@ -458,15 +471,19 @@
         a_copy(d).start()
     q_out[z] = q_send[z]
 
-    rest = [k for k in units if k not in first_up]
-    pass_along(rest, 1, start, True)
+    rest = [k for k in plan.sided if k not in first_up]
+    pass_along(plan.outs + rest, 1, start, True)
+    pass_along(plan.early, 2, start, True)
     for d in range(1, ZN):
         zs = lax.rem(z + d, ZN)
         remote(kv_send.at[0], kv_out.at[zs * rn + r], ks.at[0], kr.at[zs], s, t).wait_recv()
         for e in range(1, rn):
             side_copy(zs, e).start()
+        if d > 1:
+            pass_along(plan.outs, d, start, True)
     for d in range(2, ZN):
-        pass_along(units, d, start, True)
+        pass_along(plan.sided, d, start, True)
+    pass_along(plan.early, 3, start, True)
     for d in range(1, ZN):
         zs = lax.rem(z + d, ZN)
         remote(q_send.at[0], q_out.at[zs], as_.at[0], ar.at[zs], s, t).wait_recv()
@@ -482,8 +499,9 @@
             arrived(k)
 
 
-    q_own(done)
-    q_line(done, False)
+    for i in range(3):
+        q_own(i, done)
+    q_line(done, False, True)
     owned(units, lambda k, src: along(k, src, done, False))
     owned(plan.late, lambda k, src: along(k, src, done, True))
     owned(units, lambda k, src: beside(k, src, done))
@@ -533,7 +551,7 @@
             pltpu.VMEM((rows, D), F32),
             pltpu.VMEM((ZN, TOK_FRAME, LANES), BF16),
             pltpu.VMEM((ZN, rows, LANES), BF16),
-            DMA((6, rn - 1)), DMA((4, rn)), DMA((2 * plan.nq,)),
+            DMA((3 * CUTS, rn - 1)), DMA((2 * CUTS, rn)), DMA((CUTS * plan.nq,)),
             DMA((len(plan.outs), rn + 1)), DMA((len(plan.outs),)),
             DMA((plan.late_ranks, 2)), DMA((plan.late_ranks,)),
             DMA((plan.ranks, rn + 1)), DMA((len(plan.early),)), DMA((3,)),
@@ -614,69 +632,12 @@
     )(meta, q, kv)
 
 
-def attend_back_kernel(plan, meta, q, kv, do, ot, lse, dq, dkv, dkv_acc, dq_acc):
-    r = meta[plan.frames]
-    scale = HEAD ** (-0.5)
-    dkv_acc[...] = jnp.zeros_like(dkv_acc)
-
-    def group(zq, carry):
-        parts = []
-        for f in range(F_DEV):
-            frame = (zq * plan.r + r) * F_DEV + f
-            clip = meta[frame]
-            columns = slice(f * HEAD, (f + 1) * HEAD)
-            qz = padded(q[zq][:, columns], True) * jnp.asarray(scale, BF16)
-            grads = jnp.concatenate([do[zq, f][:, :HEAD], do[zq, f][:, HEAD:]], axis=0)
-            doz = padded(grads, False)
-            delta = jnp.sum(grads.astype(F32).T * ot[zq * F_DEV + f], axis=0, keepdims=True)
-            logs = lse[zq * F_DEV + f]
-            dq_acc[...] = jnp.zeros_like(dq_acc)
-
-            def block(j, inner):
-                @pl.when(meta[j] == clip)
-                def _():
-                    g = lax.div(j, F_DEV)
-                    rows = pl.multiple_of(lax.rem(j, F_DEV) * TOK_FRAME, TOK_FRAME)
-                    keys = kv[g, pl.ds(rows, TOK_FRAME), :]
-                    pt = jnp.exp(mm_nt(keys, qz) - logs)
-                    dst = (pt * (mm_nt(keys, doz) - delta)).astype(BF16)
-                    dkv_acc[g, pl.ds(rows, TOK_FRAME), :] += mm(dst, qz) + mm(pt.astype(BF16), doz)
-                    dq_acc[...] += mm_tn(keys, dst)
-
-                return inner
-
-            lax.fori_loop(0, frame + 1, block, 0)
-            parts.append((dq_acc[:HEAD, :] * scale).T)
-        dq[zq] = jnp.concatenate(parts, axis=1).astype(BF16)
-        return carry
-
-    lax.fori_loop(0, ZN, group, 0)
-    dkv[...] = dkv_acc[...].astype(BF16)
-
-
-def attend_back(plan, meta, q, kv, do, ot, lse):
-    return call(
-        functools.partial(attend_back_kernel, plan),
-        (
-            jax.ShapeDtypeStruct((ZN, TOK_FRAME, LANES), BF16),
-            jax.ShapeDtypeStruct((plan.n, F_DEV * TOK_FRAME, LANES), BF16),
-        ),
-        [
-            pltpu.VMEM((plan.n, F_DEV * TOK_FRAME, LANES), F32),
-            pltpu.VMEM((LANES, TOK_FRAME), F32),
-        ],
-        [SM, VM, VM, VM, VM, VM],
-        cost=pl.CostEstimate(flops=3 * 10**10, bytes_accessed=9 * 10**7, transcendentals=10**7),
-        name="attend_back",
-    )(meta, q, kv, do, ot, lse)
-
-
 def middle_kernel(
     plan, o_mine, wo_across, w_out, w_side, w_beside, w_early, w_below, tokens, grad_out, mod,
-    result, gb, esum, do_out, dmid, dmod,
-    wb, eside, wo, oall, attended, attn, mid, norm, inv, sin, hidden, dmlp, slopes, dup,
+    result, late_own, late_send, esum, ebuf, do_out, dmid, dmod,
+    gb, wb, eside, eend, wo, oall, attended, attn, mid, norm, inv, sin, hidden, dmlp, slopes, dup,
     own, csend, crecv, ysend, yrecv, dattn, dsend, dwo, wsend, wrecv,
-    o_s, o_r, f_s, f_r, n_s, n_r, c_s, c_r, y_s, y_r, d_s, d_r, w_s, w_r, e_s, e_r, p_s, p_r, l_s, u_s, u_r, g_s, g_r,
+    o_s, o_r, f_s, f_r, n_s, n_r, c_s, c_r, y_s, y_r, d_s, d_r, w_s, w_r, e_s, e_r, p_s, p_r, l_s, u_s, u_r, g_s, g_r, j_s, h_s, h_r, i_s, i_r,
 ):
     s, t, z, r = place(plan)
     rn = plan.r
@@ -906,7 +867,7 @@
             return mm_nt(dup[rows, :], wb[HD + n * TILE : HD + (n + 1) * TILE, :])
         return mm(hidden[rows, :], wb[HD + FT :, n * TILE : (n + 1) * TILE])
 
-    for w in range(2):
+    def products(w):
         for n in range(TILES):
             csend[w, n] = product(w, theirs, n).astype(BF16)
             c_copy(w, n).start()
@@ -921,9 +882,6 @@
     def up_grad(at):
         gb[pl.ds(HD + at, TILE), :] = mm_tn(sin[:, pl.ds(at, TILE)], dup[...]).astype(BF16)
 
-    loop(FT, TILE, down_grad)
-    loop(D, TILE, up_grad)
-
     def early_grad(k, d):
         zo, ro, at = home(k)
         slot = lax.rem(ro - r + rn, rn) - 1 if d is None else d - 1
@@ -940,7 +898,87 @@
             def _():
                 act(early_grad(k, None))
 
+    def early_hop(rank, act):
+        for here, to in ((ZN - 1, s - rn), (0, s + rn)):
+            @pl.when(z == here)
+            def _():
+                act(remote(esum.at[rank], eend.at[rank], h_s.at[rank], h_r.at[rank], to, t))
+
+    def early_total(rank):
+        for k in plan.early:
+            if plan.rank[k] == rank:
+                zo, ro, at = home(k)
+
+                @pl.when(r == ro)
+                def _():
+                    for d in range(1, rn):
+                        early_grad(k, d).wait_recv()
+
+                    def body(at):
+                        rows = pl.ds(at, 16)
+                        total = gb[pl.ds((k - plan.nq) * plan.ub + at, 16), :].astype(F32)
+                        for d in range(1, rn):
+                            total = total + eside[d - 1, rank, rows, :].astype(F32)
+                        esum[rank, rows, :] = total.astype(BF16)
+
+                    loop(plan.ub, 16, body)
+                    early_hop(rank, start)
+
+    def early_pass(rank, to):
+        return remote(esum.at[rank], ebuf.at[rank], i_s.at[rank], i_r.at[rank], to, t)
+
+    def early_inner(rank):
+        for k in plan.early:
+            if plan.rank[k] == rank:
+                zo, ro, at = home(k)
+
+                @pl.when((r == ro) & (z > 0) & (z < ZN - 1))
+                def _():
+                    remote(
+                        esum.at[rank], eend.at[rank], h_s.at[rank], h_r.at[rank], s, t
+                    ).wait_recv()
+
+                    def body(at):
+                        rows = pl.ds(at, 16)
+                        esum[rank, rows, :] = (
+                            esum[rank, rows, :].astype(F32) + eend[rank, rows, :].astype(F32)
+                        ).astype(BF16)
+
+                    loop(plan.ub, 16, body)
+
+                    @pl.when(z != zo)
+                    def _():
+                        early_pass(rank, s + rn if zo == 2 else s - rn).start()
+
+    def early_close(rank):
+        for k in plan.early:
+            if plan.rank[k] == rank:
+                zo, ro, at = home(k)
+
+                @pl.when((r == ro) & (z == zo))
+                def _():
+                    early_pass(rank, s).wait_recv()
+
+                @pl.when((r == ro) & (z == 3 - zo))
+                def _():
+                    early_pass(rank, s).wait_send()
+
+    def early_hops_done(rank):
+        for k in plan.early:
+            if plan.rank[k] == rank:
+                @pl.when(r == home(k)[1])
+                def _():
+                    early_hop(rank, lambda copy: copy.wait_send())
+
+    loop(FT, TILE, down_grad)
+    up_grad(D - TILE)
     early_grads(start)
+    products(0)
+    products(1)
+    loop(D - TILE, TILE, up_grad)
+    early_total(0)
+    early_total(1)
+    early_inner(0)
 
     dm = dmod
     dm[...] = jnp.zeros_like(dm)
@@ -984,6 +1022,8 @@
     for d, e in pairs:
         d_copy(d, e).start()
     do_out[z, c] = dsend[c * ZN + z]
+    for rank in range(2, plan.ranks):
+        early_total(rank)
 
     def o_grad(head_core):
         cols = pl.ds(pl.multiple_of((2 * y + head_core) * HD, HD), HD)
@@ -993,6 +1033,7 @@
     wsend[...] = o_grad(1 - c).astype(BF16)
     w_copy.start()
     dwo[...] = o_grad(c)
+    early_inner(1)
 
     for n in range(TILES):
         y_copy(1, n).wait_recv()
@@ -1011,6 +1052,8 @@
         return remote(ref, ref, e_s, e_r, s, sib)
 
     e_copy(mine).start()
+    for rank in range(2, plan.ranks):
+        early_inner(rank)
     w_copy.wait_recv()
     gb[:HD, :] = (dwo[...] + wrecv[...].astype(F32)).astype(BF16)
 
@@ -1019,27 +1062,29 @@
         remote(
             dsend.at[0], do_out.at[zd, cd], d_s.at[0], d_r.at[2 * zd + cd], s, t
         ).wait_recv()
-    for k in plan.early:
-        zo, ro, at = home(k)
-
-        @pl.when(r == ro)
-        def _():
-            rank = plan.rank[k]
-            for d in range(1, rn):
-                early_grad(k, d).wait_recv()
-
-            def body(at):
-                rows = pl.ds(at, 16)
-                total = gb[pl.ds((k - plan.nq) * plan.ub + at, 16), :].astype(F32)
-                for d in range(1, rn):
-                    total = total + eside[d - 1, rank, rows, :].astype(F32)
-                esum[rank, rows, :] = total.astype(BF16)
-
-            loop(plan.ub, 16, body)
-
+    def late_grads(act):
+        for k in plan.late:
+            zo, ro = plan.home(k)
+            rank, sem = plan.grad_rank[k], j_s.at[k - plan.nq]
+
+            @pl.when(r == ro)
+            def _():
+                act(pltpu.make_async_copy(w_rows(gb, k), late_own.at[rank], sem))
+
+            @pl.when(r != ro)
+            def _():
+                d = lax.rem(ro - r + rn, rn)
+                act(pltpu.make_async_copy(w_rows(gb, k), late_send.at[d - 1, rank], sem))
+
+    late_grads(start)
+    for rank in range(plan.ranks):
+        early_close(rank)
     e_copy(theirs).wait_recv()
     done = lambda copy: copy.wait_send()
     early_grads(done)
+    for rank in range(plan.ranks):
+        early_hops_done(rank)
+    late_grads(lambda copy: copy.wait())
     rises(done, True, False)
     rises(done, False, False)
     for d, e in pairs:
@@ -1068,7 +1113,9 @@
         functools.partial(middle_kernel, plan),
         (
             jax.ShapeDtypeStruct((rows, D), BF16),
-            jax.ShapeDtypeStruct((BROWS, D), BF16),
+            jax.ShapeDtypeStruct((plan.grad_ranks, plan.ub, D), BF16),
+            jax.ShapeDtypeStruct((rn - 1, plan.grad_ranks, plan.ub, D), BF16),
+            jax.ShapeDtypeStruct((plan.ranks, plan.ub, D), BF16),
             jax.ShapeDtypeStruct((plan.ranks, plan.ub, D), BF16),
             jax.ShapeDtypeStruct((ZN, F_DEV, PACK, LANES), BF16),
             jax.ShapeDtypeStruct((TOK_FRAME, D), F32),
@@ -1076,7 +1123,9 @@
         ),
         [
             pltpu.VMEM((BROWS, D), BF16),
+            pltpu.VMEM((BROWS, D), BF16),
             pltpu.VMEM((rn - 1, plan.ranks, plan.ub, D), BF16),
+            pltpu.VMEM((plan.ranks, plan.ub, D), BF16),
             pltpu.VMEM((HEADS * HEAD, D), BF16),
             pltpu.VMEM((HEADS, PACK, LANES), BF16),
             half(BF16), half(F32), half(F32), half(F32), pltpu.VMEM((TOK_FRAME, 1), F32),
@@ -1088,20 +1137,24 @@
             DMA((2, TILES)), DMA((2, TILES)), DMA((2, TILES)), DMA((2, TILES)),
             DMA((8,)), DMA((8,)), DMA, DMA, DMA, DMA, DMA((2,)), DMA((2,)),
             DMA((len(plan.late) + count,)), DMA((count, rn)), DMA((count,)), DMA((count,)), DMA((rn - 1, plan.ranks)),
+            DMA((len(plan.late),)), DMA((plan.ranks,)), DMA((plan.ranks,)),
+            DMA((plan.ranks,)), DMA((plan.ranks,)),
         ],
         [VM, VM, ANY, ANY, ANY, ANY, ANY, VM, VM, VM],
         cid,
+        out_specs=(VM, ANY, ANY, VM, VM, VM, VM, VM),
         name="middle_part",
     )(o_mine, wo_across, *weights, tokens, grad_out, mod_rows)
 
 
 def tail_kernel(
-    plan, dq, dkv, first_in, wq, tokens, dmid, mod, dm4, gb, esum, e_above, e_below,
+    plan, meta, q, kv, do, ot, lse, first_in, wq, tokens, dmid, mod, dm4, late_own, late_send, esum, ebuf,
     igrad, oq, ob, dall,
+    keys, flipped, qs, gs, qgt, drow, acc, dq_acc, dq, kv_two, lside,
     stage, side, q_in, kv_in, dqkv, gq, own, csend, crecv, ysend, yrecv, dm, dm3, dboth,
-    rb, cb, estage, ebuf, qside, qpeer, qchain, qstage,
-    q_s, q_r, k_s, k_r, x_s, x_r, c_s, c_r, y_s, y_r, e_s, e_r, h_s, h_r, m_s, m_r, r_s, r_r, t_s, t_r,
-    es_s, es_r, qo_s, qs_r, qp_r, qc_s, qc_r,
+    lstage, cb, qside, qpeer, qchain, qstage,
+    q_s, q_r, k_s, k_r, x_s, x_r, c_s, c_r, y_s, y_r, e_s, e_r, h_s, h_r, m_s, m_r, t_s, t_r,
+    kv_s, ls_s, ls_r, qo_s, qs_r, qp_r, qc_s, qc_r,
 ):
     s, t, z, r = place(plan)
     n, rn = plan.n, plan.r
@@ -1113,113 +1166,187 @@
     theirs = pl.multiple_of((1 - c) * TOK_FRAME, TOK_FRAME)
     greet([(lax.rem(s + d, n), t) for d in range(1, n)] + [(s, sib), (s, across)])
 
-    def side_copy(d, e):
-        zs = lax.rem(z + d, ZN)
+    def side_copy(zs, e):
         other = lax.rem(r + e, rn)
         return remote(
-            dkv.at[zs * rn + other], side.at[e - 1, d], x_s.at[d, e - 1], x_r.at[d, e - 1],
+            keys.at[zs * rn + other], side.at[e - 1, zs], x_s.at[zs, e - 1], x_r.at[zs, e - 1],
             z * rn + other, t,
         )
 
-    def q_copy(d):
-        to = lax.rem(z + d, ZN)
-        return remote(dq.at[to], q_in.at[z], q_s.at[d - 1], q_r.at[z], to * rn + r, t)
-
-    def kv_copy(d):
-        to = lax.rem(z + d, ZN)
-        return remote(stage.at[d], kv_in.at[z], k_s.at[d - 1], k_r.at[z], to * rn + r, t)
-
-    order = list(range(1, ZN)) + [0]
-    for d in order:
+    def q_copy(zs):
+        return remote(dq.at[zs], q_in.at[z], q_s.at[zs], q_r.at[z], zs * rn + r, t)
+
+    def kv_copy(zs):
+        return remote(stage.at[zs], kv_in.at[z], k_s.at[zs], k_r.at[z], zs * rn + r, t)
+
+    def send_q(zs):
+        @pl.when(z == zs)
+        def _():
+            q_in[zs] = dq[zs]
+
+        @pl.when(z != zs)
+        def _():
+            q_copy(zs).start()
+
+    def send_kv(zs):
+        total = keys[zs * rn + r].astype(F32)
         for e in range(1, rn):
-            side_copy(d, e).start()
-    for d in range(1, ZN):
-        q_copy(d).start()
-    q_in[z] = dq[z]
-    for d in order:
-        zs = lax.rem(z + d, ZN)
-        total = dkv[zs * rn + r].astype(F32)
-        for e in range(1, rn):
-            side_copy(d, e).wait_recv()
-            total = total + side[e - 1, d].astype(F32)
-        if d == 0:
-            kv_in[z] = total.astype(BF16)
-        else:
-            stage[d] = total.astype(BF16)
-            kv_copy(d).start()
-
-    def b_rows(k):
-        return gb.at[pl.ds(pl.multiple_of((k - plan.nq) * plan.ub, plan.ub), plan.ub)]
-
-    def late(k, act):
-        by_kind(plan, k, lambda kind: act(), plan.nq, plan.half)
-
-    def late_sides(act):
-        for zo in range(2):
-            for i in range(3):
-                for d in range(1, rn):
-                    other = lax.rem(r + d, rn)
-                    k = 3 * (zo * rn + other) + i
-                    lu = 3 * zo + i
-                    late(
-                        k,
-                        lambda: act(
-                            remote(
-                                b_rows(k), rb.at[d - 1, lu], r_s.at[lu, d - 1], r_r.at[lu, d - 1],
-                                z * rn + other, t,
-                            )
-                        ),
-                    )
-
-    def late_copy(lu, below, to):
-        return remote(rb.at[0, lu], cb.at[below, lu], t_s.at[lu], t_r.at[lu, below], to, t)
-
-    def late_step(zo, i, here_z, above, below, final):
-        k = 3 * (zo * rn + r) + i
-        lu = 3 * zo + i
-
-        def act():
-            unit = b_rows(k)
+            side_copy(zs, e).wait_recv()
+            total = total + side[e - 1, zs].astype(F32)
+        stage[zs] = total.astype(BF16)
+
+        @pl.when(z == zs)
+        def _():
+            kv_in[zs] = stage[zs]
+
+        @pl.when(z != zs)
+        def _():
+            kv_copy(zs).start()
+
+    scale = HEAD ** (-0.5)
+    acc[...] = jnp.zeros_like(acc)
+
+    def load(g, slot):
+        return pltpu.make_async_copy(kv.at[g], kv_two.at[slot], kv_s.at[slot])
+
+    load(0, 0).start()
+
+    def sort_group(g, carry):
+        slot = lax.rem(g, 2)
+
+        @pl.when(g + 1 < n)
+        def _():
+            load(g + 1, 1 - slot).start()
+
+        load(g, slot).wait()
+        first = meta[2 * g] == 0
+        a, b = kv_two[slot, :TOK_FRAME, :], kv_two[slot, TOK_FRAME:, :]
+        keys[g, 0] = jnp.where(first, a, b)
+        keys[g, 1] = jnp.where(first, b, a)
+        for kind in range(2):
+            flipped[kind, g] = keys[g, kind].T
+        return carry
+
+    lax.fori_loop(0, n, sort_group, 0)
+
+    def attend_back_group(zq):
+        gq = zq * rn + r
+        first = meta[2 * gq] == 0
+        clip = meta[2 * gq] + meta[2 * gq + 1]
+        parts = []
+        for kind in range(2):
+            low = first if kind == 0 else jnp.logical_not(first)
+            qz = padded(jnp.where(low, q[zq][:, :HEAD], q[zq][:, HEAD:]), True) * jnp.asarray(scale, BF16)
+            gpack = jnp.where(low, do[zq, 0], do[zq, 1])
+            grads = jnp.concatenate([gpack[:, :HEAD], gpack[:, HEAD:]], axis=0)
+            out = jnp.where(low, ot[2 * zq], ot[2 * zq + 1])
+            logs = jnp.where(low, lse[2 * zq], lse[2 * zq + 1])
+            gz = padded(grads, False)
+            qs[...] = qz
+            gs[...] = gz
+            qgt[:, :TOK_FRAME] = qz.T
+            qgt[:, TOK_FRAME:] = gz.T
+            drow[...] = jnp.sum(grads.astype(F32).T * out, axis=0, keepdims=True)
+            dq_acc[...] = jnp.zeros_like(dq_acc)
+
+            def block(p, inner):
+                total = dq_acc[...]
+                for e in range(2):
+                    g = jnp.minimum(2 * p + e, gq)
+                    shown = 2 * p + e <= gq
+                    if kind == 1:
+                        shown = shown & (meta[2 * g] + meta[2 * g + 1] == clip)
+                    off = jnp.where(shown, 0.0, 1e30)
+                    key = keys[g, kind]
+                    pt = jnp.exp(mm(key, qgt[:, :TOK_FRAME]) - (logs + off))
+                    dst = (pt * (mm(key, qgt[:, TOK_FRAME:]) - drow[...])).astype(BF16)
+                    acc[kind, g] += mm(dst, qs[...]) + mm(pt.astype(BF16), gs[...])
+                    total = total + mm(flipped[kind, g], dst)
+                dq_acc[...] = total
+                return inner
+
+            lax.fori_loop(0, lax.div(gq + 2, 2), block, 0)
+            parts.append((dq_acc[:HEAD, :] * scale).T.astype(BF16))
+        dq[zq] = jnp.concatenate(
+            [jnp.where(first, parts[0], parts[1]), jnp.where(first, parts[1], parts[0])], axis=1
+        )
+        for other in range(rn):
+            g = zq * rn + other
+            low = meta[2 * g] == 0
+            a, b = acc[0, g].astype(BF16), acc[1, g].astype(BF16)
+            keys[g, 0] = jnp.where(low, a, b)
+            keys[g, 1] = jnp.where(low, b, a)
+
+    def late(units, act):
+        for k in units:
+            zo, ro = plan.home(k)
+
+            @pl.when(r == ro)
+            def _():
+                act(k, zo, plan.grad_rank[k])
+
+    def late_copy(rank, below, to):
+        return remote(lstage.at[rank], cb.at[below, rank], t_s.at[rank], t_r.at[below, rank], to, t)
+
+    def late_side(rank, d):
+        return remote(
+            late_send.at[d - 1, rank], lside.at[d - 1, rank], ls_s.at[rank, d - 1],
+            ls_r.at[rank, d - 1], z * rn + lax.rem(r + d, rn), t,
+        )
+
+    def late_sides(rank, act):
+        for d in range(1, rn):
+            act(late_side(rank, d))
+
+    def late_step(k, zo, rank, here_z, above, below, final):
+        @pl.when(z == here_z)
+        def _():
             for d in range(1, rn):
-                remote(
-                    unit, rb.at[d - 1, lu], r_s.at[lu, d - 1], r_r.at[lu, d - 1], s, t
-                ).wait_recv()
+                late_side(rank, d).wait_recv()
             if above:
-                late_copy(lu, 0, s).wait_recv()
+                late_copy(rank, 0, s).wait_recv()
             if below:
-                late_copy(lu, 1, s).wait_recv()
+                late_copy(rank, 1, s).wait_recv()
 
             def body(at):
                 rows = pl.ds(at, 16)
-                total = unit[rows, :].astype(F32)
+                total = late_own[rank, rows, :].astype(F32)
                 for d in range(1, rn):
-                    total = total + rb[d - 1, lu, rows, :].astype(F32)
+                    total = total + lside[d - 1, rank, rows, :].astype(F32)
                 if above:
-                    total = total + cb[0, lu, rows, :].astype(F32)
+                    total = total + cb[0, rank, rows, :].astype(F32)
                 if below:
-                    total = total + cb[1, lu, rows, :].astype(F32)
+                    total = total + cb[1, rank, rows, :].astype(F32)
                 if final:
-                    ob[i, rows, :] = total
+                    ob[k % 3, rows, :] = total
                 else:
-                    rb[0, lu, rows, :] = total.astype(BF16)
+                    lstage[rank, rows, :] = total.astype(BF16)
 
             loop(plan.ub, 16, body)
             if not final:
-                late_copy(lu, 0 if here_z > zo else 1, s - rn if here_z > zo else s + rn).start()
-
-        @pl.when(z == here_z)
-        def _():
-            late(k, act)
-
-    def late_close():
-        late_sides(lambda copy: copy.wait_send())
-        for zo in range(2):
-            for i in range(3):
-                @pl.when(z != zo)
-                def _():
-                    late(
-                        3 * (zo * rn + r) + i, lambda: late_copy(3 * zo + i, 0, s).wait_send()
-                    )
+                late_copy(
+                    rank, 0 if here_z > zo else 1, s - rn if here_z > zo else s + rn
+                ).start()
+
+    def late_ends(k, zo, rank):
+        late_step(k, zo, rank, ZN - 1, False, False, False)
+        if zo > 0:
+            late_step(k, zo, rank, 0, False, False, False)
+
+    def late_inner(here):
+        def act(k, zo, rank):
+            if here > zo:
+                late_step(k, zo, rank, here, True, False, False)
+
+        return act
+
+    def late_final(k, zo, rank):
+        late_step(k, zo, rank, zo, True, zo > 0, True)
+
+    def late_done(k, zo, rank):
+        @pl.when(z != zo)
+        def _():
+            late_copy(rank, 0, s).wait_send()
 
     def early_units(act):
         for k in plan.early:
@@ -1229,60 +1356,30 @@
             def _():
                 act(k, zo, rank)
 
-    def early_copy(rank, to):
-        return remote(estage.at[rank], ebuf.at[rank], es_s.at[rank], es_r.at[rank], to, t)
-
-    def early_send(k, zo, rank):
-        source, came, step = (1, e_below, rn) if zo == 2 else (2, e_above, -rn)
-
-        @pl.when(z == source)
+    def early_final(k, zo, rank):
+        @pl.when(z == zo)
         def _():
             def body(at):
                 rows = pl.ds(at, 16)
-                estage[rank, rows, :] = (
-                    esum[rank, rows, :].astype(F32) + came[rank, rows, :].astype(F32)
-                ).astype(BF16)
+                ob[k % 3, rows, :] = esum[rank, rows, :].astype(F32) + ebuf[rank, rows, :].astype(F32)
 
             loop(plan.ub, 16, body)
-            early_copy(rank, s + step).start()
-
-    def early_final(k, zo, rank):
-        came = e_above if zo == 2 else e_below
-
-        @pl.when(z == zo)
-        def _():
-            early_copy(rank, s).wait_recv()
-
-            def body(at):
-                rows = pl.ds(at, 16)
-                ob[k % 3, rows, :] = (
-                    esum[rank, rows, :].astype(F32)
-                    + came[rank, rows, :].astype(F32)
-                    + ebuf[rank, rows, :].astype(F32)
-                )
-
-            loop(plan.ub, 16, body)
-
-    def early_done(k, zo, rank):
-        @pl.when(z == 3 - zo)
-        def _():
-            early_copy(rank, s).wait_send()
-
-    hq = plan.uq // 2
+
+    hq = plan.uq // CUTS
 
     def q_rows(k, h):
         return gq.at[pl.ds(pl.multiple_of(k * plan.uq + h * hq, hq), hq)]
 
     def q_sides(k, act):
         tc, ro, j = k % rn, k // 3, k // rn
-        for h in range(2):
+        for h in range(CUTS):
             @pl.when((z > 0) & (r != tc))
             def _():
                 slot = lax.rem(tc - r + rn, rn) - 1
                 act(
                     remote(
-                        q_rows(k, h), qside.at[slot, 2 * j + h], qo_s.at[2 * k + h],
-                        qs_r.at[slot, 2 * j + h], z * rn + tc, t,
+                        q_rows(k, h), qside.at[slot, CUTS * j + h], qo_s.at[CUTS * k + h],
+                        qs_r.at[slot, CUTS * j + h], z * rn + tc, t,
                     )
                 )
 
@@ -1291,21 +1388,22 @@
                 slot = lax.rem(ro - r + rn, rn) - 1
                 act(
                     remote(
-                        q_rows(k, h), qpeer.at[slot, 2 * (k % 3) + h], qo_s.at[2 * k + h],
-                        qp_r.at[slot, 2 * (k % 3) + h], ro, t,
+                        q_rows(k, h), qpeer.at[slot, CUTS * (k % 3) + h], qo_s.at[CUTS * k + h],
+                        qp_r.at[slot, CUTS * (k % 3) + h], ro, t,
                     )
                 )
 
     def q_down(at, to):
         return remote(qstage.at[at], qchain.at[at], qc_s.at[at], qc_r.at[at], to, t)
 
-    def q_chain(top):
-        for j in range(2):
+    def q_chain(here, only_j):
+        top = here == ZN - 1
+        for j in (only_j,):
             k = r + rn * j
-            for h in range(2):
-                at = 2 * j + h
-
-                @pl.when(z == ZN - 1 if top else (z > 0) & (z < ZN - 1))
+            for h in range(CUTS):
+                at = CUTS * j + h
+
+                @pl.when(z == here)
                 def _():
                     for d in range(1, rn):
                         remote(
@@ -1331,8 +1429,8 @@
         tc, ro, j = k % rn, k // 3, k // rn
         slot = (ro - tc + rn) % rn - 1
         return remote(
-            qstage.at[2 * j + h], qpeer.at[slot, 2 * (k % 3) + h], qc_s.at[2 * j + h],
-            qp_r.at[slot, 2 * (k % 3) + h], ro, t,
+            qstage.at[CUTS * j + h], qpeer.at[slot, CUTS * (k % 3) + h], qc_s.at[CUTS * j + h],
+            qp_r.at[slot, CUTS * (k % 3) + h], ro, t,
         )
 
     def q_ground(act):
@@ -1340,11 +1438,11 @@
             if k % rn != k // 3:
                 @pl.when((z == 0) & (r == k % rn))
                 def _():
-                    for h in range(2):
+                    for h in range(CUTS):
                         act(k, h)
 
     def q_turn(k, h):
-        at = 2 * (k // rn) + h
+        at = CUTS * (k // rn) + h
         q_down(at, s).wait_recv()
         unit = q_rows(k, h)
 
@@ -1362,14 +1460,14 @@
             @pl.when((z == 0) & (r == k // 3))
             def _():
                 straight = k % rn == k // 3
-                for h in range(2):
-                    at = 2 * (k // rn) + h
+                for h in range(CUTS):
+                    at = CUTS * (k // rn) + h
                     if straight:
                         q_down(at, s).wait_recv()
                     for d in range(1, rn):
                         remote(
-                            q_rows(k, h), qpeer.at[d - 1, 2 * (k % 3) + h], qo_s.at[0],
-                            qp_r.at[d - 1, 2 * (k % 3) + h], s, t,
+                            q_rows(k, h), qpeer.at[d - 1, CUTS * (k % 3) + h], qo_s.at[0],
+                            qp_r.at[d - 1, CUTS * (k % 3) + h], s, t,
                         ).wait_recv()
                     unit = q_rows(k, h)
 
@@ -1377,7 +1475,7 @@
                         rows = pl.ds(row, 16)
                         total = unit[rows, :].astype(F32)
                         for d in range(1, rn):
-                            total = total + qpeer[d - 1, 2 * (k % 3) + h, rows, :].astype(F32)
+                            total = total + qpeer[d - 1, CUTS * (k % 3) + h, rows, :].astype(F32)
                         if straight:
                             total = total + qchain[at, rows, :].astype(F32)
                         oq[k % 3, pl.ds(h * hq + row, 16), :] = total
@@ -1386,24 +1484,38 @@
 
     start = lambda copy: copy.start()
     done = lambda copy: copy.wait_send()
-    late_sides(start)
-    early_units(early_send)
-    for zo in range(2):
-        for i in range(3):
-            late_step(zo, i, ZN - 1, False, False, False)
-    for i in range(3):
-        late_step(1, i, 0, False, False, False)
-
-    for d in range(1, ZN):
-        zs = lax.rem(z + d, ZN)
-        remote(dq.at[0], q_in.at[zs], q_s.at[0], q_r.at[zs], s, t).wait_recv()
-        remote(stage.at[d], kv_in.at[zs], k_s.at[0], k_r.at[zs], s, t).wait_recv()
+    def only(rank, act):
+        return lambda k, zo, own_rank: act(k, zo, own_rank) if own_rank == rank else None
+
+    last = plan.grad_ranks - 1
+    late_sides(0, start)
+    for zq in range(ZN - 1, -1, -1):
+        attend_back_group(zq)
+        for e in range(1, rn):
+            side_copy(zq, e).start()
+        send_q(zq)
+        if zq == ZN - 1:
+            late(plan.late, only(0, late_ends))
+        else:
+            send_kv(zq + 1)
+    for rank in range(1, plan.grad_ranks):
+        late_sides(rank, start)
+    send_kv(0)
+    late(plan.late, only(0, late_inner(2)))
+    late(plan.late, only(0, late_inner(1)))
+    late(plan.late, only(1, late_ends))
+    for zs in range(ZN):
+        @pl.when(z != zs)
+        def _():
+            remote(dq.at[0], q_in.at[zs], q_s.at[0], q_r.at[zs], s, t).wait_recv()
+            remote(stage.at[0], kv_in.at[zs], k_s.at[0], k_r.at[zs], s, t).wait_recv()
+
     for p in range(2):
         cols = slice(p * LANES, (p + 1) * LANES)
         a, b = q_in[2 * p], q_in[2 * p + 1]
         dqkv[:TOK_FRAME, cols] = jnp.concatenate([a[:, :HEAD], b[:, :HEAD]], axis=1)
         dqkv[TOK_FRAME:, cols] = jnp.concatenate([a[:, HEAD:], b[:, HEAD:]], axis=1)
-        a, b = kv_in[2 * p], kv_in[2 * p + 1]
+        a, b = [kv_in[2 * p + i].reshape(F_DEV * TOK_FRAME, LANES) for i in range(2)]
         dqkv[:, HD + p * LANES : HD + (p + 1) * LANES] = jnp.concatenate(
             [a[:, :HEAD], b[:, :HEAD]], axis=1
         )
@@ -1438,13 +1550,18 @@
             pass_on(w - 1)
     pass_on(TILES - 1)
 
-    for here in (2, 1):
-        for zo in range(2):
-            if zo != here:
-                for i in range(3):
-                    late_step(zo, i, here, True, False, False)
-    q_chain(True)
-    q_chain(False)
+    for rank in range(2, plan.grad_ranks):
+        late(plan.late, only(rank, late_ends))
+    q_chain(ZN - 1, 0)
+    q_chain(ZN - 1, 1)
+    late(plan.late, only(1, late_inner(2)))
+    q_chain(2, 0)
+    late(plan.late, only(last, late_inner(2)))
+    q_chain(2, 1)
+    q_chain(1, 0)
+    late(plan.late, only(1, late_inner(1)))
+    q_chain(1, 1)
+    late(plan.late, only(last, late_inner(1)))
 
     for w in range(TILES):
         y_copy(w).wait_recv()
@@ -1494,9 +1611,7 @@
             m_copy(src).start()
 
     q_ground(q_turn)
-    for i in range(3):
-        late_step(1, i, 1, True, True, True)
-        late_step(0, i, 0, True, False, True)
+    late(plan.late, late_final)
     early_units(early_final)
     q_final()
 
@@ -1507,20 +1622,23 @@
             remote(dboth, dall.at[other], m_s.at[0], m_r.at[other], s, t).wait_recv()
 
     e_copy(theirs).wait_recv()
-    for d in range(1, ZN):
-        q_copy(d).wait_send()
-        kv_copy(d).wait_send()
-    for d in order:
+    for zs in range(ZN):
+        @pl.when(z != zs)
+        def _():
+            q_copy(zs).wait_send()
+            kv_copy(zs).wait_send()
+
         for e in range(1, rn):
-            side_copy(d, e).wait_send()
-    late_close()
-    early_units(early_done)
+            side_copy(zs, e).wait_send()
+    for rank in range(plan.grad_ranks):
+        late_sides(rank, done)
+    late(plan.late, late_done)
     for k in range(plan.nq):
         q_sides(k, done)
 
     @pl.when(z > 0)
     def _():
-        for at in range(4):
+        for at in range(2 * CUTS):
             q_down(at, s).wait_send()
 
     q_ground(lambda k, h: q_last_copy(k, h).wait_send())
@@ -1535,7 +1653,7 @@
             m_copy(src).wait_send()
 
 
-def tail_part(plan, dq, dkv, first_in, wq, tokens, dmid, mod_rows, dm4, gb, early, cid):
+def tail_part(plan, meta, q, kv, do, ot, lse, first_in, wq, tokens, dmid, mod_rows, dm4, late_own, late_send, esum, ebuf, cid):
     n, rn = plan.n, plan.r
     rows = F_DEV * TOK_FRAME
     tiles = pltpu.VMEM((TILES, TOK_FRAME, TILE), BF16)
@@ -1549,35 +1667,45 @@
             jax.ShapeDtypeStruct((n, F_DEV, 16, LANES), F32),
         ),
         [
-            pltpu.VMEM((ZN, rows, LANES), BF16),
-            pltpu.VMEM((rn - 1, ZN, rows, LANES), BF16),
+            pltpu.VMEM((n, 2, TOK_FRAME, LANES), BF16),
+            pltpu.VMEM((2, n, LANES, TOK_FRAME), BF16),
+            pltpu.VMEM((TOK_FRAME, LANES), BF16),
+            pltpu.VMEM((TOK_FRAME, LANES), BF16),
+            pltpu.VMEM((LANES, 2 * TOK_FRAME), BF16),
+            pltpu.VMEM((1, TOK_FRAME), F32),
+            pltpu.VMEM((2, n, TOK_FRAME, LANES), F32),
+            pltpu.VMEM((LANES, TOK_FRAME), F32),
             pltpu.VMEM((ZN, TOK_FRAME, LANES), BF16),
-            pltpu.VMEM((ZN, rows, LANES), BF16),
+            pltpu.VMEM((2, rows, LANES), BF16),
+            pltpu.VMEM((rn - 1, plan.grad_ranks, plan.ub, D), BF16),
+            pltpu.VMEM((ZN, 2, TOK_FRAME, LANES), BF16),
+            pltpu.VMEM((rn - 1, ZN, 2, TOK_FRAME, LANES), BF16),
+            pltpu.VMEM((ZN, TOK_FRAME, LANES), BF16),
+            pltpu.VMEM((ZN, 2, TOK_FRAME, LANES), BF16),
             pltpu.VMEM((rows, QKV), BF16),
             pltpu.VMEM((D, QKV), BF16),
             pltpu.VMEM((TILES, TOK_FRAME, TILE), F32), tiles, tiles, tiles, tiles,
             pltpu.VMEM((8, D), F32),
             pltpu.VMEM((TP, 16, LANES), F32),
             pltpu.VMEM((F_DEV, 16, LANES), F32),
-            pltpu.VMEM((rn - 1, 6, plan.ub, D), BF16),
-            pltpu.VMEM((2, 6, plan.ub, D), BF16),
-            pltpu.VMEM((plan.ranks, plan.ub, D), BF16),
-            pltpu.VMEM((plan.ranks, plan.ub, D), BF16),
-            pltpu.VMEM((rn - 1, 4, plan.uq // 2, QKV), BF16),
-            pltpu.VMEM((rn - 1, 6, plan.uq // 2, QKV), BF16),
-            pltpu.VMEM((4, plan.uq // 2, QKV), BF16),
-            pltpu.VMEM((4, plan.uq // 2, QKV), BF16),
-            DMA((ZN - 1,)), DMA((ZN,)), DMA((ZN - 1,)), DMA((ZN,)), DMA((ZN, rn - 1)), DMA((ZN, rn - 1)),
+            pltpu.VMEM((plan.grad_ranks, plan.ub, D), BF16),
+            pltpu.VMEM((2, plan.grad_ranks, plan.ub, D), BF16),
+            pltpu.VMEM((rn - 1, 2 * CUTS, plan.uq // CUTS, QKV), BF16),
+            pltpu.VMEM((rn - 1, 3 * CUTS, plan.uq // CUTS, QKV), BF16),
+            pltpu.VMEM((2 * CUTS, plan.uq // CUTS, QKV), BF16),
+            pltpu.VMEM((2 * CUTS, plan.uq // CUTS, QKV), BF16),
+            DMA((ZN,)), DMA((ZN,)), DMA((ZN,)), DMA((ZN,)), DMA((ZN, rn - 1)), DMA((ZN, rn - 1)),
             DMA((TILES,)), DMA((TILES,)), DMA((TILES,)), DMA((TILES,)),
             DMA, DMA, DMA, DMA, DMA((mods,)), DMA((n,)),
-            DMA((6, rn - 1)), DMA((6, rn - 1)), DMA((6,)), DMA((6, 2)),
-            DMA((plan.ranks,)), DMA((plan.ranks,)), DMA((2 * plan.nq,)),
-            DMA((rn - 1, 4)), DMA((rn - 1, 6)), DMA((4,)), DMA((4,)),
+            DMA((plan.grad_ranks,)), DMA((2, plan.grad_ranks)),
+            DMA((2,)), DMA((plan.grad_ranks, rn - 1)), DMA((plan.grad_ranks, rn - 1)),
+            DMA((CUTS * plan.nq,)),
+            DMA((rn - 1, 2 * CUTS)), DMA((rn - 1, 3 * CUTS)), DMA((2 * CUTS,)), DMA((2 * CUTS,)),
         ],
-        [VM] * 12,
+        [SM, VM, ANY] + [VM] * 10 + [ANY, VM, VM],
         cid,
         name="tail_part",
-    )(dq, dkv, first_in, wq, tokens, dmid, mod_rows, dm4, gb, *early)
+    )(meta, q, kv, do, ot, lse, first_in, wq, tokens, dmid, mod_rows, dm4, late_own, late_send, esum, ebuf)
 
 
 def adam_kernel(plan, meta, oq, ob, cond, dmod, master, one, two, average, n_master, n_one, n_two, n_average):
@@ -1599,9 +1727,9 @@
         n_master[rows, :] = weight
         n_average[rows, :] = AVERAGE_RATE * average[rows, :] + (1.0 - AVERAGE_RATE) * weight
 
-    for i in range(3):
-        k = 3 * s + i
-        base = i * plan.flat_rows
+    if True:
+        k = 3 * s + pl.program_id(0)
+        base = 0
 
         def from_matrix(kind):
             src = oq if kind == "q" else ob
@@ -1609,7 +1737,7 @@
             cols = (QKV if kind == "q" else D) // LANES
             for j in range(cols):
                 update(
-                    pl.ds(base + j, rows, stride=cols), src[i, :, j * LANES : (j + 1) * LANES]
+                    pl.ds(base + j, rows, stride=cols), src[0, :, j * LANES : (j + 1) * LANES]
                 )
 
         by_kind(plan, k, from_matrix)
@@ -1626,11 +1754,16 @@
 
 def adam(plan, meta, oq, ob, cond_rows, dmod, master, one, two, average):
     shape = jax.ShapeDtypeStruct(master.shape, F32)
-    return call(
+    flat = pl.BlockSpec((plan.flat_rows, LANES), lambda i: (i, 0))
+    unit = lambda rows, cols: pl.BlockSpec((1, rows, cols), lambda i: (i, 0, 0))
+    whole = lambda x: pl.BlockSpec(x.shape, lambda i: (0,) * x.ndim)
+    return pl.pallas_call(
         functools.partial(adam_kernel, plan),
-        (shape,) * 4,
-        [],
-        [SM] + [VM] * 8,
+        out_shape=(shape,) * 4,
+        grid=(3,),
+        in_specs=[SM, unit(plan.uq, QKV), unit(plan.ub, D), whole(cond_rows), whole(dmod)] + [flat] * 4,
+        out_specs=(flat,) * 4,
+        compiler_params=pltpu.CompilerParams(vmem_limit_bytes=VMEM_LIMIT),
         name="adam",
     )(meta, oq, ob, cond_rows, dmod, master, one, two, average)
 
@@ -1677,16 +1810,13 @@
     )
     meta = jnp.concatenate([frame_clip, lax.rem(s, plan.r)[None]]).astype(jnp.int32)
     o_mine, o_rows, lse = attend(plan, meta, q_mine, kv_all)
-    result, grads_b, early_sum, do_mine, middle_grad, mod_four = middle_part(
+    result, late_own, late_send, early_sum, early_in, do_mine, middle_grad, mod_four = middle_part(
         plan, o_mine, wo_across, (w_out, w_side, w_beside, w_early, w_below),
         tokens, grad_out, mod_rows, 2
     )
-    dq_mine, dkv_all = attend_back(plan, meta, q_mine, kv_all, do_mine, o_rows, lse)
-    e_above = lax.ppermute(early_sum, "seq", [(i, i - rn) for i in range(3 * rn, n)])
-    e_below = lax.ppermute(early_sum, "seq", [(i, i + rn) for i in range(rn)])
     input_grad, own_q, own_b, mod_all = tail_part(
-        plan, dq_mine, dkv_all, first_in, wq, tokens, middle_grad, mod_rows, mod_four, grads_b,
-        (early_sum, e_above, e_below), 3
+        plan, meta, q_mine, kv_all, do_mine, o_rows, lse, first_in, wq, tokens, middle_grad,
+        mod_rows, mod_four, late_own, late_send, early_sum, early_in, 3,
     )
     updated = adam(
         plan,

time: 382 us -> 367 us (0.961); the launches traced: 380 us -> 361 us
  Pallas kernels: 347 us -> 340 us
  waiting for transfers between devices: 11.8 us -> 5.04 us
  starting transfers between devices: 9.67 us -> 5.26 us
    pallas_call x2 -> x1, Pallas kernels: 31.7 us -> 11.4 us  [adam(): pl.pallas_call(functools.partial(adam_kernel, plan), out_shape=(shape,) *...]
    pallas_call x1, Pallas kernels: 84.4 us -> 96.6 us  [middle_part(): call(functools.partial(middle_kernel, plan), (jax.ShapeDtypeStruct((rows,...]
    pallas_call x1, Pallas kernels: 111 us -> 120 us  [tail_part(): call(functools.partial(tail_kernel, plan), (jax.ShapeDtypeStruct((rows, D...]
    pallas_call x1, Pallas kernels: 101 us -> 93.7 us  [head_part(): call(functools.partial(head_kernel, plan), (jax.ShapeDtypeStruct((D, QKV)...]
    ppermute x2 -> x0, waiting for transfers between devices: 5.68 us -> none  [the longest x1 5.67 us: local(): e_below = lax.ppermute(early_sum, 'seq', [(i, i + rn) for i in range(rn)])]
    ppermute x2 -> x0, starting transfers between devices: 5.61 us -> none  [the longest x1 4.65 us: local(): e_below = lax.ppermute(early_sum, 'seq', [(i, i + rn) for i in range(rn)])]
  transfers between devices with their start and end apart: 5 -> 3, of which waited for: 2 -> 1; matrix products, arithmetic and copies ran while one was open for 0% -> 0% of each run, Pallas kernels for 10% -> 5%
where the time goes in v6:
time: 367 us; the launch traced here: 361 us
  Pallas kernels  340 us (93%)
  local copies, waits for them, and re-layouts  7.68 us (2%)
  starting transfers between devices  5.26 us (1%)
  waiting for transfers between devices  5.04 us (1%)
    pallas_call x1, Pallas kernels, tail_part(): call(functools.partial(tail_kernel, plan), (jax.ShapeDtypeStruct((rows, D...  120 us
    pallas_call x1, Pallas kernels, middle_part(): call(functools.partial(middle_kernel, plan), (jax.ShapeDtypeStruct((rows,...  96.6 us
    pallas_call x1, Pallas kernels, head_part(): call(functools.partial(head_kernel, plan), (jax.ShapeDtypeStruct((D, QKV)...  93.7 us
    pallas_call x1, Pallas kernels, attend(): call(functools.partial(attend_kernel, plan), (jax.ShapeDtypeStruct((ZN, F...  18.2 us
    pallas_call x1, Pallas kernels, adam(): pl.pallas_call(functools.partial(adam_kernel, plan), out_shape=(shape,) *...  11.4 us
  transfers between devices with their start and end apart: 3, of which 1 were waited for; matrix products, arithmetic and copies ran while one was open for 0% of the time, Pallas kernels for 5%

profile of v6, /device:TPU:0, one launch (start us, length us, event | category | flops | bytes accessed | tf_op | source)
XLA Modules:
  0.0 360.7 jit_solution(17091540117005744553)
XLA Ops:
  0.6 0.0 copy-start
  0.6 0.8 subtract_multiply_fusion
  1.5 0.8 copy-done
  2.2 0.5 multiply_convert_fusion
  2.7 0.2 copy.16
  2.9 0.0 copy-start.2
  2.9 0.7 copy.17.cond
  3.6 0.0 copy-start.5
  3.6 93.7 %head_part.1 = (bf16[1024,768]{1,0:T(8,128)(2,1)}, bf16[2,192,1024]{2,1,0:T(8,128)(2,1)}, bf16[3,192,1024]{2,1,0:T(8,128)(2,1)}, bf16[6,192,1024]{2,1,0:T(8,128)...) custom-call(f32[4608,128]{1,0:T(8,128)} %bitcast.19, ...), custom_call_target="tpu_custom_call" | custom-call | tf_op jit(solution)/shard_map/head_part/pallas_call | solution.py:532
  97.4 0.0 copy-done.2
  97.4 1.9 slice.4
  99.3 1.6 collective-permute-start
  100.9 0.9 collective-permute-start.2
  101.8 2.7 collective-permute-start.1
  104.5 0.0 copy-done.5
  104.5 0.6 pad_add_fusion.meta
  105.1 18.2 %attend.1 = (bf16[4,2,192,128]{3,2,1,0:T(8,128)(2,1)}, f32[8,64,384]{2,1,0:T(8,128)}, f32[8,1,384]{2,1,0:T(1,128)}) custom-call(s32[17]{0:T(128)} %pad_add_fusion.meta, bf16[4,384,128]{2,1,0:T(8,128)(2,1)} %get-tuple-element.34.q, bf16[8,768,128]{2,1,0:T(8,128)(2,1)} %get-tuple-element.35.kv), custom_call_target="tpu_custom_call" | custom-call | flops 20000000000 | bytes 60000000 | tf_op jit(solution)/shard_map/attend/pallas_call | solution.py:617
  123.3 0.0 collective-permute-done.wo_across
  123.3 0.0 collective-permute-done.2.w_below
  123.4 0.0 copy-start.4
  123.4 5.0 %collective-permute-done.1 = bf16[3,192,1024]{2,1,0:T(8,128)(2,1)} collective-permute-done((bf16[3,192,1024]{2,1,0:T(8,128)(2,1)}, bf16[3,192,1024]{2,1,0:T(8,128)(2,1)}, u32[]{:S(2)}, u32[]{:S(2)}) %collective-permute-start.1) | collective-permute-done | bytes 1179680 | tf_op jit(solution)/shard_map/ppermute | solution.py:1805
  128.4 0.0 copy-done.4
  128.4 96.6 %middle_part.1 = (bf16[768,1024]{1,0:T(8,128)(2,1)}, bf16[3,192,1024]{2,1,0:T(8,128)(2,1)}, bf16[1,3,192,1024]{3,2,1,0:T(8,128)(2,1)}, bf16[3,192,1024]{2,1,0:T(...) custom-call(bf16[4,2,192,128]{3,2,1,0:T(8,128)(2,1)} %get-tuple-elem, ...), custom_call_target="tpu_custom_call" | custom-call | tf_op jit(solution)/shard_map/middle_part/pallas_call | solution.py:1112
  225.0 119.7 %tail_part.1 = (f32[768,1024]{1,0:T(8,128)}, f32[3,256,768]{2,1,0:T(8,128)}, f32[3,192,1024]{2,1,0:T(8,128)}, f32[8,2,16,128]{3,2,1,0:T(8,128)}) custom-call(s32[17]{0:T(128)} %pad_add_fusion.meta, bf16[4,384,128]{2,1,0:T(8,128)(2,1)} %get-tuple-element.34.q, bf16[8,768,128]{2,1,0:T(8,128)(2,1)} %get-tuple-element.35.kv, ...), custom_call_target="tpu_custom_call" | custom-call | tf_op jit(solution)/shard_map/tail_part/pallas_call | solution.py:1661
  344.8 0.0 copy-start.3
  344.8 11.4 %adam.1 = (f32[4608,128]{1,0:T(8,128)}, f32[4608,128]{1,0:T(8,128)}, f32[4608,128]{1,0:T(8,128)}, f32[4608,128]{1,0:T(8,128)}) custom-call(s32[1]{0:T(128)} %bitcast.6.meta, f32[3,256,768]{2,1,0:T(8,128)} %get-tuple-element.55.oq, f32[3,192,1024]{2,1,0:T(8,128)} %get-tuple-element.56.ob, bf16[8,128,16]{2,1,0:T(8,128)(2,1)} %bitcast.22, f32[256,128]{1,0:T(8,128)} %bitcast.27, ...), custom_call_target="tpu_custom_call" | custom-call | tf_op jit(solution)/shard_map/adam/pallas_call | solution.py:1760
  356.1 0.0 copy-start.1
  356.1 0.0 copy-done.3
  356.2 1.1 copy.20
  357.3 1.3 copy-done.1
  358.6 1.7 copy.21
Async XLA Ops:
  0.6 1.6 copy-start
  2.9 94.5 %copy-start.2 = (bf16[16,1024]{0,1:T(8,128)(2,1)}, bf16[16,1024]{0,1:T(8,128)(2,1)S(1)}, u32[]{:S(2)}) copy-start(bf16[16,1024]{0,1:T(8,128)(2,1)S(1)} %copy.16) | copy-start | bytes 98308
  3.6 100.9 %copy-start.5 = (s32[16]{0:T(128)S(1)}, s32[16]{0:T(128)}, u32[]{:S(2)}) copy-start(s32[16]{0:T(128)} %param.14) | copy-start | bytes 196
  99.3 24.1 %collective-permute-start = (bf16[256,1024]{1,0:T(8,128)(2,1)}, bf16[256,1024]{1,0:T(8,128)(2,1)}, u32[]{:S(2)}, u32[]{:S(2)}) collective-permute-start(bf16[256,1024]{1,0:T(8,128)(2,1)} %slice.4), channel_id=1, source_target_pairs={{0,2},{1,3},{2,0},{3,1},{4,6},{5,7},{6,4},{7,5},{8,10},{9,11},{10,... | collective-permute-start | bytes 1572872 | tf_op jit(solution)/shard_map/ppermute | solution.py:1800
  100.9 22.5 %collective-permute-start.2 = (bf16[3,192,1024]{2,1,0:T(8,128)(2,1)}, bf16[3,192,1024]{2,1,0:T(8,128)(2,1)S(1)}, u32[]{:S(2)}, u32[]{:S(2)}) collective-permute-start(bf16[3,192,1024]{2,1,0:T(8,128)(2,1)} %get-tuple-element.40), channel_id=1, source_target_pairs={{8,16},{12,20},{16,24},{20,28},{9,17},{13,21},{17,25},{21,29},{10,... | collective-permute-start | bytes 3538952 | tf_op jit(solution)/shard_map/ppermute | solution.py:1799
  101.8 26.6 %collective-permute-start.1 = (bf16[3,192,1024]{2,1,0:T(8,128)(2,1)}, bf16[3,192,1024]{2,1,0:T(8,128)(2,1)}, u32[]{:S(2)}, u32[]{:S(2)}) collective-permute-start(bf16[3,192,1024]{2,1,0:T(8,128)(2,1)} %get-tuple-element.38.w_side), channel_id=1, source_target_pairs={{0,4},{4,0},{8,12},{12,8},{16,20},{20,16},{24,28},{28,24},{1,5},{5... | collective-permute-start | bytes 3538952 | tf_op jit(solution)/shard_map/ppermute | solution.py:1805
  123.4 5.0 %copy-start.4 = (bf16[3,192,1024]{2,1,0:T(8,128)(2,1)}, bf16[3,192,1024]{2,1,0:T(8,128)(2,1)S(1)}, u32[]{:S(2)}) copy-start(bf16[3,192,1024]{2,1,0:T(8,128)(2,1)S(1)} %collective-permute-done.2.w_below) | copy-start | bytes 3538948
  344.8 11.4 %copy-start.3 = (bf16[768,1024]{1,0:T(8,128)(2,1)S(1)}, bf16[768,1024]{1,0:T(8,128)(2,1)}, u32[]{:S(2)}) copy-start(bf16[768,1024]{1,0:T(8,128)(2,1)} %get-tuple-element.68) | copy-start | bytes 4718596
  356.1 2.5 copy-start.1
